TPU v7x, 256 devices: a whole 4x4x8 slice. The times are simulated.
256 devices in a mesh: band: 128 (over z_hi, y, x, core), head: 2 (over z_lo).
Axes of the slice: x: 4, y: 4, z: 8 (z_hi: 4, z_lo: 2; z = z_hi * 2 + z_lo), core: 2. Of those that a mesh axis runs over, the one named last changes fastest.
Arguments:
- queries: bfloat16 [128, 3, 128, 512], P('band', None, None, 'head'), may hold values from -16 to 16
- attn_keys: bfloat16 [128, 3, 128, 512], P('band', None, None, 'head'), may hold values from -16 to 16
- attn_values: bfloat16 [128, 3, 128, 512], P('band', None, None, 'head'), may hold values from -16 to 16
- out_proj: bfloat16 [512, 1024], P('head'), may hold values from -0.25 to 0.25
- grad_out: bfloat16 [128, 3, 128, 1024], P('band', None, 'head'), may hold values from -24 to 24
- plane_axes: int32 [3, 2], replicated, may hold values from 0 to 2, as said below
Outputs:
- layer_out: bfloat16 [128, 3, 128, 1024], P('band', None, 'head')
- grad_queries: bfloat16 [128, 3, 128, 512], P('band', None, None, 'head')
- grad_keys: bfloat16 [128, 3, 128, 512], P('band', None, None, 'head')
- grad_values: bfloat16 [128, 3, 128, 512], P('band', None, None, 'head')
Inputs may be any that keep to these rules, and one draw needn't show every extreme that they name: `plane_axes`: row p holds plane p's row axis and then its column axis, two different world axes; the three planes lack three different world axes.
All inputs are finite; a program needn't handle non-finite values.
Results may differ from a plain program's by a relative error of at most 0.018.
Values may be sent and summed in bfloat16 or wider, within the bound.
No kernel may reach another device: no remote copies, remote signals or barrier semaphores. Data moves between devices by JAX's collectives and lax.ppermute only.
A program may use at most 64 MiB of HBM per device.

v0:
```python
import jax
import jax.numpy as jnp
from jax import lax
from jax.sharding import PartitionSpec as P

HEAD_DIM = 64


def partner_blocks(plane_axes):
    axis_of = jnp.concatenate([plane_axes[:, 0], plane_axes[:, 1]])
    blocks = jnp.arange(6, dtype=jnp.int32)
    same = (axis_of[:, None] == axis_of[None, :]) & (blocks[:, None] != blocks[None, :])
    return jnp.sum(jnp.where(same, blocks[None, :], 0), axis=1)


def by_head(values):
    return values.reshape(values.shape[:-1] + (values.shape[-1] // HEAD_DIM, HEAD_DIM))


def flatten(values):
    return values.reshape(values.shape[:2] + (-1,))


def log_total(scores):
    top = jnp.max(scores, axis=-1, keepdims=True)
    return top[..., 0] + jnp.log(jnp.sum(jnp.exp(scores - top), axis=-1))


def line_scores(query_line, key_line, partner):
    factor = HEAD_DIM ** (-0.5)
    query_heads = by_head(query_line)
    key_heads = by_head(key_line)
    partner_keys = jnp.take(key_heads, partner, axis=0)
    cross = (
        jnp.einsum("bahe,bche->bhac", query_heads, partner_keys, preferred_element_type=jnp.float32)
        * factor
    )
    own = (
        jnp.einsum(
            "bahe,bche->bhac", query_heads[:3], key_heads[:3], preferred_element_type=jnp.float32
        )
        * factor
    )
    return (own, cross)


def forward_core(own, cross, value_line, partner):
    value_heads = by_head(value_line)
    partner_values = jnp.take(value_heads, partner, axis=0)
    length = own.shape[-1]
    near_scores = jnp.concatenate([own, cross[:3]], axis=-1)
    near_total = log_total(near_scores)
    near_prob = jnp.exp(near_scores - near_total[..., None]).astype(jnp.bfloat16)
    near_out = jnp.einsum(
        "bhac,bche->bahe",
        near_prob[..., :length],
        value_heads[:3],
        preferred_element_type=jnp.float32,
    )
    near_out = near_out + jnp.einsum(
        "bhac,bche->bahe",
        near_prob[..., length:],
        partner_values[:3],
        preferred_element_type=jnp.float32,
    )
    far_total = log_total(cross[3:])
    far_prob = jnp.exp(cross[3:] - far_total[..., None]).astype(jnp.bfloat16)
    far_out = jnp.einsum(
        "bhac,bche->bahe", far_prob, partner_values[3:], preferred_element_type=jnp.float32
    )
    return (
        jnp.transpose(near_total, (0, 2, 1)),
        flatten(near_out),
        jnp.transpose(far_total, (0, 2, 1)),
        flatten(far_out),
    )


def backward_core(own, cross, line, partner):
    factor = HEAD_DIM ** (-0.5)
    query_line, key_line, value_line, grad_line, total_line, delta_line = line
    query_heads = by_head(query_line)
    key_heads = by_head(key_line)
    value_heads = by_head(value_line)
    grad_heads = by_head(grad_line)
    partner_keys = jnp.take(key_heads, partner, axis=0)
    partner_values = jnp.take(value_heads, partner, axis=0)
    total = jnp.transpose(total_line, (0, 2, 1))[..., None]
    delta = jnp.transpose(delta_line, (0, 2, 1))[..., None]
    cross_prob = jnp.exp(cross - total).astype(jnp.bfloat16)
    own_prob = jnp.exp(own - total[:3]).astype(jnp.bfloat16)
    cross_grad = jnp.einsum(
        "bahe,bche->bhac", grad_heads, partner_values, preferred_element_type=jnp.float32
    )
    own_grad = jnp.einsum(
        "bahe,bche->bhac", grad_heads[:3], value_heads[:3], preferred_element_type=jnp.float32
    )
    cross_step = (cross_prob.astype(jnp.float32) * (cross_grad - delta) * factor).astype(
        jnp.bfloat16
    )
    own_step = (own_prob.astype(jnp.float32) * (own_grad - delta[:3]) * factor).astype(jnp.bfloat16)
    grad_query = jnp.einsum(
        "bhac,bche->bahe", cross_step, partner_keys, preferred_element_type=jnp.float32
    )
    grad_query = grad_query.at[:3].add(
        jnp.einsum("bhac,bche->bahe", own_step, key_heads[:3], preferred_element_type=jnp.float32)
    )
    toward_keys = jnp.einsum(
        "bhac,bahe->bche", cross_step, query_heads, preferred_element_type=jnp.float32
    )
    toward_values = jnp.einsum(
        "bhac,bahe->bche", cross_prob, grad_heads, preferred_element_type=jnp.float32
    )
    grad_key = jnp.take(toward_keys, partner, axis=0)
    grad_key = grad_key.at[:3].add(
        jnp.einsum("bhac,bahe->bche", own_step, query_heads[:3], preferred_element_type=jnp.float32)
    )
    grad_value = jnp.take(toward_values, partner, axis=0)
    grad_value = grad_value.at[:3].add(
        jnp.einsum("bhac,bahe->bche", own_prob, grad_heads[:3], preferred_element_type=jnp.float32)
    )
    return (flatten(grad_query), flatten(grad_key), flatten(grad_value))


def to_columns(values):
    return jnp.transpose(values, (2, 1, 0, 3))


def body(queries, attn_keys, attn_values, out_proj, grad_out, plane_axes):
    partner = partner_blocks(plane_axes)
    column_q, column_k, column_v = (
        lax.all_to_all(to_columns(queries), "band", split_axis=0, concat_axis=2, tiled=True),
        lax.all_to_all(to_columns(attn_keys), "band", split_axis=0, concat_axis=2, tiled=True),
        lax.all_to_all(to_columns(attn_values), "band", split_axis=0, concat_axis=2, tiled=True),
    )
    query_lines = jnp.concatenate([queries, column_q], axis=1)
    key_lines = jnp.concatenate([attn_keys, column_k], axis=1)
    value_lines = jnp.concatenate([attn_values, column_v], axis=1)
    lines = (query_lines, key_lines, value_lines)

    def forward_fresh(line):
        own, cross = line_scores(line[0], line[1], partner)
        return forward_core(own, cross, line[2], partner)

    near_total, near_out, far_total, far_out = lax.map(forward_fresh, lines)
    far_back, far_total_back = (
        lax.all_to_all(far_out, "band", split_axis=2, concat_axis=0, tiled=True),
        lax.all_to_all(far_total, "band", split_axis=2, concat_axis=0, tiled=True),
    )
    far_out = to_columns(far_back)
    far_total = to_columns(far_total_back)
    top = jnp.maximum(near_total, far_total)
    log_all = top + jnp.log(jnp.exp(near_total - top) + jnp.exp(far_total - top))
    attended = (
        by_head(near_out) * jnp.exp(near_total - log_all)[..., None]
        + by_head(far_out) * jnp.exp(far_total - log_all)[..., None]
    )
    attended = attended.reshape(queries.shape).astype(jnp.bfloat16)
    summed = lax.psum_scatter(
        jnp.einsum("ipjf,fd->jipd", attended, out_proj, preferred_element_type=jnp.float32).astype(
            jnp.bfloat16
        ),
        "head",
        scatter_dimension=0,
        tiled=True,
    ).astype(jnp.float32)
    layer_out = jnp.transpose(summed, (1, 2, 0, 3)).astype(jnp.bfloat16)
    grad_attended = jnp.einsum(
        "ipjd,fd->ipjf",
        lax.all_gather(grad_out, "head", axis=2, tiled=True),
        out_proj,
        preferred_element_type=jnp.float32,
    ).astype(jnp.bfloat16)
    delta = jnp.sum(
        by_head(grad_attended).astype(jnp.float32) * by_head(attended).astype(jnp.float32), axis=-1
    )
    grad_column, total_column, delta_column = (
        lax.all_to_all(
            to_columns(grad_attended.astype(jnp.float32)),
            "band",
            split_axis=0,
            concat_axis=2,
            tiled=True,
        ),
        lax.all_to_all(to_columns(log_all), "band", split_axis=0, concat_axis=2, tiled=True),
        lax.all_to_all(to_columns(delta), "band", split_axis=0, concat_axis=2, tiled=True),
    )
    grad_lines = jnp.concatenate([grad_attended, grad_column.astype(jnp.bfloat16)], axis=1)
    total_lines = jnp.concatenate([log_all, total_column], axis=1)
    delta_lines = jnp.concatenate([delta, delta_column], axis=1)
    back_lines = (query_lines, key_lines, value_lines, grad_lines, total_lines, delta_lines)

    def backward_fresh(line):
        own, cross = line_scores(line[0], line[1], partner)
        return backward_core(own, cross, line, partner)

    grad_q, grad_k, grad_v = lax.map(backward_fresh, back_lines)
    back_q, back_k, back_v = (
        lax.all_to_all(
            grad_q[:, 3:].astype(jnp.bfloat16), "band", split_axis=2, concat_axis=0, tiled=True
        ).astype(jnp.float32),
        lax.all_to_all(
            grad_k[:, 3:].astype(jnp.bfloat16), "band", split_axis=2, concat_axis=0, tiled=True
        ).astype(jnp.float32),
        lax.all_to_all(
            grad_v[:, 3:].astype(jnp.bfloat16), "band", split_axis=2, concat_axis=0, tiled=True
        ).astype(jnp.float32),
    )
    grad_queries = (grad_q[:, :3] + to_columns(back_q)).astype(jnp.bfloat16)
    grad_keys = (grad_k[:, :3] + to_columns(back_k)).astype(jnp.bfloat16)
    grad_values = (grad_v[:, :3] + to_columns(back_v)).astype(jnp.bfloat16)
    return (layer_out, grad_queries, grad_keys, grad_values)


def solution(mesh):
    in_specs = (
        P("band", None, None, "head"),
        P("band", None, None, "head"),
        P("band", None, None, "head"),
        P("head", None),
        P("band", None, "head", None),
        P(),
    )
    out_specs = (
        P("band", None, "head", None),
        P("band", None, None, "head"),
        P("band", None, None, "head"),
        P("band", None, None, "head"),
    )
    return jax.shard_map(body, mesh=mesh, in_specs=in_specs, out_specs=out_specs, check_vma=False)
```

profile of v0, /device:TPU:1, one launch (start us, length us, event | category | flops | bytes accessed | tf_op | source)
XLA Modules:
  0.0 298.8 jit_solution(12313239052928605685)
XLA Ops:
  9.1 16.4 %all-to-all-start = ((bf16[128,3,1,256]{3,1,2,0:T(4,128)(2,1)}), bf16[128,3,1,256]{3,1,2,0:T(4,128)(2,1)S(1)}, u32[]{:S(2)}, u32[]{:S(2)}) async-start(bf16[128,3,1,256]{3,1,2,0:T(4,128)(2,1)} %bitcast.209), calls=%async_computation | async-start | bytes 524288 | tf_op jit(solution)/shard_map/all_to_all | solution.py:132
  28.3 12.2 %all_gather.3 = bf16[1,3,128,1024]{3,2,1,0:T(8,128)(2,1)S(1)} all-gather(bf16[1,3,64,1024]{3,2,1,0:T(8,128)(2,1)S(1)} %copy-done.21), channel_id=1, replica_groups=mesh['band'=128,'head'=2] {'head'}, dimensions={2}, use_global_device_ids=true | all-gather | bytes 1179648 | tf_op jit(solution)/shard_map/all_gather | solution.py:170
  41.0 14.0 %all-to-all-start.1 = ((bf16[128,3,1,256]{3,1,2,0:T(4,128)(2,1)}), bf16[128,3,1,256]{3,1,2,0:T(4,128)(2,1)S(1)}, u32[]{:S(2)}, u32[]{:S(2)}) async-start(bf16[128,3,1,256]{3,1,2,0:T(4,128)(2,1)} %bitcast.208), calls=%async_computation.1 | async-start | bytes 524288 | tf_op jit(solution)/shard_map/all_to_all | solution.py:133
  60.7 9.6 %all-to-all-done.1 = bf16[128,3,1,256]{3,1,2,0:T(4,128)(2,1)S(1)} async-done(((bf16[128,3,1,256]{3,1,2,0:T(4,128)(2,1)}), bf16[128,3,1,256]{3,1,2,0:T(4,128)(2,1)S(1)}, u32[]{:S(2)}, u32[]{:S(2)}) %all-to-all-start.1) | async-done | bytes 196640 | tf_op jit(solution)/shard_map/all_to_all | solution.py:133
  70.2 7.4 %all-to-all-start.2 = ((bf16[128,3,1,256]{3,1,2,0:T(4,128)(2,1)}), bf16[128,3,1,256]{3,1,2,0:T(4,128)(2,1)}, u32[]{:S(2)}, u32[]{:S(2)}) async-start(bf16[128,3,1,256]{3,1,2,0:T(4,128)(2,1)} %bitcast.207), calls=%async_computation.2 | async-start | bytes 524288 | tf_op jit(solution)/shard_map/all_to_all | solution.py:134
  81.8 10.9 %all-to-all-done.2 = bf16[128,3,1,256]{3,1,2,0:T(4,128)(2,1)} async-done(((bf16[128,3,1,256]{3,1,2,0:T(4,128)(2,1)}), bf16[128,3,1,256]{3,1,2,0:T(4,128)(2,1)}, u32[]{:S(2)}, u32[]{:S(2)}) %all-to-all-start.2) | async-done | bytes 196640 | tf_op jit(solution)/shard_map/all_to_all | solution.py:134
  92.7 7.5 %all-to-all-start.3 = ((f32[1,3,128,4]{3,0,1,2:T(1,128)}), f32[1,3,128,4]{3,0,1,2:T(1,128)}, u32[]{:S(2)}, u32[]{:S(2)}) async-start(f32[1,3,128,4]{3,0,1,2:T(1,128)} %copy.289), calls=%async_computation.3 | async-start | bytes 393216 | tf_op jit(solution)/shard_map/all_to_all | solution.py:148
  103.8 2.4 gather_fusion.1
  106.2 8.1 %all-to-all-done.3 = f32[1,3,128,4]{3,0,1,2:T(1,128)} async-done(((f32[1,3,128,4]{3,0,1,2:T(1,128)}), f32[1,3,128,4]{3,0,1,2:T(1,128)}, u32[]{:S(2)}, u32[]{:S(2)}) %all-to-all-start.3) | async-done | bytes 6176 | tf_op jit(solution)/shard_map/all_to_all | solution.py:148
  114.2 7.4 %all-to-all-start.6 = ((bf16[128,2,384]{2,1,0:T(2,128)(2,1)}), bf16[128,2,384]{2,1,0:T(2,128)(2,1)}, u32[]{:S(2)}, u32[]{:S(2)}) async-start(bf16[128,2,384]{2,1,0:T(2,128)(2,1)} %reshape.398), calls=%async_computation.7 | async-start | bytes 393216 | tf_op jit(solution)/shard_map/all_to_all | solution.py:178
  124.9 10.7 %all-to-all-done.6 = bf16[128,2,384]{2,1,0:T(2,128)(2,1)} async-done(((bf16[128,2,384]{2,1,0:T(2,128)(2,1)}), bf16[128,2,384]{2,1,0:T(2,128)(2,1)}, u32[]{:S(2)}, u32[]{:S(2)}) %all-to-all-start.6) | async-done | bytes 196640 | tf_op jit(solution)/shard_map/all_to_all | solution.py:178
  135.6 7.3 %all-to-all-start.5 = ((f32[128,3,1,4]{3,2,1,0:T(1,128)}), f32[128,3,1,4]{3,2,1,0:T(1,128)}, u32[]{:S(2)}, u32[]{:S(2)}) async-start(f32[128,3,1,4]{3,2,1,0:T(1,128)} %copy.296), calls=%async_computation.6 | async-start | bytes 393216 | tf_op jit(solution)/shard_map/all_to_all | solution.py:185
  146.7 10.1 %all-to-all-done.5 = f32[128,3,1,4]{3,2,1,0:T(1,128)} async-done(((f32[128,3,1,4]{3,2,1,0:T(1,128)}), f32[128,3,1,4]{3,2,1,0:T(1,128)}, u32[]{:S(2)}, u32[]{:S(2)}) %all-to-all-start.5) | async-done | bytes 6176 | tf_op jit(solution)/shard_map/all_to_all | solution.py:185
  156.8 7.3 %all-to-all-start.4 = ((f32[1,3,128,256]{3,0,1,2:T(1,128)}), f32[1,3,128,256]{3,0,1,2:T(1,128)}, u32[]{:S(2)}, u32[]{:S(2)}) async-start(f32[1,3,128,256]{3,0,1,2:T(1,128)} %copy.292), calls=%async_computation.4 | async-start | bytes 786432 | tf_op jit(solution)/shard_map/all_to_all | solution.py:147
  175.0 7.2 %all-to-all-done.4 = f32[1,3,128,256]{3,0,1,2:T(1,128)} async-done(((f32[1,3,128,256]{3,0,1,2:T(1,128)}), f32[1,3,128,256]{3,0,1,2:T(1,128)}, u32[]{:S(2)}, u32[]{:S(2)}) %all-to-all-start.4) | async-done | bytes 393248 | tf_op jit(solution)/shard_map/all_to_all | solution.py:147
  187.2 7.4 %all-to-all-start.7 = ((f32[128,3,1,4]{3,2,1,0:T(1,128)}), f32[128,3,1,4]{3,2,1,0:T(1,128)}, u32[]{:S(2)}, u32[]{:S(2)}) async-start(f32[128,3,1,4]{3,2,1,0:T(1,128)} %copy.302), calls=%async_computation.8 | async-start | bytes 393216 | tf_op jit(solution)/shard_map/all_to_all | solution.py:186
  197.1 11.4 %all-to-all-done.7 = f32[128,3,1,4]{3,2,1,0:T(1,128)} async-done(((f32[128,3,1,4]{3,2,1,0:T(1,128)}), f32[128,3,1,4]{3,2,1,0:T(1,128)}, u32[]{:S(2)}, u32[]{:S(2)}) %all-to-all-start.7) | async-done | bytes 6176 | tf_op jit(solution)/shard_map/all_to_all | solution.py:186
  209.6 2.8 multiply_convert_fusion
  223.8 7.4 %all-to-all-start.10 = ((bf16[1,3,128,256]{3,1,0,2:T(4,128)(2,1)}), bf16[1,3,128,256]{3,1,0,2:T(4,128)(2,1)}, u32[]{:S(2)}, u32[]{:S(2)}) async-start(bf16[1,3,128,256]{3,1,0,2:T(4,128)(2,1)} %copy.319), calls=%async_computation.11 | async-start | bytes 524288 | tf_op jit(solution)/shard_map/all_to_all | solution.py:205
  233.4 13.1 %all-to-all-done.10 = bf16[1,3,128,256]{3,1,0,2:T(4,128)(2,1)} async-done(((bf16[1,3,128,256]{3,1,0,2:T(4,128)(2,1)}), bf16[1,3,128,256]{3,1,0,2:T(4,128)(2,1)}, u32[]{:S(2)}, u32[]{:S(2)}) %all-to-all-start.10) | async-done | bytes 196640 | tf_op jit(solution)/shard_map/all_to_all | solution.py:205
  246.5 7.3 %all-to-all-start.9 = ((bf16[1,3,128,256]{3,1,0,2:T(4,128)(2,1)}), bf16[1,3,128,256]{3,1,0,2:T(4,128)(2,1)}, u32[]{:S(2)}, u32[]{:S(2)}) async-start(bf16[1,3,128,256]{3,1,0,2:T(4,128)(2,1)} %copy.314), calls=%async_computation.10 | async-start | bytes 524288 | tf_op jit(solution)/shard_map/all_to_all | solution.py:202
  258.3 10.8 %all-to-all-done.9 = bf16[1,3,128,256]{3,1,0,2:T(4,128)(2,1)} async-done(((bf16[1,3,128,256]{3,1,0,2:T(4,128)(2,1)}), bf16[1,3,128,256]{3,1,0,2:T(4,128)(2,1)}, u32[]{:S(2)}, u32[]{:S(2)}) %all-to-all-start.9) | async-done | bytes 196640 | tf_op jit(solution)/shard_map/all_to_all | solution.py:202
  269.1 6.3 %all-to-all-start.8 = ((bf16[1,3,128,256]{3,1,0,2:T(4,128)(2,1)}), bf16[1,3,128,256]{3,1,0,2:T(4,128)(2,1)S(1)}, u32[]{:S(2)}, u32[]{:S(2)}) async-start(bf16[1,3,128,256]{3,1,0,2:T(4,128)(2,1)} %copy.309), calls=%async_computation.9 | async-start | bytes 524288 | tf_op jit(solution)/shard_map/all_to_all | solution.py:199
  279.9 11.0 %all-to-all-done.8 = bf16[1,3,128,256]{3,1,0,2:T(4,128)(2,1)S(1)} async-done(((bf16[1,3,128,256]{3,1,0,2:T(4,128)(2,1)}), bf16[1,3,128,256]{3,1,0,2:T(4,128)(2,1)S(1)}, u32[]{:S(2)}, u32[]{:S(2)}) %all-to-all-start.8) | async-done | bytes 196640 | tf_op jit(solution)/shard_map/all_to_all | solution.py:199
  (130 shorter events, 68.4 us)
Async XLA Ops:
  7.2 33.4 %copy-start = (bf16[256,1024]{1,0:T(8,128)(2,1)S(1)}, bf16[256,1024]{1,0:T(8,128)(2,1)}, u32[]{:S(2)}) copy-start(bf16[256,1024]{1,0:T(8,128)(2,1)} %param.19) | copy-start | bytes 1572868
  7.2 21.1 %copy-start.21 = (bf16[1,3,64,1024]{3,2,1,0:T(8,128)(2,1)S(1)}, bf16[1,3,64,1024]{3,2,1,0:T(8,128)(2,1)}, u32[]{:S(2)}) copy-start(bf16[1,3,64,1024]{3,2,1,0:T(8,128)(2,1)} %param.20) | copy-start | bytes 1179652
  9.1 31.9 %all-to-all-start = ((bf16[128,3,1,256]{3,1,2,0:T(4,128)(2,1)}), bf16[128,3,1,256]{3,1,2,0:T(4,128)(2,1)S(1)}, u32[]{:S(2)}, u32[]{:S(2)}) async-start(bf16[128,3,1,256]{3,1,2,0:T(4,128)(2,1)} %bitcast.209), calls=%async_computation | async-start | bytes 524288 | tf_op jit(solution)/shard_map/all_to_all | solution.py:132
  28.3 26.8 %copy-start.17 = (bf16[1,3,128,256]{3,2,1,0:T(8,128)(2,1)S(1)}, bf16[1,3,128,256]{3,2,1,0:T(8,128)(2,1)}, u32[]{:S(2)}) copy-start(bf16[1,3,128,256]{3,2,1,0:T(8,128)(2,1)} %param.16) | copy-start | bytes 589828
  40.5 14.7 %copy-start.18 = (bf16[1,3,128,256]{3,2,1,0:T(8,128)(2,1)S(1)}, bf16[1,3,128,256]{3,2,1,0:T(8,128)(2,1)}, u32[]{:S(2)}) copy-start(bf16[1,3,128,256]{3,2,1,0:T(8,128)(2,1)} %param.17) | copy-start | bytes 589828
  40.5 14.9 %copy-start.19 = (bf16[1,3,128,256]{3,2,1,0:T(8,128)(2,1)S(1)}, bf16[1,3,128,256]{3,2,1,0:T(8,128)(2,1)}, u32[]{:S(2)}) copy-start(bf16[1,3,128,256]{3,2,1,0:T(8,128)(2,1)} %param.18) | copy-start | bytes 589828
  41.0 17.6 %copy-start.16 = (bf16[3,128,256]{2,1,0:T(8,128)(2,1)}, bf16[3,128,256]{2,1,0:T(8,128)(2,1)S(1)}, u32[]{:S(2)}) copy-start(bf16[3,128,256]{2,1,0:T(8,128)(2,1)S(1)} %convolution_convert_fusion.1) | copy-start | bytes 589828
  41.0 29.2 %all-to-all-start.1 = ((bf16[128,3,1,256]{3,1,2,0:T(4,128)(2,1)}), bf16[128,3,1,256]{3,1,2,0:T(4,128)(2,1)S(1)}, u32[]{:S(2)}, u32[]{:S(2)}) async-start(bf16[128,3,1,256]{3,1,2,0:T(4,128)(2,1)} %bitcast.208), calls=%async_computation.1 | async-start | bytes 524288 | tf_op jit(solution)/shard_map/all_to_all | solution.py:133
  55.4 22.4 %copy-start.10 = (bf16[1,3,128,256]{2,3,1,0:T(8,128)(2,1)}, bf16[1,3,128,256]{2,3,1,0:T(8,128)(2,1)S(1)}, u32[]{:S(2)}) copy-start(bf16[1,3,128,256]{2,3,1,0:T(8,128)(2,1)S(1)} %copy.279) | copy-start | bytes 589828
  70.2 22.5 %all-to-all-start.2 = ((bf16[128,3,1,256]{3,1,2,0:T(4,128)(2,1)}), bf16[128,3,1,256]{3,1,2,0:T(4,128)(2,1)}, u32[]{:S(2)}, u32[]{:S(2)}) async-start(bf16[128,3,1,256]{3,1,2,0:T(4,128)(2,1)} %bitcast.207), calls=%async_computation.2 | async-start | bytes 524288 | tf_op jit(solution)/shard_map/all_to_all | solution.py:134
  92.7 21.6 %all-to-all-start.3 = ((f32[1,3,128,4]{3,0,1,2:T(1,128)}), f32[1,3,128,4]{3,0,1,2:T(1,128)}, u32[]{:S(2)}, u32[]{:S(2)}) async-start(f32[1,3,128,4]{3,0,1,2:T(1,128)} %copy.289), calls=%async_computation.3 | async-start | bytes 393216 | tf_op jit(solution)/shard_map/all_to_all | solution.py:148
  114.2 21.3 %all-to-all-start.6 = ((bf16[128,2,384]{2,1,0:T(2,128)(2,1)}), bf16[128,2,384]{2,1,0:T(2,128)(2,1)}, u32[]{:S(2)}, u32[]{:S(2)}) async-start(bf16[128,2,384]{2,1,0:T(2,128)(2,1)} %reshape.398), calls=%async_computation.7 | async-start | bytes 393216 | tf_op jit(solution)/shard_map/all_to_all | solution.py:178
  135.6 21.2 %all-to-all-start.5 = ((f32[128,3,1,4]{3,2,1,0:T(1,128)}), f32[128,3,1,4]{3,2,1,0:T(1,128)}, u32[]{:S(2)}, u32[]{:S(2)}) async-start(f32[128,3,1,4]{3,2,1,0:T(1,128)} %copy.296), calls=%async_computation.6 | async-start | bytes 393216 | tf_op jit(solution)/shard_map/all_to_all | solution.py:185
  156.8 25.4 %all-to-all-start.4 = ((f32[1,3,128,256]{3,0,1,2:T(1,128)}), f32[1,3,128,256]{3,0,1,2:T(1,128)}, u32[]{:S(2)}, u32[]{:S(2)}) async-start(f32[1,3,128,256]{3,0,1,2:T(1,128)} %copy.292), calls=%async_computation.4 | async-start | bytes 786432 | tf_op jit(solution)/shard_map/all_to_all | solution.py:147
  187.2 21.3 %all-to-all-start.7 = ((f32[128,3,1,4]{3,2,1,0:T(1,128)}), f32[128,3,1,4]{3,2,1,0:T(1,128)}, u32[]{:S(2)}, u32[]{:S(2)}) async-start(f32[128,3,1,4]{3,2,1,0:T(1,128)} %copy.302), calls=%async_computation.8 | async-start | bytes 393216 | tf_op jit(solution)/shard_map/all_to_all | solution.py:186
  194.6 97.4 %reduce-scatter.2.cloned.1.call-start = ((), (), s32[]{:S(2)}) async-start(), calls=%async_computation.12 | async-start | bytes 1179648 | tf_op jit(solution)/shard_map/reduce_scatter | solution.py:159
  221.5 9.7 %copy-start.12 = (bf16[1,3,128,256]{2,3,1,0:T(8,128)(2,1)S(1)}, bf16[1,3,128,256]{2,3,1,0:T(8,128)(2,1)}, u32[]{:S(2)}) copy-start(bf16[1,3,128,256]{2,3,1,0:T(8,128)(2,1)} %copy.284) | copy-start | bytes 589828
  222.8 8.8 %copy-start.3 = (f32[6,128,4,64]{1,3,2,0:T(8,128)S(1)}, f32[6,128,4,64]{1,3,2,0:T(8,128)}, u32[]{:S(2)}) copy-start(f32[6,128,4,64]{1,3,2,0:T(8,128)} %get-tuple-element.146) | copy-start | bytes 2359300
  223.8 22.6 %all-to-all-start.10 = ((bf16[1,3,128,256]{3,1,0,2:T(4,128)(2,1)}), bf16[1,3,128,256]{3,1,0,2:T(4,128)(2,1)}, u32[]{:S(2)}, u32[]{:S(2)}) async-start(bf16[1,3,128,256]{3,1,0,2:T(4,128)(2,1)} %copy.319), calls=%async_computation.11 | async-start | bytes 524288 | tf_op jit(solution)/shard_map/all_to_all | solution.py:205
  231.6 22.2 %copy-start.9 = (bf16[6,4,128,128]{2,3,1,0:T(8,128)(2,1)S(1)}, bf16[6,4,128,128]{2,3,1,0:T(8,128)(2,1)}, u32[]{:S(2)}) copy-start(bf16[6,4,128,128]{2,3,1,0:T(8,128)(2,1)} %multiply_convert_fusion) | copy-start | bytes 2359300
  246.5 22.6 %all-to-all-start.9 = ((bf16[1,3,128,256]{3,1,0,2:T(4,128)(2,1)}), bf16[1,3,128,256]{3,1,0,2:T(4,128)(2,1)}, u32[]{:S(2)}, u32[]{:S(2)}) async-start(bf16[1,3,128,256]{3,1,0,2:T(4,128)(2,1)} %copy.314), calls=%async_computation.10 | async-start | bytes 524288 | tf_op jit(solution)/shard_map/all_to_all | solution.py:202
  254.9 20.5 %copy-start.5 = (f32[6,128,4,64]{1,3,2,0:T(8,128)S(1)}, f32[6,128,4,64]{1,3,2,0:T(8,128)}, u32[]{:S(2)}) copy-start(f32[6,128,4,64]{1,3,2,0:T(8,128)} %copy-done.4) | copy-start | bytes 2359300
  269.1 21.8 %all-to-all-start.8 = ((bf16[1,3,128,256]{3,1,0,2:T(4,128)(2,1)}), bf16[1,3,128,256]{3,1,0,2:T(4,128)(2,1)S(1)}, u32[]{:S(2)}, u32[]{:S(2)}) async-start(bf16[1,3,128,256]{3,1,0,2:T(4,128)(2,1)} %copy.309), calls=%async_computation.9 | async-start | bytes 524288 | tf_op jit(solution)/shard_map/all_to_all | solution.py:199
  275.4 15.7 %copy-start.14 = (f32[6,128,4,64]{1,3,2,0:T(8,128)S(1)}, f32[6,128,4,64]{1,3,2,0:T(8,128)}, u32[]{:S(2)}) copy-start(f32[6,128,4,64]{1,3,2,0:T(8,128)} %copy-done.13) | copy-start | bytes 2359300
  (10 other events, 15.1 us)
Sparse Core Ops, SparseCore 0:
  198.5 23.9 reduce-scatter.1
where the time goes:
time: 300 us; the launch traced here: 299 us
  waiting for transfers between devices  103 us (34%)
  starting transfers between devices  95.8 us (32%)
  local copies, waits for them, and re-layouts  45.7 us (15%)
  matrix products  17.7 us (6%)
  between operations  14.6 us (5%)
  blocking collectives  12.2 us (4%)
  other arithmetic  9.94 us (3%)
    all_to_all x1, starting transfers between devices, body(): lax.all_to_all(to_columns(queries), 'band', split_axis=0, concat_axis=2,...  16.4 us
    unnamed x60, local copies, waits for them, and re-layouts  15.6 us
    all_to_all x1, starting transfers between devices, body(): lax.all_to_all(to_columns(attn_keys), 'band', split_axis=0, concat_axis=2...  14 us
    all_to_all x1, waiting for transfers between devices, body(): lax.all_to_all(grad_v[:, 3:].astype(jnp.bfloat16), 'band', split_axis=2,...  13.1 us
    all_gather x1, blocking collectives, body(): lax.all_gather(grad_out, 'head', axis=2, tiled=True)  12.2 us
    all_to_all x1, waiting for transfers between devices, body(): lax.all_to_all(to_columns(delta), 'band', split_axis=0, concat_axis=2, ti...  11.4 us
    all_to_all x1, waiting for transfers between devices, body(): lax.all_to_all(grad_q[:, 3:].astype(jnp.bfloat16), 'band', split_axis=2,...  11 us
    all_to_all x1, waiting for transfers between devices, body(): lax.all_to_all(to_columns(attn_values), 'band', split_axis=0, concat_axis...  10.9 us
  transfers between devices with their start and end apart: 12, of which 10 were waited for; matrix products, arithmetic and copies ran while one was open for 21% of the time, Pallas kernels for 0%

commit v1 on v0

v1 whole, which is shorter than its diff:
```python
import jax
import jax.numpy as jnp
from jax import lax
from jax.experimental import pallas as pl
from jax.experimental.pallas import tpu as pltpu
from jax.sharding import PartitionSpec as P

BF = jnp.bfloat16
F32 = jnp.float32
N = 128
HALF = 64
SENT = 18
MIXED = 14
FACTOR = 0.125
PARAMS = pltpu.CompilerParams(vmem_limit_bytes=48 * 1024 * 1024)
VMEM = pl.BlockSpec(memory_space=pltpu.VMEM)
SMEM = pl.BlockSpec(memory_space=pltpu.SMEM)


def nt(a, b):
    return lax.dot_general(a, b, (((1,), (1,)), ((), ())), preferred_element_type=F32)


def tn(a, b):
    return lax.dot_general(a, b, (((0,), (0,)), ((), ())), preferred_element_type=F32)


def nn(a, b):
    return lax.dot_general(a, b, (((1,), (0,)), ((), ())), preferred_element_type=F32)


def lane_masks():
    lane = lax.broadcasted_iota(jnp.int32, (N, N), 1)
    first = jnp.where(lane < HALF, 1.0, 0.0)
    return first.astype(BF), (1.0 - first).astype(BF)


def stack(x, masks):
    return jnp.concatenate([x * masks[0], x * masks[1]], axis=0)


def head_sums(product):
    row = lax.broadcasted_iota(jnp.int32, (8, 256), 0)
    lane = lax.broadcasted_iota(jnp.int32, (8, 256), 1)
    pick = jnp.where(lane // HALF == row, 1.0, 0.0).astype(BF)
    high = product.astype(BF)
    low = (product - high.astype(F32)).astype(BF)
    return nt(pick, high) + nt(pick, low)


def partners(axes_ref):
    axis = [axes_ref[b % 3, b // 3] for b in range(6)]
    found = []
    for b in range(6):
        other = jnp.int32(0)
        for c in range(6):
            if c != b:
                other = other + jnp.where(axis[c] == axis[b], jnp.int32(c), jnp.int32(0))
        found.append(other)
    return found


def pack_lines_kernel(q_ref, k_ref, v_ref, out_ref, stage):
    for a, ref in enumerate((q_ref, k_ref, v_ref)):
        for p in range(3):
            for g in range(2):
                rows = pl.ds(2 * (3 * a + p) + g, N, stride=SENT)
                stage[rows, :] = ref[p, :, N * g : N * g + N].astype(F32)
    out_ref[...] = stage[...].astype(BF)


def cotangent_kernel(own_ref, other_ref, proj_ref, out_ref):
    me = lax.axis_index("head")
    for ref, side in ((own_ref, me), (other_ref, 1 - me)):
        made = nt(ref[...], proj_ref[...]).astype(BF)
        for p in range(3):
            out_ref[p, pl.ds(pl.multiple_of(side * HALF, HALF), HALF), :] = made[
                HALF * p : HALF * p + HALF
            ]


def forward_kernel(
    axes_ref, q_ref, k_ref, v_ref, ga_ref, got_ref,
    send_ref, q6, k6, v6, near_ref, far_ref, totals_ref,
    stage, parts,
):
    partner = partners(axes_ref)
    masks = lane_masks()
    stage[...] = got_ref[...].astype(F32)
    for a, (mine, six) in enumerate(((q_ref, q6), (k_ref, k6), (v_ref, v6))):
        for p in range(3):
            six[p] = mine[p]
            for g in range(2):
                rows = pl.ds(2 * (3 * a + p) + g, N, stride=SENT)
                six[3 + p, :, N * g : N * g + N] = stage[rows, :].astype(BF)
    for b in range(6):
        for g in range(2):
            lanes = slice(N * g, N * g + N)
            queries = stack(q6[b, :, lanes] * BF(FACTOR), masks)
            scores = [nt(k6[partner[b], :, lanes], queries)]
            values = [v6[partner[b], :, lanes]]
            if b < 3:
                scores.append(nt(k6[b, :, lanes], queries))
                values.append(v6[b, :, lanes])
            top = jnp.max(scores[0], axis=0, keepdims=True)
            for s in scores[1:]:
                top = jnp.maximum(top, jnp.max(s, axis=0, keepdims=True))
            raised = [jnp.exp(s - top) for s in scores]
            total = jnp.sum(raised[0], axis=0, keepdims=True)
            for e in raised[1:]:
                total = total + jnp.sum(e, axis=0, keepdims=True)
            scale = 1.0 / total
            total = top + jnp.log(total)
            out = None
            for e, v in zip(raised, values):
                prob = (e * scale).astype(BF)
                both = jnp.concatenate([prob[:, :N], prob[:, N:]], axis=0)
                term = tn(both, stack(v, masks))
                out = term if out is None else out + term
            row = (0 if b < 3 else 24) + 4 * (b % 3) + 2 * g
            totals_ref[row : row + 1, :] = total[:, :N]
            totals_ref[row + 1 : row + 2, :] = total[:, N:]
            if b < 3:
                near_ref[b, :, lanes] = out
            else:
                far_ref[b - 3, :, lanes] = out.astype(BF)
    for p in range(3):
        totals_ref[12 + 4 * p : 16 + 4 * p, :] = head_sums(
            ga_ref[p].astype(F32) * near_ref[p]
        )[:4]
    totals_ref[36:40, :] = jnp.zeros((4, N), F32)
    parts[...] = jnp.zeros((N, N), F32)
    left = totals_ref[...]
    for piece in range(3):
        rounded = left.astype(BF).astype(F32)
        parts[40 * piece : 40 * piece + 40, :] = rounded
        left = left - rounded
    stage[pl.ds(12, N, stride=MIXED), :] = jnp.transpose(parts[...])
    stage[pl.ds(13, N, stride=MIXED), :] = jnp.zeros((N, N), F32)
    for p in range(3):
        for g in range(2):
            lanes = slice(N * g, N * g + N)
            stage[pl.ds(2 * p + g, N, stride=MIXED), :] = far_ref[p, :, lanes].astype(F32)
            stage[pl.ds(6 + 2 * p + g, N, stride=MIXED), :] = ga_ref[p, :, lanes].astype(F32)
    send_ref[...] = stage[: MIXED * N, :].astype(BF)


def both_totals(near, far):
    top = jnp.maximum(near, far)
    log_all = top + jnp.log(jnp.exp(near - top) + jnp.exp(far - top))
    return log_all, jnp.exp(near - log_all), jnp.exp(far - log_all)


def backward_kernel(
    axes_ref, q6, k6, v6, ga_ref, near_ref, far_ref, totals_ref, got_ref,
    att_ref, dq_ref, dk_ref, dv_ref, send_ref,
    stage, parts, ga6, log_all_ref, delta_ref, dk6, dv6,
):
    partner = partners(axes_ref)
    masks = lane_masks()
    stage[: MIXED * N, :] = got_ref[...].astype(F32)
    parts[...] = jnp.transpose(stage[pl.ds(12, N, stride=MIXED), :])
    arrived = parts[0:40, :] + (parts[40:80, :] + parts[80:120, :])
    for p in range(3):
        ga6[p] = ga_ref[p]
        for g in range(2):
            ga6[3 + p, :, N * g : N * g + N] = stage[
                pl.ds(6 + 2 * p + g, N, stride=MIXED), :
            ].astype(BF)
    row_log, row_near, row_far = both_totals(totals_ref[0:12, :], arrived[24:36])
    col_log, col_near, col_far = both_totals(arrived[0:12], totals_ref[24:36, :])
    log_all_ref[0:12, :] = row_log
    log_all_ref[12:24, :] = col_log
    row_delta = row_near * totals_ref[12:24, :]
    col_delta = col_near * arrived[12:24]
    for p in range(3):
        far_row = jnp.concatenate(
            [stage[pl.ds(2 * p + g, N, stride=MIXED), :] for g in range(2)], axis=1
        )
        heads = slice(4 * p, 4 * p + 4)
        delta_ref[4 * p : 4 * p + 4, :] = (
            row_delta[heads] + row_far[heads] * head_sums(ga_ref[p].astype(F32) * far_row)[:4]
        )
        delta_ref[12 + 4 * p : 16 + 4 * p, :] = (
            col_delta[heads]
            + col_far[heads]
            * head_sums(ga6[3 + p].astype(F32) * far_ref[p].astype(F32))[:4]
        )
    parts[0:12, :] = row_near
    parts[12:24, :] = row_far
    weights = jnp.transpose(parts[...])
    lane = lax.broadcasted_iota(jnp.int32, (N, N), 1)
    for p in range(3):
        for g in range(2):
            r = 4 * p + 2 * g
            near_weight = jnp.where(lane < HALF, weights[:, r : r + 1], weights[:, r + 1 : r + 2])
            far_weight = jnp.where(
                lane < HALF, weights[:, 12 + r : 13 + r], weights[:, 13 + r : 14 + r]
            )
            att_ref[p, :, N * g : N * g + N] = (
                near_weight * near_ref[p, :, N * g : N * g + N]
                + far_weight * stage[pl.ds(2 * p + g, N, stride=MIXED), :]
            ).astype(BF)
    dk6[3:] = jnp.zeros((3, N, 256), F32)
    dv6[3:] = jnp.zeros((3, N, 256), F32)

    def pair_step(b, c, g):
        lanes = slice(N * g, N * g + N)
        queries = stack(q6[b, :, lanes] * BF(FACTOR), masks)
        grads = stack(ga6[b, :, lanes], masks)
        r = 4 * b + 2 * g
        log_all = jnp.concatenate([log_all_ref[r : r + 1, :], log_all_ref[r + 1 : r + 2, :]], axis=1)
        delta = jnp.concatenate([delta_ref[r : r + 1, :], delta_ref[r + 1 : r + 2, :]], axis=1)
        keys = k6[c, :, lanes]
        prob = jnp.exp(nt(keys, queries) - log_all).astype(BF)
        step = (prob.astype(F32) * (nt(v6[c, :, lanes], grads) - delta)).astype(BF)
        tall = jnp.concatenate([step[:, :N], step[:, N:]], axis=0)
        return tn(tall, stack(keys, masks)) * FACTOR, nn(step, queries), nn(prob, grads)

    for b in range(3):
        for g in range(2):
            lanes = slice(N * g, N * g + N)
            dq_ref[b, :, lanes], dk6[b, :, lanes], dv6[b, :, lanes] = pair_step(b, b, g)
    for b in range(6):
        for g in range(2):
            lanes = slice(N * g, N * g + N)
            dq, dk, dv = pair_step(b, partner[b], g)
            if b < 3:
                dq_ref[b, :, lanes] += dq
            else:
                stage[pl.ds(2 * (b - 3) + g, N, stride=SENT), :] = dq
            dk6[partner[b], :, lanes] += dk
            dv6[partner[b], :, lanes] += dv
    for p in range(3):
        dk_ref[p] = dk6[p]
        dv_ref[p] = dv6[p]
        for g in range(2):
            lanes = slice(N * g, N * g + N)
            stage[pl.ds(6 + 2 * p + g, N, stride=SENT), :] = dk6[3 + p, :, lanes]
            stage[pl.ds(12 + 2 * p + g, N, stride=SENT), :] = dv6[3 + p, :, lanes]
    send_ref[...] = stage[...].astype(BF)


def finish_kernel(dq_ref, dk_ref, dv_ref, got_ref, q_out, k_out, v_out, stage):
    stage[...] = got_ref[...].astype(F32)
    for a, (mine, out) in enumerate(((dq_ref, q_out), (dk_ref, k_out), (dv_ref, v_out))):
        for p in range(3):
            for g in range(2):
                lanes = slice(N * g, N * g + N)
                rows = pl.ds(2 * (3 * a + p) + g, N, stride=SENT)
                out[p, :, lanes] = (mine[p, :, lanes] + stage[rows, :]).astype(BF)


def shape(*dims, dtype=BF):
    return jax.ShapeDtypeStruct(dims, dtype)


def cost(flops, moved):
    return pl.CostEstimate(flops=flops, bytes_accessed=moved, transcendentals=0)


def exchange(sent, rows):
    sent = sent.reshape(N, rows // 2, 2, N)
    got = lax.all_to_all(sent, "band", split_axis=0, concat_axis=0, tiled=True)
    return got.reshape(N * rows, N)


def body(queries, attn_keys, attn_values, out_proj, grad_out, plane_axes):
    me = lax.axis_index("head")
    swap = [(0, 1), (1, 0)]
    q, k, v = queries[0], attn_keys[0], attn_values[0]
    line = (3, N, 256)
    stage = pltpu.VMEM((SENT * N, N), F32)
    square = pltpu.VMEM((N, N), F32)

    own_cotangent = grad_out.reshape(3 * HALF, 1024)
    other_cotangent = lax.ppermute(own_cotangent, "head", swap)
    sent = pl.pallas_call(
        pack_lines_kernel,
        out_shape=shape(SENT * N, N),
        in_specs=[VMEM] * 3,
        out_specs=VMEM,
        scratch_shapes=[stage],
        compiler_params=PARAMS,
        name="pack_lines",
    )(q, k, v)
    lines = exchange(sent, SENT)
    grad_attended = pl.pallas_call(
        cotangent_kernel,
        out_shape=shape(*line),
        in_specs=[VMEM] * 3,
        out_specs=VMEM,
        compiler_params=PARAMS,
        cost_estimate=cost(2 * 384 * 1024 * 256, 1500000),
        name="cotangent",
    )(own_cotangent, other_cotangent, out_proj)

    sent, q6, k6, v6, near_out, far_out, totals = pl.pallas_call(
        forward_kernel,
        out_shape=(
            shape(MIXED * N, N),
            shape(6, N, 256),
            shape(6, N, 256),
            shape(6, N, 256),
            shape(*line, dtype=F32),
            shape(*line),
            shape(40, N, dtype=F32),
        ),
        in_specs=[SMEM] + [VMEM] * 5,
        out_specs=(VMEM,) * 7,
        scratch_shapes=[stage, square],
        compiler_params=PARAMS,
        name="forward",
    )(plane_axes, q, k, v, grad_attended, lines)
    mixed = exchange(sent, MIXED)

    attended, dq, dk, dv, sent = pl.pallas_call(
        backward_kernel,
        out_shape=(
            shape(*line),
            shape(*line, dtype=F32),
            shape(*line, dtype=F32),
            shape(*line, dtype=F32),
            shape(SENT * N, N),
        ),
        in_specs=[SMEM] + [VMEM] * 8,
        out_specs=(VMEM,) * 5,
        scratch_shapes=[
            stage,
            square,
            pltpu.VMEM((6, N, 256), BF),
            pltpu.VMEM((24, N), F32),
            pltpu.VMEM((24, N), F32),
            pltpu.VMEM((6, N, 256), F32),
            pltpu.VMEM((6, N, 256), F32),
        ],
        compiler_params=PARAMS,
        name="backward",
    )(plane_axes, q6, k6, v6, grad_attended, near_out, far_out, totals, mixed)
    returned = exchange(sent, SENT)

    def share(side):
        part = lax.dynamic_slice_in_dim(attended, side * HALF, HALF, axis=1)
        return jnp.dot(part.reshape(3 * HALF, 256), out_proj, preferred_element_type=F32)

    arrived = lax.ppermute(share(1 - me).astype(BF), "head", swap)
    layer_out = (share(me) + arrived.astype(F32)).astype(BF).reshape(1, 3, HALF, 1024)

    dq, dk, dv = pl.pallas_call(
        finish_kernel,
        out_shape=(shape(*line),) * 3,
        in_specs=[VMEM] * 4,
        out_specs=(VMEM,) * 3,
        scratch_shapes=[stage],
        compiler_params=PARAMS,
        name="finish",
    )(dq, dk, dv, returned)
    return layer_out, dq[None], dk[None], dv[None]


def solution(mesh):
    lines = P("band", None, None, "head")
    columns = P("band", None, "head", None)
    return jax.shard_map(
        body,
        mesh=mesh,
        in_specs=(lines, lines, lines, P("head", None), columns, P()),
        out_specs=(columns, lines, lines, lines),
        check_vma=False,
    )
```

time: 300 us -> 118 us (0.39)
  starting transfers between devices: 95.8 us -> 25.4 us
  waiting for transfers between devices: 103 us -> 41.1 us
  local copies, waits for them, and re-layouts: 45.7 us -> 2.91 us
  blocking collectives: 12.2 us -> 33.1 us
  matrix products: 17.7 us -> 1.29 us
  between operations: 14.6 us -> 0.72 us
  Pallas kernels: 0 us -> 12.8 us
  other arithmetic: 9.94 us -> 0 us
    all_to_all x11 -> x2, waiting for transfers between devices: 103 us -> 0.25 us  [exchange(): got = lax.all_to_all(sent, 'band', split_axis=0, concat_axis=0, tiled=True)]
    all_to_all x11 -> x2, starting transfers between devices: 95.6 us -> 23.6 us  [exchange(): got = lax.all_to_all(sent, 'band', split_axis=0, concat_axis=0, tiled=True)]
    ppermute x0 -> x2, waiting for transfers between devices: none -> 40.8 us  [the longest x1 20.5 us: body(): other_cotangent = lax.ppermute(own_cotangent, 'head', swap)]
    all_to_all x0 -> x1, blocking collectives: none -> 33.1 us  [exchange(): got = lax.all_to_all(sent, 'band', split_axis=0, concat_axis=0, tiled=True)]
    dot_general x15 -> x2, matrix products: 17.7 us -> 1.29 us  [share(): jnp.dot(part.reshape(3 * HALF, 256), out_proj, preferred_element_type=F32)]
    pallas_call x0 -> x5, Pallas kernels: none -> 12.8 us  [the longest x1 6.77 us: body(): pl.pallas_call(backward_kernel, out_shape=(shape(*line), shape(*line, dty...]
    unnamed x60 -> x19, local copies, waits for them, and re-layouts: 15.6 us -> 2.89 us
    all_gather x1 -> x0, blocking collectives: 12.2 us -> none  [body(): lax.all_gather(grad_out, 'head', axis=2, tiled=True)]
  transfers between devices with their start and end apart: 12 -> 4, of which waited for: 10 -> 3; matrix products, arithmetic and copies ran while one was open for 21% -> 1% of each run, Pallas kernels for 0% -> 0%
where the time goes in v1:
time: 118 us; the launch traced here: 117 us
  waiting for transfers between devices  41.1 us (35%)
  blocking collectives  33.1 us (28%)
  starting transfers between devices  25.4 us (22%)
  Pallas kernels  12.8 us (11%)
  local copies, waits for them, and re-layouts  2.91 us (2%)
  matrix products  1.29 us (1%)
    all_to_all x1, blocking collectives, exchange(): got = lax.all_to_all(sent, 'band', split_axis=0, concat_axis=0, tiled=True)  33.1 us
    all_to_all x2, starting transfers between devices, exchange(): got = lax.all_to_all(sent, 'band', split_axis=0, concat_axis=0, tiled=True)  23.6 us
    ppermute x1, waiting for transfers between devices, body(): other_cotangent = lax.ppermute(own_cotangent, 'head', swap)  20.5 us
    ppermute x1, waiting for transfers between devices, body(): arrived = lax.ppermute(share(1 - me).astype(BF), 'head', swap)  20.3 us
    pallas_call x1, Pallas kernels, body(): pl.pallas_call(backward_kernel, out_shape=(shape(*line), shape(*line, dty...  6.77 us
    pallas_call x1, Pallas kernels, body(): pl.pallas_call(forward_kernel, out_shape=(shape(MIXED * N, N), shape(6, N...  3.63 us
    unnamed x19, local copies, waits for them, and re-layouts  2.89 us
  transfers between devices with their start and end apart: 4, of which 3 were waited for; matrix products, arithmetic and copies ran while one was open for 1% of the time, Pallas kernels for 0%

profile of v1, /device:TPU:1, one launch (start us, length us, event | category | flops | bytes accessed | tf_op | source)
XLA Modules:
  0.0 117.3 jit_solution(16946398268701371201)
XLA Ops:
  0.6 0.0 copy-start.1
  0.6 0.9 copy-done.1
  1.6 0.9 copy-done.3
  2.5 0.9 copy-done.5
  3.4 1.0 pack_lines.1
  4.4 16.5 %all-to-all-start = ((bf16[128,9,2,128]{3,2,1,0:T(2,128)(2,1)}), bf16[128,9,2,128]{3,2,1,0:T(2,128)(2,1)S(1)}, u32[]{:S(2)}, u32[]{:S(2)}) async-start(bf16[128,9,2,128]{3,2,1,0:T(2,128)(2,1)} %bitcast.4), calls=%async_computation | async-start | bytes 1179648 | tf_op jit(solution)/shard_map/all_to_all | solution.py:264
  20.9 0.0 copy-start.8
  20.9 0.0 copy-done.7
  20.9 0.8 collective-permute-start
  21.8 0.1 copy.11.axes_ref
  21.9 20.5 %collective-permute-done.other_ref = bf16[192,1024]{1,0:T(8,128)(2,1)S(1)} collective-permute-done((bf16[192,1024]{1,0:T(8,128)(2,1)S(1)}, bf16[192,1024]{1,0:T(8,128)(2,1)S(1)}, u32[]{:S(2)}, u32[]{:S(2)}) %collective-permute-start) | collective-permute-done | bytes 393248 | tf_op jit(solution)/shard_map/ppermute | solution.py:277
  42.4 0.0 copy-done
  42.4 0.5 cotangent.1.ga_ref
  42.9 0.2 all-to-all-done
  43.2 3.6 %forward.1 = (bf16[1792,128]{1,0:T(8,128)(2,1)S(1)}, bf16[6,128,256]{2,1,0:T(8,128)(2,1)S(1)}, bf16[6,128,256]{2,1,0:T(8,128)(2,1)S(1)}, bf16[6,128,256]{2,1,0:T...) custom-call(s32[3,2]{1,0:T(4,128)S(1)} %copy.11.axes_ref, ...), custom_call_target="tpu_custom_call" | custom-call | tf_op jit(solution)/shard_map/forward/pallas_call | solution.py:298
  46.8 33.1 %all_to_all.15 = bf16[128,7,2,128]{3,2,1,0:T(2,128)(2,1)S(1)} all-to-all(bf16[128,7,2,128]{3,2,1,0:T(2,128)(2,1)S(1)} %bitcast.29), channel_id=1, replica_groups=mesh['band'=128,'head'=2] {'band'}, dimensions={0} | all-to-all | bytes 917504 | tf_op jit(solution)/shard_map/all_to_all | solution.py:264
  79.9 6.8 %backward.1 = (bf16[3,128,256]{2,1,0:T(8,128)(2,1)S(1)}, f32[3,128,256]{2,1,0:T(8,128)S(1)}, f32[3,128,256]{2,1,0:T(8,128)S(1)}, f32[3,128,256]{2,1,0:T(8,128)S(1)}, bf16[2304,128]{1,0:T(8,128)(2,1)}) custom-call(s32[3,2]{1,0:T(4,128)S(1)} %copy.11.axes_ref, bf16[6,128,256]{2,1,0:T(8,128)(2,1)S(1)} %get-tuple-element.19.q6, ...), custom_call_target="tpu_custom_call" | custom-call | tf_op jit(solution)/shard_map/backward/pallas_call | solution.py:317
  86.7 7.0 %all-to-all-start.2 = ((bf16[128,9,2,128]{3,2,1,0:T(2,128)(2,1)}), bf16[128,9,2,128]{3,2,1,0:T(2,128)(2,1)S(1)}, u32[]{:S(2)}, u32[]{:S(2)}) async-start(bf16[128,9,2,128]{3,2,1,0:T(2,128)(2,1)} %bitcast.11), calls=%async_computation.2 | async-start | bytes 1179648 | tf_op jit(solution)/shard_map/all_to_all | solution.py:264
  93.8 0.3 convolution_convert_fusion
  94.0 1.0 collective-permute-start.1
  95.0 20.3 %collective-permute-done.1 = bf16[192,1024]{1,0:T(8,128)(2,1)S(1)} collective-permute-done((bf16[192,1024]{1,0:T(8,128)(2,1)S(1)}, bf16[192,1024]{1,0:T(8,128)(2,1)S(1)}, u32[]{:S(2)}, u32[]{:S(2)}) %collective-permute-start.1) | collective-permute-done | bytes 393248 | tf_op jit(solution)/shard_map/ppermute | solution.py:346
  115.3 1.0 add_convert_fusion
  116.3 0.0 all-to-all-done.2
  116.3 0.9 finish.1
  (12 shorter events, 0.0 us)
Async XLA Ops:
  0.6 0.9 copy-start.1
  1.6 0.9 copy-start.3
  2.5 0.9 copy-start.5
  4.4 16.6 %copy-start.7 = (bf16[1,3,64,1024]{3,2,1,0:T(8,128)(2,1)S(1)}, bf16[1,3,64,1024]{3,2,1,0:T(8,128)(2,1)}, u32[]{:S(2)}) copy-start(bf16[1,3,64,1024]{3,2,1,0:T(8,128)(2,1)} %param.10) | copy-start | bytes 1179652
  4.4 38.0 %copy-start = (bf16[256,1024]{1,0:T(8,128)(2,1)S(1)}, bf16[256,1024]{1,0:T(8,128)(2,1)}, u32[]{:S(2)}) copy-start(bf16[256,1024]{1,0:T(8,128)(2,1)} %proj_ref.1) | copy-start | bytes 1572868
  4.4 38.8 %all-to-all-start = ((bf16[128,9,2,128]{3,2,1,0:T(2,128)(2,1)}), bf16[128,9,2,128]{3,2,1,0:T(2,128)(2,1)S(1)}, u32[]{:S(2)}, u32[]{:S(2)}) async-start(bf16[128,9,2,128]{3,2,1,0:T(2,128)(2,1)} %bitcast.4), calls=%async_computation | async-start | bytes 1179648 | tf_op jit(solution)/shard_map/all_to_all | solution.py:264
  20.9 0.8 copy-start.8
  20.9 21.5 %collective-permute-start = (bf16[192,1024]{1,0:T(8,128)(2,1)S(1)}, bf16[192,1024]{1,0:T(8,128)(2,1)S(1)}, u32[]{:S(2)}, u32[]{:S(2)}) collective-permute-start(bf16[192,1024]{1,0:T(8,128)(2,1)S(1)} %bitcast.30), channel_id=1, source_target_pairs={{0,1},{1,0},{2,3},{3,2},{4,5},{5,4},{6,7},{7,6},{8,9},{9,8},{10,11... | collective-permute-start | bytes 1179656 | tf_op jit(solution)/shard_map/ppermute | solution.py:277
  21.9 21.3 %copy-start.2 = (bf16[1,3,128,256]{3,2,1,0:T(8,128)(2,1)S(1)}, bf16[1,3,128,256]{3,2,1,0:T(8,128)(2,1)}, u32[]{:S(2)}) copy-start(bf16[1,3,128,256]{3,2,1,0:T(8,128)(2,1)} %param.6) | copy-start | bytes 589828
  21.9 21.3 %copy-start.4 = (bf16[1,3,128,256]{3,2,1,0:T(8,128)(2,1)S(1)}, bf16[1,3,128,256]{3,2,1,0:T(8,128)(2,1)}, u32[]{:S(2)}) copy-start(bf16[1,3,128,256]{3,2,1,0:T(8,128)(2,1)} %param.7) | copy-start | bytes 589828
  21.9 21.3 %copy-start.6 = (bf16[1,3,128,256]{3,2,1,0:T(8,128)(2,1)S(1)}, bf16[1,3,128,256]{3,2,1,0:T(8,128)(2,1)}, u32[]{:S(2)}) copy-start(bf16[1,3,128,256]{3,2,1,0:T(8,128)(2,1)} %param.8) | copy-start | bytes 589828
  86.7 29.6 %all-to-all-start.2 = ((bf16[128,9,2,128]{3,2,1,0:T(2,128)(2,1)}), bf16[128,9,2,128]{3,2,1,0:T(2,128)(2,1)S(1)}, u32[]{:S(2)}, u32[]{:S(2)}) async-start(bf16[128,9,2,128]{3,2,1,0:T(2,128)(2,1)} %bitcast.11), calls=%async_computation.2 | async-start | bytes 1179648 | tf_op jit(solution)/shard_map/all_to_all | solution.py:264
  94.0 21.3 %collective-permute-start.1 = (bf16[192,1024]{1,0:T(8,128)(2,1)S(1)}, bf16[192,1024]{1,0:T(8,128)(2,1)S(1)}, u32[]{:S(2)}, u32[]{:S(2)}) collective-permute-start(bf16[192,1024]{1,0:T(8,128)(2,1)S(1)} %convolution_convert_fusion), channel_id=1, source_target_pairs={{0,1},{1,0},{2,3},{3,2},{4,5},{5,4},{6,7},{7,6},{8,9},{9,8},{10,11... | collective-permute-start | bytes 1179656 | tf_op jit(solution)/shard_map/ppermute | solution.py:346

commit v2 on v1

--- a/solution.py
+++ b/solution.py
@@ -12,7 +12,9 @@
 SENT = 18
 MIXED = 14
 FACTOR = 0.125
+LONG = 60 * 10**9
 PARAMS = pltpu.CompilerParams(vmem_limit_bytes=48 * 1024 * 1024)
+ROOMY = pltpu.CompilerParams(vmem_limit_bytes=60 * 1024 * 1024)
 VMEM = pl.BlockSpec(memory_space=pltpu.VMEM)
 SMEM = pl.BlockSpec(memory_space=pltpu.SMEM)
 
@@ -60,12 +62,19 @@
     return found
 
 
-def pack_lines_kernel(q_ref, k_ref, v_ref, out_ref, stage):
-    for a, ref in enumerate((q_ref, k_ref, v_ref)):
+def pack_lines_kernel(q_ref, k_ref, v_ref, out_ref, held, stage, sems):
+    copies = [
+        pltpu.make_async_copy(ref, held.at[a], sems.at[a])
+        for a, ref in enumerate((q_ref, k_ref, v_ref))
+    ]
+    for copy in copies:
+        copy.start()
+    for a, copy in enumerate(copies):
+        copy.wait()
         for p in range(3):
             for g in range(2):
                 rows = pl.ds(2 * (3 * a + p) + g, N, stride=SENT)
-                stage[rows, :] = ref[p, :, N * g : N * g + N].astype(F32)
+                stage[rows, :] = held[a, p, :, N * g : N * g + N].astype(F32)
     out_ref[...] = stage[...].astype(BF)
 
 
@@ -151,20 +160,17 @@
     return log_all, jnp.exp(near - log_all), jnp.exp(far - log_all)
 
 
-def backward_kernel(
-    axes_ref, q6, k6, v6, ga_ref, near_ref, far_ref, totals_ref, got_ref,
-    att_ref, dq_ref, dk_ref, dv_ref, send_ref,
-    stage, parts, ga6, log_all_ref, delta_ref, dk6, dv6,
+def merge_kernel(
+    ga_ref, near_ref, far_ref, totals_ref, proj_ref, got_ref,
+    ga_col_ref, log_all_ref, delta_ref, given_ref, kept_ref,
+    stage, parts, att,
 ):
-    partner = partners(axes_ref)
-    masks = lane_masks()
-    stage[: MIXED * N, :] = got_ref[...].astype(F32)
+    stage[...] = got_ref[...].astype(F32)
     parts[...] = jnp.transpose(stage[pl.ds(12, N, stride=MIXED), :])
     arrived = parts[0:40, :] + (parts[40:80, :] + parts[80:120, :])
     for p in range(3):
-        ga6[p] = ga_ref[p]
-        for g in range(2):
-            ga6[3 + p, :, N * g : N * g + N] = stage[
+        for g in range(2):
+            ga_col_ref[p, :, N * g : N * g + N] = stage[
                 pl.ds(6 + 2 * p + g, N, stride=MIXED), :
             ].astype(BF)
     row_log, row_near, row_far = both_totals(totals_ref[0:12, :], arrived[24:36])
@@ -184,7 +190,7 @@
         delta_ref[12 + 4 * p : 16 + 4 * p, :] = (
             col_delta[heads]
             + col_far[heads]
-            * head_sums(ga6[3 + p].astype(F32) * far_ref[p].astype(F32))[:4]
+            * head_sums(ga_col_ref[p].astype(F32) * far_ref[p].astype(F32))[:4]
         )
     parts[0:12, :] = row_near
     parts[12:24, :] = row_far
@@ -197,10 +203,31 @@
             far_weight = jnp.where(
                 lane < HALF, weights[:, 12 + r : 13 + r], weights[:, 13 + r : 14 + r]
             )
-            att_ref[p, :, N * g : N * g + N] = (
+            att[p, :, N * g : N * g + N] = (
                 near_weight * near_ref[p, :, N * g : N * g + N]
                 + far_weight * stage[pl.ds(2 * p + g, N, stride=MIXED), :]
             ).astype(BF)
+    me = lax.axis_index("head")
+    for side, out in ((1 - me, given_ref), (me, kept_ref)):
+        tokens = pl.ds(pl.multiple_of(side * HALF, HALF), HALF)
+        for p in range(3):
+            out[HALF * p : HALF * p + HALF, :] = nn(att[p, tokens, :], proj_ref[...]).astype(out.dtype)
+
+
+def layer_kernel(kept_ref, got_ref, out_ref):
+    out_ref[...] = (kept_ref[...] + got_ref[...].astype(F32)).astype(BF)
+
+
+def backward_kernel(
+    axes_ref, q6, k6, v6, ga_ref, ga_col_ref, log_all_ref, delta_ref,
+    dq_ref, dk_ref, dv_ref, send_ref,
+    stage, ga6, dk6, dv6,
+):
+    partner = partners(axes_ref)
+    masks = lane_masks()
+    for p in range(3):
+        ga6[p] = ga_ref[p]
+        ga6[3 + p] = ga_col_ref[p]
     dk6[3:] = jnp.zeros((3, N, 256), F32)
     dv6[3:] = jnp.zeros((3, N, 256), F32)
 
@@ -266,7 +293,6 @@
 
 
 def body(queries, attn_keys, attn_values, out_proj, grad_out, plane_axes):
-    me = lax.axis_index("head")
     swap = [(0, 1), (1, 0)]
     q, k, v = queries[0], attn_keys[0], attn_values[0]
     line = (3, N, 256)
@@ -278,10 +304,10 @@
     sent = pl.pallas_call(
         pack_lines_kernel,
         out_shape=shape(SENT * N, N),
-        in_specs=[VMEM] * 3,
+        in_specs=[pl.BlockSpec(memory_space=pltpu.HBM)] * 3,
         out_specs=VMEM,
-        scratch_shapes=[stage],
-        compiler_params=PARAMS,
+        scratch_shapes=[pltpu.VMEM((3, *line), BF), stage, pltpu.SemaphoreType.DMA((3,))],
+        compiler_params=ROOMY,
         name="pack_lines",
     )(q, k, v)
     lines = exchange(sent, SENT)
@@ -291,7 +317,7 @@
         in_specs=[VMEM] * 3,
         out_specs=VMEM,
         compiler_params=PARAMS,
-        cost_estimate=cost(2 * 384 * 1024 * 256, 1500000),
+        cost_estimate=cost(LONG, 1500000),
         name="cotangent",
     )(own_cotangent, other_cotangent, out_proj)
 
@@ -314,37 +340,52 @@
     )(plane_axes, q, k, v, grad_attended, lines)
     mixed = exchange(sent, MIXED)
 
-    attended, dq, dk, dv, sent = pl.pallas_call(
+    tokens = (3 * HALF, 1024)
+    ga_columns, log_all, delta, given, kept = pl.pallas_call(
+        merge_kernel,
+        out_shape=(
+            shape(*line),
+            shape(24, N, dtype=F32),
+            shape(24, N, dtype=F32),
+            shape(*tokens),
+            shape(*tokens, dtype=F32),
+        ),
+        in_specs=[VMEM] * 6,
+        out_specs=(VMEM,) * 5,
+        scratch_shapes=[pltpu.VMEM((MIXED * N, N), F32), square, pltpu.VMEM(line, BF)],
+        compiler_params=PARAMS,
+        name="merge",
+    )(grad_attended, near_out, far_out, totals, out_proj, mixed)
+    arrived = lax.ppermute(given, "head", swap)
+    dq, dk, dv, sent = pl.pallas_call(
         backward_kernel,
         out_shape=(
-            shape(*line),
             shape(*line, dtype=F32),
             shape(*line, dtype=F32),
             shape(*line, dtype=F32),
             shape(SENT * N, N),
         ),
-        in_specs=[SMEM] + [VMEM] * 8,
-        out_specs=(VMEM,) * 5,
+        in_specs=[SMEM] + [VMEM] * 7,
+        out_specs=(VMEM,) * 4,
         scratch_shapes=[
             stage,
-            square,
             pltpu.VMEM((6, N, 256), BF),
-            pltpu.VMEM((24, N), F32),
-            pltpu.VMEM((24, N), F32),
             pltpu.VMEM((6, N, 256), F32),
             pltpu.VMEM((6, N, 256), F32),
         ],
         compiler_params=PARAMS,
         name="backward",
-    )(plane_axes, q6, k6, v6, grad_attended, near_out, far_out, totals, mixed)
+    )(plane_axes, q6, k6, v6, grad_attended, ga_columns, log_all, delta)
     returned = exchange(sent, SENT)
-
-    def share(side):
-        part = lax.dynamic_slice_in_dim(attended, side * HALF, HALF, axis=1)
-        return jnp.dot(part.reshape(3 * HALF, 256), out_proj, preferred_element_type=F32)
-
-    arrived = lax.ppermute(share(1 - me).astype(BF), "head", swap)
-    layer_out = (share(me) + arrived.astype(F32)).astype(BF).reshape(1, 3, HALF, 1024)
+    layer_out = pl.pallas_call(
+        layer_kernel,
+        out_shape=shape(*tokens),
+        in_specs=[VMEM] * 2,
+        out_specs=VMEM,
+        compiler_params=PARAMS,
+        cost_estimate=cost(LONG, 1500000),
+        name="layer",
+    )(kept, arrived).reshape(1, 3, HALF, 1024)
 
     dq, dk, dv = pl.pallas_call(
         finish_kernel,

time: 118 us -> 111 us (0.941)
  blocking collectives: 33.1 us -> 25.5 us
  Pallas kernels: 12.8 us -> 15.9 us
  local copies, waits for them, and re-layouts: 2.91 us -> 0.12 us
  waiting for transfers between devices: 41.1 us -> 42.8 us
  matrix products: 1.29 us -> 0 us
    all_to_all x2, waiting for transfers between devices: 0.25 us -> 42.8 us  [exchange(): got = lax.all_to_all(sent, 'band', split_axis=0, concat_axis=0, tiled=True)]
    ppermute x1, waiting for transfers between devices: 20.5 us -> 0.01 us  [body(): other_cotangent = lax.ppermute(own_cotangent, 'head', swap)]
    ppermute x1, waiting for transfers between devices: 20.3 us -> 0.01 us  [body(): arrived = lax.ppermute(given, 'head', swap)]
    all_to_all x1, blocking collectives: 33.1 us -> 25.5 us  [exchange(): got = lax.all_to_all(sent, 'band', split_axis=0, concat_axis=0, tiled=True)]
    unnamed x19 -> x13, local copies, waits for them, and re-layouts: 2.89 us -> 0.12 us
    pallas_call x1 -> x3, Pallas kernels: 6.77 us -> 8.79 us  [the longest x1 6.56 us: body(): pl.pallas_call(backward_kernel, out_shape=(shape(*line, dtype=F32), shape...]
    ppermute x1, starting transfers between devices: 0.83 us -> 2.55 us  [body(): other_cotangent = lax.ppermute(own_cotangent, 'head', swap)]
    dot_general x2 -> x0, matrix products: 1.29 us -> none  [share(): jnp.dot(part.reshape(3 * HALF, 256), out_proj, preferred_element_type=F32)]
  transfers between devices with their start and end apart: 4 -> 4, of which waited for: 3 -> 2; matrix products, arithmetic and copies ran while one was open for 1% -> 0% of each run, Pallas kernels for 0% -> 9%
where the time goes in v2:
time: 111 us
  waiting for transfers between devices  42.8 us (39%)
  starting transfers between devices  25.8 us (23%)
  blocking collectives  25.5 us (23%)
  Pallas kernels  15.9 us (14%)
    all_to_all x2, waiting for transfers between devices, exchange(): got = lax.all_to_all(sent, 'band', split_axis=0, concat_axis=0, tiled=True)  42.8 us
    all_to_all x1, blocking collectives, exchange(): got = lax.all_to_all(sent, 'band', split_axis=0, concat_axis=0, tiled=True)  25.5 us
    all_to_all x2, starting transfers between devices, exchange(): got = lax.all_to_all(sent, 'band', split_axis=0, concat_axis=0, tiled=True)  23 us
    pallas_call x1, Pallas kernels, body(): pl.pallas_call(backward_kernel, out_shape=(shape(*line, dtype=F32), shape...  6.56 us
    pallas_call x1, Pallas kernels, body(): pl.pallas_call(forward_kernel, out_shape=(shape(MIXED * N, N), shape(6, N...  3.62 us
    ppermute x1, starting transfers between devices, body(): other_cotangent = lax.ppermute(own_cotangent, 'head', swap)  2.55 us
  transfers between devices with their start and end apart: 4, of which 2 were waited for; matrix products, arithmetic and copies ran while one was open for 0% of the time, Pallas kernels for 9%

profile of v2, /device:TPU:1, one launch (start us, length us, event | category | flops | bytes accessed | tf_op | source)
XLA Modules:
  0.0 110.8 jit_solution(14918629070906580603)
XLA Ops:
  0.6 2.6 %collective-permute-start = (bf16[192,1024]{1,0:T(8,128)(2,1)}, bf16[192,1024]{1,0:T(8,128)(2,1)S(1)}, u32[]{:S(2)}, u32[]{:S(2)}) collective-permute-start(bf16[192,1024]{1,0:T(8,128)(2,1)} %bitcast.24), channel_id=1, source_target_pairs={{0,1},{1,0},{2,3},{3,2},{4,5},{5,4},{6,7},{7,6},{8,9},{9,8},{10,11... | collective-permute-start | bytes 1179656 | tf_op jit(solution)/shard_map/ppermute | solution.py:303
  3.2 2.0 %pack_lines.1 = bf16[2304,128]{1,0:T(8,128)(2,1)} custom-call(bf16[3,128,256]{2,1,0:T(8,128)(2,1)} %bitcast.17, bf16[3,128,256]{2,1,0:T(8,128)(2,1)} %bitcast.19, bf16[3,128,256]{2,1,0:T(8,128)(2,1)} %bitcast.21), custom_call_target="tpu_custom_call" | custom-call | tf_op jit(solution)/shard_map/pack_lines/pallas_call | solution.py:304
  5.2 0.0 copy-start.5
  5.2 0.0 copy-start.3
  5.3 0.0 copy-start.4
  5.3 15.1 %all-to-all-start = ((bf16[128,9,2,128]{3,2,1,0:T(2,128)(2,1)}), bf16[128,9,2,128]{3,2,1,0:T(2,128)(2,1)S(1)}, u32[]{:S(2)}, u32[]{:S(2)}) async-start(bf16[128,9,2,128]{3,2,1,0:T(2,128)(2,1)} %bitcast.26), calls=%async_computation | async-start | bytes 1179648 | tf_op jit(solution)/shard_map/all_to_all | solution.py:291
  20.4 0.0 copy-done.5
  20.4 0.1 copy.10.axes_ref
  20.5 0.0 collective-permute-done.other_ref
  20.5 0.0 copy-done.3
  20.5 0.0 copy-done.4
  20.5 0.5 cotangent.1.ga_ref
  21.0 21.6 %all-to-all-done = bf16[128,9,2,128]{3,2,1,0:T(2,128)(2,1)S(1)} async-done(((bf16[128,9,2,128]{3,2,1,0:T(2,128)(2,1)}), bf16[128,9,2,128]{3,2,1,0:T(2,128)(2,1)S(1)}, u32[]{:S(2)}, u32[]{:S(2)}) %all-to-all-start) | async-done | bytes 589856 | tf_op jit(solution)/shard_map/all_to_all | solution.py:291
  42.6 0.0 copy-done
  42.6 3.6 %forward.1 = (bf16[1792,128]{1,0:T(8,128)(2,1)S(1)}, bf16[6,128,256]{2,1,0:T(8,128)(2,1)S(1)}, bf16[6,128,256]{2,1,0:T(8,128)(2,1)S(1)}, bf16[6,128,256]{2,1,0:T...) custom-call(s32[3,2]{1,0:T(4,128)S(1)} %copy.10.axes_ref, ...), custom_call_target="tpu_custom_call" | custom-call | tf_op jit(solution)/shard_map/forward/pallas_call | solution.py:324
  46.2 25.5 %all_to_all.15 = bf16[128,7,2,128]{3,2,1,0:T(2,128)(2,1)S(1)} all-to-all(bf16[128,7,2,128]{3,2,1,0:T(2,128)(2,1)S(1)} %bitcast.23), channel_id=1, replica_groups=mesh['band'=128,'head'=2] {'band'}, dimensions={0} | all-to-all | bytes 917504 | tf_op jit(solution)/shard_map/all_to_all | solution.py:291
  71.7 1.4 %merge.1 = (bf16[3,128,256]{2,1,0:T(8,128)(2,1)S(1)}, f32[24,128]{1,0:T(8,128)S(1)}, f32[24,128]{1,0:T(8,128)S(1)}, bf16[192,1024]{1,0:T(8,128)(2,1)S(1)}, f32[192,1024]{1,0:T(8,128)S(1)}) custom-call(bf16[3,128,256]{2,1,0:T(8,128)(2,1)S(1)} %cotangent.1.ga_ref, f32[3,128,256]{2,1,0:T(8,128)S(1)} %get-tuple-element.23.near_ref, ...), custom_call_target="tpu_custom_call" | custom-call | tf_op jit(solution)/shard_map/merge/pallas_call | solution.py:344
  73.1 0.3 collective-permute-start.1
  73.4 6.6 %backward.1 = (f32[3,128,256]{2,1,0:T(8,128)S(1)}, f32[3,128,256]{2,1,0:T(8,128)S(1)}, f32[3,128,256]{2,1,0:T(8,128)S(1)}, bf16[2304,128]{1,0:T(8,128)(2,1)}) custom-call(s32[3,2]{1,0:T(4,128)S(1)} %copy.10.axes_ref, bf16[6,128,256]{2,1,0:T(8,128)(2,1)S(1)} %get-tuple-element.29.q6, bf16[6,128,256]{2,1,0:T(8,128)(2,1)S(1)} %get-tuple-element.30.k6, ...), custom_call_target="tpu_custom_call" | custom-call | tf_op jit(solution)/shard_map/backward/pallas_call | solution.py:360
  79.9 7.9 %all-to-all-start.2 = ((bf16[128,9,2,128]{3,2,1,0:T(2,128)(2,1)}), bf16[128,9,2,128]{3,2,1,0:T(2,128)(2,1)S(1)}, u32[]{:S(2)}, u32[]{:S(2)}) async-start(bf16[128,9,2,128]{3,2,1,0:T(2,128)(2,1)} %bitcast.9), calls=%async_computation.2 | async-start | bytes 1179648 | tf_op jit(solution)/shard_map/all_to_all | solution.py:291
  87.8 0.0 collective-permute-done.1.got_ref
  87.8 0.8 layer.1
  88.6 21.2 %all-to-all-done.2 = bf16[128,9,2,128]{3,2,1,0:T(2,128)(2,1)S(1)} async-done(((bf16[128,9,2,128]{3,2,1,0:T(2,128)(2,1)}), bf16[128,9,2,128]{3,2,1,0:T(2,128)(2,1)S(1)}, u32[]{:S(2)}, u32[]{:S(2)}) %all-to-all-start.2) | async-done | bytes 589856 | tf_op jit(solution)/shard_map/all_to_all | solution.py:291
  109.8 0.9 finish.1
  (5 shorter events, 0.0 us)
Async XLA Ops:
  0.6 19.9 %collective-permute-start = (bf16[192,1024]{1,0:T(8,128)(2,1)}, bf16[192,1024]{1,0:T(8,128)(2,1)S(1)}, u32[]{:S(2)}, u32[]{:S(2)}) collective-permute-start(bf16[192,1024]{1,0:T(8,128)(2,1)} %bitcast.24), channel_id=1, source_target_pairs={{0,1},{1,0},{2,3},{3,2},{4,5},{5,4},{6,7},{7,6},{8,9},{9,8},{10,11... | collective-permute-start | bytes 1179656 | tf_op jit(solution)/shard_map/ppermute | solution.py:303
  5.2 15.1 %copy-start.5 = (s32[3,2]{0,1:T(2,128)S(1)}, s32[3,2]{0,1:T(2,128)}, u32[]{:S(2)}) copy-start(s32[3,2]{0,1:T(2,128)} %param.11) | copy-start | bytes 76
  5.2 15.2 %copy-start.3 = (bf16[256,1024]{1,0:T(8,128)(2,1)S(1)}, bf16[256,1024]{1,0:T(8,128)(2,1)}, u32[]{:S(2)}) copy-start(bf16[256,1024]{1,0:T(8,128)(2,1)} %proj_ref.3) | copy-start | bytes 1572868
  5.3 15.2 %copy-start.4 = (bf16[1,3,64,1024]{3,2,1,0:T(8,128)(2,1)S(1)}, bf16[1,3,64,1024]{3,2,1,0:T(8,128)(2,1)}, u32[]{:S(2)}) copy-start(bf16[1,3,64,1024]{3,2,1,0:T(8,128)(2,1)} %param.10) | copy-start | bytes 1179652
  5.3 37.3 %all-to-all-start = ((bf16[128,9,2,128]{3,2,1,0:T(2,128)(2,1)}), bf16[128,9,2,128]{3,2,1,0:T(2,128)(2,1)S(1)}, u32[]{:S(2)}, u32[]{:S(2)}) async-start(bf16[128,9,2,128]{3,2,1,0:T(2,128)(2,1)} %bitcast.26), calls=%async_computation | async-start | bytes 1179648 | tf_op jit(solution)/shard_map/all_to_all | solution.py:291
  20.5 22.1 %copy-start = (bf16[1,3,128,256]{3,2,1,0:T(8,128)(2,1)S(1)}, bf16[1,3,128,256]{3,2,1,0:T(8,128)(2,1)}, u32[]{:S(2)}) copy-start(bf16[1,3,128,256]{3,2,1,0:T(8,128)(2,1)} %param.6) | copy-start | bytes 589828
  20.5 22.1 %copy-start.1 = (bf16[1,3,128,256]{3,2,1,0:T(8,128)(2,1)S(1)}, bf16[1,3,128,256]{3,2,1,0:T(8,128)(2,1)}, u32[]{:S(2)}) copy-start(bf16[1,3,128,256]{3,2,1,0:T(8,128)(2,1)} %param.7) | copy-start | bytes 589828
  20.5 22.1 %copy-start.2 = (bf16[1,3,128,256]{3,2,1,0:T(8,128)(2,1)S(1)}, bf16[1,3,128,256]{3,2,1,0:T(8,128)(2,1)}, u32[]{:S(2)}) copy-start(bf16[1,3,128,256]{3,2,1,0:T(8,128)(2,1)} %param.8) | copy-start | bytes 589828
  73.1 14.7 %collective-permute-start.1 = (bf16[192,1024]{1,0:T(8,128)(2,1)S(1)}, bf16[192,1024]{1,0:T(8,128)(2,1)S(1)}, u32[]{:S(2)}, u32[]{:S(2)}) collective-permute-start(bf16[192,1024]{1,0:T(8,128)(2,1)S(1)} %get-tuple-element.28), channel_id=1, source_target_pairs={{0,1},{1,0},{2,3},{3,2},{4,5},{5,4},{6,7},{7,6},{8,9},{9,8},{10,11... | collective-permute-start | bytes 1179656 | tf_op jit(solution)/shard_map/ppermute | solution.py:359
  79.9 29.9 %all-to-all-start.2 = ((bf16[128,9,2,128]{3,2,1,0:T(2,128)(2,1)}), bf16[128,9,2,128]{3,2,1,0:T(2,128)(2,1)S(1)}, u32[]{:S(2)}, u32[]{:S(2)}) async-start(bf16[128,9,2,128]{3,2,1,0:T(2,128)(2,1)} %bitcast.9), calls=%async_computation.2 | async-start | bytes 1179648 | tf_op jit(solution)/shard_map/all_to_all | solution.py:291

commit v3 on v2

v3 whole, which is shorter than its diff:
```python
import jax
import jax.numpy as jnp
from jax import lax
from jax.experimental import pallas as pl
from jax.experimental.pallas import tpu as pltpu
from jax.sharding import PartitionSpec as P

BF = jnp.bfloat16
F32 = jnp.float32
N = 128
HALF = 64
SENT = 18
MIXED = 14
UNROLL = True
FACTOR = 0.125
LONG = 60 * 10**9
PARAMS = pltpu.CompilerParams(vmem_limit_bytes=48 * 1024 * 1024)
ROOMY = pltpu.CompilerParams(vmem_limit_bytes=60 * 1024 * 1024)
VMEM = pl.BlockSpec(memory_space=pltpu.VMEM)
SMEM = pl.BlockSpec(memory_space=pltpu.SMEM)


def nt(a, b):
    return lax.dot_general(a, b, (((1,), (1,)), ((), ())), preferred_element_type=F32)


def tn(a, b):
    return lax.dot_general(a, b, (((0,), (0,)), ((), ())), preferred_element_type=F32)


def nn(a, b):
    return lax.dot_general(a, b, (((1,), (0,)), ((), ())), preferred_element_type=F32)


def lane_masks():
    lane = lax.broadcasted_iota(jnp.int32, (N, N), 1)
    first = jnp.where(lane < HALF, 1.0, 0.0)
    return first.astype(BF), (1.0 - first).astype(BF)


def stack(x, masks):
    return jnp.concatenate([x * masks[0], x * masks[1]], axis=0)


def head_sums(product):
    row = lax.broadcasted_iota(jnp.int32, (8, 256), 0)
    lane = lax.broadcasted_iota(jnp.int32, (8, 256), 1)
    pick = jnp.where(lane // HALF == row, 1.0, 0.0).astype(BF)
    high = product.astype(BF)
    low = (product - high.astype(F32)).astype(BF)
    return nt(pick, high) + nt(pick, low)


def partner_of(axes_ref, b):
    axis = axes_ref[lax.rem(b, 3), lax.div(b, 3)]
    found = jnp.int32(0)
    for c in range(6):
        same = jnp.logical_and(axes_ref[c % 3, c // 3] == axis, b != c)
        found = found + jnp.where(same, jnp.int32(c), jnp.int32(0))
    return found


def planes(step):
    lax.fori_loop(0, 3, lambda p, _: (step(p), 0)[1], 0, unroll=UNROLL)


def tall(x):
    return jnp.concatenate([x[:, :N], x[:, N:]], axis=0)


def wide(rows, r):
    return jnp.concatenate([rows[r : r + 1], rows[r + 1 : r + 2]], axis=1)


def spread(columns, r):
    lane = lax.broadcasted_iota(jnp.int32, (N, N), 1)
    return jnp.where(lane < HALF, columns[:, r : r + 1], columns[:, r + 1 : r + 2])


def pack_lines_kernel(q_ref, k_ref, v_ref, out_ref, held, stage, sems):
    copies = [
        pltpu.make_async_copy(ref, held.at[a], sems.at[a])
        for a, ref in enumerate((q_ref, k_ref, v_ref))
    ]
    for copy in copies:
        copy.start()
    for a, copy in enumerate(copies):
        copy.wait()
        for p in range(3):
            for g in range(2):
                rows = pl.ds(2 * (3 * a + p) + g, N, stride=SENT)
                stage[rows, :] = held[a, p, :, N * g : N * g + N].astype(F32)
    out_ref[...] = stage[...].astype(BF)


def own_kernel(
    own_ref, other_ref, proj_ref, q_ref, k_ref, v_ref,
    ga_ref, top_ref, sum_ref, out_ref,
):
    me = lax.axis_index("head")
    for ref, side in ((own_ref, me), (other_ref, 1 - me)):
        made = nt(ref[...], proj_ref[...]).astype(BF)
        for p in range(3):
            ga_ref[p, pl.ds(pl.multiple_of(side * HALF, HALF), HALF), :] = made[
                HALF * p : HALF * p + HALF
            ]
    masks = lane_masks()

    def step(p):
        for g in range(2):
            lanes = slice(N * g, N * g + N)
            scores = nt(k_ref[p, :, lanes], stack(q_ref[p, :, lanes] * BF(FACTOR), masks))
            top = jnp.max(scores, axis=0, keepdims=True)
            raised = jnp.exp(scores - top)
            top_ref[p, g] = top
            sum_ref[p, g] = jnp.sum(raised, axis=0, keepdims=True)
            out_ref[p, :, lanes] = tn(tall(raised.astype(BF)), stack(v_ref[p, :, lanes], masks))

    planes(step)


def forward_kernel(
    axes_ref, q_ref, k_ref, v_ref, ga_ref, top_ref, sum_ref, own_ref, got_ref,
    send_ref, q6, k6, v6, near_ref, far_ref, totals_ref,
    stage, parts, rows,
):
    masks = lane_masks()
    stage[...] = got_ref[...].astype(F32)
    for a, (mine, six) in enumerate(((q_ref, q6), (k_ref, k6), (v_ref, v6))):
        for p in range(3):
            six[p] = mine[p]
            for g in range(2):
                lines = pl.ds(2 * (3 * a + p) + g, N, stride=SENT)
                six[3 + p, :, N * g : N * g + N] = stage[lines, :].astype(BF)

    def step(p):
        for b in (p, p + 3):
            partner = partner_of(axes_ref, b)
            for g in range(2):
                lanes = slice(N * g, N * g + N)
                queries = stack(q6[b, :, lanes] * BF(FACTOR), masks)
                scores = nt(k6[partner, :, lanes], queries)
                top = jnp.max(scores, axis=0, keepdims=True)
                if b is p:
                    top = jnp.maximum(top, top_ref[p, g])
                    before = jnp.exp(top_ref[p, g] - top)
                raised = jnp.exp(scores - top)
                total = jnp.sum(raised, axis=0, keepdims=True)
                if b is p:
                    total = total + sum_ref[p, g] * before
                scale = 1.0 / total
                out = tn(tall((raised * scale).astype(BF)), stack(v6[partner, :, lanes], masks))
                total = top + jnp.log(total)
                if b is p:
                    rows[0, p, g] = total
                    rows[1, p, g] = before * scale
                    near_ref[p, :, lanes] = out
                else:
                    rows[2, p, g] = total
                    far_ref[p, :, lanes] = out.astype(BF)

    planes(step)
    totals_ref[...] = jnp.zeros((40, N), F32)
    parts[...] = jnp.zeros((N, N), F32)
    for p in range(3):
        for g in range(2):
            for h in range(2):
                r = 4 * p + 2 * g + h
                half = slice(N * h, N * h + N)
                totals_ref[r : r + 1, :] = rows[0, p, g, :, half]
                totals_ref[24 + r : 25 + r, :] = rows[2, p, g, :, half]
                parts[r : r + 1, :] = rows[1, p, g, :, half]
    weights = jnp.transpose(parts[...])
    for p in range(3):
        for g in range(2):
            lanes = slice(N * g, N * g + N)
            near_ref[p, :, lanes] += spread(weights, 4 * p + 2 * g) * own_ref[p, :, lanes]
        totals_ref[12 + 4 * p : 16 + 4 * p, :] = head_sums(
            ga_ref[p].astype(F32) * near_ref[p]
        )[:4]
    left = totals_ref[...]
    for piece in range(3):
        rounded = left.astype(BF).astype(F32)
        parts[40 * piece : 40 * piece + 40, :] = rounded
        left = left - rounded
    stage[pl.ds(12, N, stride=MIXED), :] = jnp.transpose(parts[...])
    stage[pl.ds(13, N, stride=MIXED), :] = jnp.zeros((N, N), F32)
    for p in range(3):
        for g in range(2):
            lanes = slice(N * g, N * g + N)
            stage[pl.ds(2 * p + g, N, stride=MIXED), :] = far_ref[p, :, lanes].astype(F32)
            stage[pl.ds(6 + 2 * p + g, N, stride=MIXED), :] = ga_ref[p, :, lanes].astype(F32)
    send_ref[...] = stage[: MIXED * N, :].astype(BF)


def ready_kernel(axes_ref, q6, k6, v6, ga_ref, totals_ref, own_ref, near_ref, far_ref, own_dot, near_dot, rows):
    masks = lane_masks()
    for p in range(3):
        for g in range(2):
            r = 4 * p + 2 * g
            rows[0, p, g] = wide(totals_ref[0:12, :], r)
            rows[1, p, g] = wide(totals_ref[24:36, :], r)

    def step(p):
        near, far = partner_of(axes_ref, p), partner_of(axes_ref, p + 3)
        for g in range(2):
            lanes = slice(N * g, N * g + N)
            queries = stack(q6[p, :, lanes] * BF(FACTOR), masks)
            grads = stack(ga_ref[p, :, lanes], masks)
            total = rows[0, p, g]
            own_ref[p, g] = jnp.exp(nt(k6[p, :, lanes], queries) - total).astype(BF)
            near_ref[p, g] = jnp.exp(nt(k6[near, :, lanes], queries) - total).astype(BF)
            own_dot[p, g] = nt(v6[p, :, lanes], grads)
            near_dot[p, g] = nt(v6[near, :, lanes], grads)
            queries = stack(q6[p + 3, :, lanes] * BF(FACTOR), masks)
            far_ref[p, g] = jnp.exp(nt(k6[far, :, lanes], queries) - rows[1, p, g]).astype(BF)

    planes(step)


def both_weights(near, far):
    top = jnp.maximum(near, far)
    log_all = top + jnp.log(jnp.exp(near - top) + jnp.exp(far - top))
    return jnp.exp(near - log_all), jnp.exp(far - log_all)


def merge_kernel(
    ga_ref, near_ref, far_ref, totals_ref, proj_ref, got_ref, first_ref,
    ga_col_ref, weight_ref, delta_ref, given_ref, kept_ref,
    stage, parts, att,
):
    stage[...] = got_ref[...].astype(F32)
    parts[...] = jnp.transpose(stage[pl.ds(12, N, stride=MIXED), :])
    arrived = parts[0:40, :] + (parts[40:80, :] + parts[80:120, :])
    for p in range(3):
        for g in range(2):
            ga_col_ref[p, :, N * g : N * g + N] = stage[
                pl.ds(6 + 2 * p + g, N, stride=MIXED), :
            ].astype(BF)
    row_near, row_far = both_weights(totals_ref[0:12, :], arrived[24:36])
    col_near, col_far = both_weights(arrived[0:12], totals_ref[24:36, :])
    row_delta = row_near * totals_ref[12:24, :]
    col_delta = col_near * arrived[12:24]
    for p in range(3):
        far_row = jnp.concatenate(
            [stage[pl.ds(2 * p + g, N, stride=MIXED), :] for g in range(2)], axis=1
        )
        heads = slice(4 * p, 4 * p + 4)
        row_sums = head_sums(ga_ref[p].astype(F32) * far_row)[:4]
        col_sums = head_sums(ga_col_ref[p].astype(F32) * far_ref[p].astype(F32))[:4]
        row = row_delta[heads] + row_far[heads] * row_sums
        col = col_delta[heads] + col_far[heads] * col_sums
        for g in range(2):
            weight_ref[p, g] = wide(row_near, 4 * p + 2 * g)
            weight_ref[3 + p, g] = wide(col_far, 4 * p + 2 * g)
            delta_ref[p, g] = wide(row, 2 * g)
            delta_ref[3 + p, g] = wide(col, 2 * g)
    parts[0:12, :] = row_near
    parts[12:24, :] = row_far
    weights = jnp.transpose(parts[...])
    for p in range(3):
        for g in range(2):
            r = 4 * p + 2 * g
            att[p, :, N * g : N * g + N] = (
                spread(weights, r) * near_ref[p, :, N * g : N * g + N]
                + spread(weights, 12 + r) * stage[pl.ds(2 * p + g, N, stride=MIXED), :]
            ).astype(BF)
    me = lax.axis_index("head")
    for side, out in ((1 - me, given_ref), (me, kept_ref)):
        tokens = pl.ds(pl.multiple_of(side * HALF, HALF), HALF)
        for p in range(3):
            out[HALF * p : HALF * p + HALF, :] = nn(att[p, tokens, :], proj_ref[...]).astype(out.dtype)


def layer_kernel(kept_ref, got_ref, out_ref):
    out_ref[...] = (kept_ref[...] + got_ref[...].astype(F32)).astype(BF)


def backward_kernel(
    axes_ref, q6, k6, v6, ga_ref, ga_col_ref, own_p, near_p, far_p, own_dot, near_dot, weight_ref, delta_ref,
    dq_ref, dk_ref, dv_ref, send_ref,
    stage, dq_col, dk6, dv6,
):
    masks = lane_masks()

    def pair_step(b, c, g, prob, dots, queries, grads):
        lanes = slice(N * g, N * g + N)
        prob = prob.astype(F32) * weight_ref[b, g]
        step = (prob * (dots - delta_ref[b, g])).astype(BF)
        dq = tn(tall(step), stack(k6[c, :, lanes], masks))
        return dq, nn(step, queries), nn(prob.astype(BF), grads)

    def first(p):
        for g in range(2):
            lanes = slice(N * g, N * g + N)
            queries = stack(q6[p, :, lanes] * BF(FACTOR), masks)
            grads = stack(ga_ref[p, :, lanes], masks)
            dq_ref[p, :, lanes], dk6[p, :, lanes], dv6[p, :, lanes] = pair_step(
                p, p, g, own_p[p, g], own_dot[p, g], queries, grads
            )
            dk6[p + 3, :, lanes] = jnp.zeros((N, N), F32)
            dv6[p + 3, :, lanes] = jnp.zeros((N, N), F32)

    def second(p):
        near, far = partner_of(axes_ref, p), partner_of(axes_ref, p + 3)
        for g in range(2):
            lanes = slice(N * g, N * g + N)
            queries = stack(q6[p, :, lanes] * BF(FACTOR), masks)
            grads = stack(ga_ref[p, :, lanes], masks)
            dq, dk, dv = pair_step(p, near, g, near_p[p, g], near_dot[p, g], queries, grads)
            dq_ref[p, :, lanes] = (dq_ref[p, :, lanes] + dq) * FACTOR
            dk6[near, :, lanes] += dk
            dv6[near, :, lanes] += dv
            queries = stack(q6[p + 3, :, lanes] * BF(FACTOR), masks)
            grads = stack(ga_col_ref[p, :, lanes], masks)
            dots = nt(v6[far, :, lanes], grads)
            dq, dk, dv = pair_step(p + 3, far, g, far_p[p, g], dots, queries, grads)
            dq_col[p, :, lanes] = dq * FACTOR
            dk6[far, :, lanes] += dk
            dv6[far, :, lanes] += dv

    planes(first)
    planes(second)
    for p in range(3):
        dk_ref[p] = dk6[p]
        dv_ref[p] = dv6[p]
        for g in range(2):
            lanes = slice(N * g, N * g + N)
            stage[pl.ds(2 * p + g, N, stride=SENT), :] = dq_col[p, :, lanes]
            stage[pl.ds(6 + 2 * p + g, N, stride=SENT), :] = dk6[3 + p, :, lanes]
            stage[pl.ds(12 + 2 * p + g, N, stride=SENT), :] = dv6[3 + p, :, lanes]
    send_ref[...] = stage[...].astype(BF)


def finish_kernel(dq_ref, dk_ref, dv_ref, got_ref, q_out, k_out, v_out, stage):
    stage[...] = got_ref[...].astype(F32)
    for a, (mine, out) in enumerate(((dq_ref, q_out), (dk_ref, k_out), (dv_ref, v_out))):
        for p in range(3):
            for g in range(2):
                lanes = slice(N * g, N * g + N)
                rows = pl.ds(2 * (3 * a + p) + g, N, stride=SENT)
                out[p, :, lanes] = (mine[p, :, lanes] + stage[rows, :]).astype(BF)


def shape(*dims, dtype=BF):
    return jax.ShapeDtypeStruct(dims, dtype)


def cost(flops, moved):
    return pl.CostEstimate(flops=flops, bytes_accessed=moved, transcendentals=0)


def exchange(sent, rows):
    sent = sent.reshape(N, rows // 2, 2, N)
    got = lax.all_to_all(sent, "band", split_axis=0, concat_axis=0, tiled=True)
    return got.reshape(N * rows, N)


LINE = (3, N, 256)
TOKENS = (3 * HALF, 1024)
PAIR = (3, 2, N, 256)
ROW = (3, 2, 1, 256)
STAGE = pltpu.VMEM((SENT * N, N), F32)
SQUARE = pltpu.VMEM((N, N), F32)


def call(kernel, ins, outs, scratch, name, params=PARAMS, estimate=None):
    many = len(outs) > 1
    return pl.pallas_call(
        kernel,
        out_shape=tuple(outs) if many else outs[0],
        in_specs=[SMEM if x.dtype == jnp.int32 else VMEM for x in ins],
        out_specs=(VMEM,) * len(outs) if many else VMEM,
        scratch_shapes=scratch,
        compiler_params=params,
        cost_estimate=estimate,
        name=name,
    )(*ins)


def own(*ins):
    outs = [shape(*LINE), shape(*ROW, dtype=F32), shape(*ROW, dtype=F32), shape(*LINE, dtype=F32)]
    return call(own_kernel, ins, outs, [], "own", estimate=cost(LONG, 3000000))


def forward(*ins):
    outs = [shape(MIXED * N, N)] + [shape(6, N, 256)] * 3
    outs += [shape(*LINE, dtype=F32), shape(*LINE), shape(40, N, dtype=F32)]
    return call(forward_kernel, ins, outs, [STAGE, SQUARE, pltpu.VMEM((3, *ROW), F32)], "forward")


def ready(*ins):
    outs = [shape(*PAIR)] * 3 + [shape(*PAIR, dtype=F32)] * 2
    return call(ready_kernel, ins, outs, [pltpu.VMEM((2, *ROW), F32)], "ready", estimate=cost(10**9, 3000000))


def merge(*ins):
    rows = shape(6, 2, 1, 256, dtype=F32)
    outs = [shape(*LINE), rows, rows, shape(*TOKENS), shape(*TOKENS, dtype=F32)]
    scratch = [pltpu.VMEM((MIXED * N, N), F32), SQUARE, pltpu.VMEM(LINE, BF)]
    return call(merge_kernel, ins, outs, scratch, "merge")


def backward(*ins):
    outs = [shape(*LINE, dtype=F32)] * 3 + [shape(SENT * N, N)]
    scratch = [STAGE, pltpu.VMEM(LINE, F32)] + [pltpu.VMEM((6, N, 256), F32)] * 2
    return call(backward_kernel, ins, outs, scratch, "backward")


def finish(*ins):
    return call(finish_kernel, ins, [shape(*LINE)] * 3, [STAGE], "finish")


def pack_lines(*ins):
    return pl.pallas_call(
        pack_lines_kernel,
        out_shape=shape(SENT * N, N),
        in_specs=[pl.BlockSpec(memory_space=pltpu.HBM)] * 3,
        out_specs=VMEM,
        scratch_shapes=[pltpu.VMEM((3, *LINE), BF), STAGE, pltpu.SemaphoreType.DMA((3,))],
        compiler_params=ROOMY,
        name="pack_lines",
    )(*ins)


def body(queries, attn_keys, attn_values, out_proj, grad_out, plane_axes):
    swap = [(0, 1), (1, 0)]
    q, k, v = queries[0], attn_keys[0], attn_values[0]

    cotangent = grad_out.reshape(TOKENS)
    other = lax.ppermute(cotangent, "head", swap)
    lines = exchange(pack_lines(q, k, v), SENT)
    ga, top, total, own_out = own(cotangent, other, out_proj, q, k, v)

    sent, q6, k6, v6, near_out, far_out, totals = forward(
        plane_axes, q, k, v, ga, top, total, own_out, lines
    )
    mixed = exchange(sent, MIXED)
    own_p, near_p, far_p, own_dot, near_dot = ready(plane_axes, q6, k6, v6, ga, totals)

    ga_columns, weight, delta, given, kept = merge(
        ga, near_out, far_out, totals, out_proj, mixed, own_p
    )
    arrived = lax.ppermute(given, "head", swap)
    dq, dk, dv, sent = backward(
        plane_axes, q6, k6, v6, ga, ga_columns, own_p, near_p, far_p, own_dot, near_dot, weight, delta
    )
    returned = exchange(sent, SENT)
    layer = call(
        layer_kernel, (kept, arrived), [shape(*TOKENS)], [], "layer", estimate=cost(LONG, 1500000)
    )
    dq, dk, dv = finish(dq, dk, dv, returned)
    return layer.reshape(1, 3, HALF, 1024), dq[None], dk[None], dv[None]


def solution(mesh):
    lines = P("band", None, None, "head")
    columns = P("band", None, "head", None)
    return jax.shard_map(
        body,
        mesh=mesh,
        in_specs=(lines, lines, lines, P("head", None), columns, P()),
        out_specs=(columns, lines, lines, lines),
        check_vma=False,
    )
```

time: 111 us -> 114 us (1.027)
  blocking collectives: 25.5 us -> 0 us
  waiting for transfers between devices: 42.8 us -> 55.1 us
  local copies, waits for them, and re-layouts: 0.12 us -> 9.38 us
  starting transfers between devices: 25.8 us -> 32 us
    all_to_all x1 -> x0, blocking collectives: 25.5 us -> none  [exchange(): got = lax.all_to_all(sent, 'band', split_axis=0, concat_axis=0, tiled=True)]
    all_to_all x2 -> x3, waiting for transfers between devices: 42.8 us -> 55.1 us  [exchange(): got = lax.all_to_all(sent, 'band', split_axis=0, concat_axis=0, tiled=True)]
    unnamed x13 -> x51, local copies, waits for them, and re-layouts: 0.12 us -> 9.38 us
    all_to_all x2 -> x3, starting transfers between devices: 23 us -> 28.3 us  [exchange(): got = lax.all_to_all(sent, 'band', split_axis=0, concat_axis=0, tiled=True)]
    pallas_call x7 -> x8, Pallas kernels: 15.9 us -> 16.1 us  [the longest x7 14 us: call(): pl.pallas_call(kernel, out_shape=tuple(outs) if many else outs[0], in_spe...]
  transfers between devices with their start and end apart: 4 -> 5, of which waited for: 2 -> 3; matrix products, arithmetic and copies ran while one was open for 0% -> 0% of each run, Pallas kernels for 9% -> 9%
where the time goes in v3:
time: 114 us; the launch traced here: 113 us
  waiting for transfers between devices  55.1 us (48%)
  starting transfers between devices  32 us (28%)
  Pallas kernels  16.1 us (14%)
  local copies, waits for them, and re-layouts  9.38 us (8%)
    all_to_all x3, waiting for transfers between devices, exchange(): got = lax.all_to_all(sent, 'band', split_axis=0, concat_axis=0, tiled=True)  55.1 us
    all_to_all x3, starting transfers between devices, exchange(): got = lax.all_to_all(sent, 'band', split_axis=0, concat_axis=0, tiled=True)  28.3 us
    pallas_call x7, Pallas kernels, call(): pl.pallas_call(kernel, out_shape=tuple(outs) if many else outs[0], in_spe...  14 us
    unnamed x51, local copies, waits for them, and re-layouts  9.38 us
    ppermute x1, starting transfers between devices, body(): other = lax.ppermute(cotangent, 'head', swap)  2.55 us
  transfers between devices with their start and end apart: 5, of which 3 were waited for; matrix products, arithmetic and copies ran while one was open for 0% of the time, Pallas kernels for 9%

profile of v3, /device:TPU:1, one launch (start us, length us, event | category | flops | bytes accessed | tf_op | source)
XLA Modules:
  0.0 113.4 jit_solution(4221740295381275341)
XLA Ops:
  0.6 2.6 %collective-permute-start = (bf16[192,1024]{1,0:T(8,128)(2,1)}, bf16[192,1024]{1,0:T(8,128)(2,1)S(1)}, u32[]{:S(2)}, u32[]{:S(2)}) collective-permute-start(bf16[192,1024]{1,0:T(8,128)(2,1)} %bitcast.26), channel_id=1, source_target_pairs={{0,1},{1,0},{2,3},{3,2},{4,5},{5,4},{6,7},{7,6},{8,9},{9,8},{10,11... | collective-permute-start | bytes 1179656 | tf_op jit(solution)/shard_map/ppermute | solution.py:431
  3.2 2.1 %pack_lines.1 = bf16[2304,128]{1,0:T(8,128)(2,1)} custom-call(bf16[3,128,256]{2,1,0:T(8,128)(2,1)} %bitcast.17, bf16[3,128,256]{2,1,0:T(8,128)(2,1)} %bitcast.20, bf16[3,128,256]{2,1,0:T(8,128)(2,1)} %bitcast.23), custom_call_target="tpu_custom_call" | custom-call | tf_op jit(solution)/shard_map/pack_lines/pallas_call | solution.py:415
  5.3 15.1 %all-to-all-start = ((bf16[128,9,2,128]{3,2,1,0:T(2,128)(2,1)}), bf16[128,9,2,128]{3,2,1,0:T(2,128)(2,1)S(1)}, u32[]{:S(2)}, u32[]{:S(2)}) async-start(bf16[128,9,2,128]{3,2,1,0:T(2,128)(2,1)} %bitcast.28), calls=%async_computation | async-start | bytes 1179648 | tf_op jit(solution)/shard_map/all_to_all | solution.py:355
  20.6 0.9 own.1
  21.5 21.1 %all-to-all-done = bf16[128,9,2,128]{3,2,1,0:T(2,128)(2,1)S(1)} async-done(((bf16[128,9,2,128]{3,2,1,0:T(2,128)(2,1)}), bf16[128,9,2,128]{3,2,1,0:T(2,128)(2,1)S(1)}, u32[]{:S(2)}, u32[]{:S(2)}) %all-to-all-start) | async-done | bytes 589856 | tf_op jit(solution)/shard_map/all_to_all | solution.py:355
  42.6 3.1 %forward.1 = (bf16[1792,128]{1,0:T(8,128)(2,1)}, bf16[6,128,256]{2,1,0:T(8,128)(2,1)S(1)}, bf16[6,128,256]{2,1,0:T(8,128)(2,1)S(1)}, bf16[6,128,256]{2,1,0:T(8,1...) custom-call(s32[3,2]{1,0:T(4,128)S(1)} %copy.10.axes_ref, ...), custom_call_target="tpu_custom_call" | custom-call | tf_op jit(solution)/shard_map/forward/pallas_call | solution.py:369
  46.5 0.7 copy-done.8
  47.2 0.7 copy-done.11
  48.7 6.5 %all-to-all-start.1 = ((bf16[128,7,2,128]{3,2,1,0:T(2,128)(2,1)}), bf16[128,7,2,128]{3,2,1,0:T(2,128)(2,1)S(1)}, u32[]{:S(2)}, u32[]{:S(2)}) async-start(bf16[128,7,2,128]{3,2,1,0:T(2,128)(2,1)} %bitcast.6), calls=%async_computation.1 | async-start | bytes 917504 | tf_op jit(solution)/shard_map/all_to_all | solution.py:355
  55.3 1.0 copy-done.9
  56.3 1.0 copy-done.12
  57.3 1.0 copy-done.15
  58.3 1.3 %ready.1 = (bf16[3,2,128,256]{3,2,1,0:T(8,128)(2,1)S(1)}, bf16[3,2,128,256]{3,2,1,0:T(8,128)(2,1)S(1)}, bf16[3,2,128,256]{3,2,1,0:T(8,128)(2,1)S(1)}, f32[3,2,12...) custom-call(s32[3,2]{1,0:T(4,128)S(1)} %copy.10.axes_ref, bf16[6,128,256]{2,1,0:T(8,128)(2,1)S(1)} %copy-done.9, ...), custom_call_target="tpu_custom_call" | custom-call | flops 1000000000 | bytes 3000000 | tf_op jit(solution)/shard_map/ready/pallas_call | solution.py:369
  59.5 0.8 copy-done.17
  60.3 0.7 copy-done.19
  61.0 13.7 %all-to-all-done.1 = bf16[128,7,2,128]{3,2,1,0:T(2,128)(2,1)S(1)} async-done(((bf16[128,7,2,128]{3,2,1,0:T(2,128)(2,1)}), bf16[128,7,2,128]{3,2,1,0:T(2,128)(2,1)S(1)}, u32[]{:S(2)}, u32[]{:S(2)}) %all-to-all-start.1) | async-done | bytes 458784 | tf_op jit(solution)/shard_map/all_to_all | solution.py:355
  74.7 1.0 copy-done.7
  75.8 1.9 %merge.1 = (bf16[3,128,256]{2,1,0:T(8,128)(2,1)S(1)}, f32[6,2,1,256]{3,2,1,0:T(1,128)S(1)}, f32[6,2,1,256]{3,2,1,0:T(1,128)S(1)}, bf16[192,1024]{1,0:T(8,128)(2,1)}, f32[192,1024]{1,0:T(8,128)S(1)}) custom-call(bf16[3,128,256]{2,1,0:T(8,128)(2,1)S(1)} %get-tuple-element.32.ga_ref, f32[3,128,256]{2,1,0:T(8,128)S(1)} %copy-done.7, ...), custom_call_target="tpu_custom_call" | custom-call | tf_op jit(solution)/shard_map/merge/pallas_call | solution.py:369
  77.7 1.2 %collective-permute-start.1 = (bf16[192,1024]{1,0:T(8,128)(2,1)}, bf16[192,1024]{1,0:T(8,128)(2,1)}, u32[]{:S(2)}, u32[]{:S(2)}) collective-permute-start(bf16[192,1024]{1,0:T(8,128)(2,1)} %get-tuple-element.45), channel_id=1, source_target_pairs={{0,1},{1,0},{2,3},{3,2},{4,5},{5,4},{6,7},{7,6},{8,9},{9,8},{10,11... | collective-permute-start | bytes 1179656 | tf_op jit(solution)/shard_map/ppermute | solution.py:444
  79.0 3.9 %backward.1 = (f32[3,128,256]{2,1,0:T(8,128)S(1)}, f32[3,128,256]{2,1,0:T(8,128)S(1)}, f32[3,128,256]{2,1,0:T(8,128)S(1)}, bf16[2304,128]{1,0:T(8,128)(2,1)}) custom-call(s32[3,2]{1,0:T(4,128)S(1)} %copy.10.axes_ref, bf16[6,128,256]{2,1,0:T(8,128)(2,1)S(1)} %copy-done.10, bf16[6,128,256]{2,1,0:T(8,128)(2,1)S(1)} %copy-done.13, ...), custom_call_target="tpu_custom_call" | custom-call | tf_op jit(solution)/shard_map/backward/pallas_call | solution.py:369
  83.6 6.7 %all-to-all-start.2 = ((bf16[128,9,2,128]{3,2,1,0:T(2,128)(2,1)}), bf16[128,9,2,128]{3,2,1,0:T(2,128)(2,1)S(1)}, u32[]{:S(2)}, u32[]{:S(2)}) async-start(bf16[128,9,2,128]{3,2,1,0:T(2,128)(2,1)} %bitcast.9), calls=%async_computation.2 | async-start | bytes 1179648 | tf_op jit(solution)/shard_map/all_to_all | solution.py:355
  90.3 1.9 %layer.1 = bf16[192,1024]{1,0:T(8,128)(2,1)} custom-call(f32[192,1024]{1,0:T(8,128)S(1)} %copy-done.22, bf16[192,1024]{1,0:T(8,128)(2,1)} %collective-permute-done.1.got_ref), custom_call_target="tpu_custom_call" | custom-call | flops 60000002048 | bytes 1500000 | tf_op jit(solution)/shard_map/layer/pallas_call | solution.py:369
  92.2 20.3 %all-to-all-done.2 = bf16[128,9,2,128]{3,2,1,0:T(2,128)(2,1)S(1)} async-done(((bf16[128,9,2,128]{3,2,1,0:T(2,128)(2,1)}), bf16[128,9,2,128]{3,2,1,0:T(2,128)(2,1)S(1)}, u32[]{:S(2)}, u32[]{:S(2)}) %all-to-all-start.2) | async-done | bytes 589856 | tf_op jit(solution)/shard_map/all_to_all | solution.py:355
  112.5 0.9 finish.1
  (45 shorter events, 2.4 us)
Async XLA Ops:
  0.6 19.9 %collective-permute-start = (bf16[192,1024]{1,0:T(8,128)(2,1)}, bf16[192,1024]{1,0:T(8,128)(2,1)S(1)}, u32[]{:S(2)}, u32[]{:S(2)}) collective-permute-start(bf16[192,1024]{1,0:T(8,128)(2,1)} %bitcast.26), channel_id=1, source_target_pairs={{0,1},{1,0},{2,3},{3,2},{4,5},{5,4},{6,7},{7,6},{8,9},{9,8},{10,11... | collective-permute-start | bytes 1179656 | tf_op jit(solution)/shard_map/ppermute | solution.py:431
  3.2 17.4 %copy-start.23 = (bf16[1,3,64,1024]{3,2,1,0:T(8,128)(2,1)S(1)}, bf16[1,3,64,1024]{3,2,1,0:T(8,128)(2,1)}, u32[]{:S(2)}) copy-start(bf16[1,3,64,1024]{3,2,1,0:T(8,128)(2,1)} %param.10) | copy-start | bytes 1179652
  5.3 15.2 %copy-start.24 = (s32[3,2]{0,1:T(2,128)S(1)}, s32[3,2]{0,1:T(2,128)}, u32[]{:S(2)}) copy-start(s32[3,2]{0,1:T(2,128)} %param.11) | copy-start | bytes 76
  5.3 15.3 %copy-start = (bf16[1,3,128,256]{3,2,1,0:T(8,128)(2,1)S(1)}, bf16[1,3,128,256]{3,2,1,0:T(8,128)(2,1)}, u32[]{:S(2)}) copy-start(bf16[1,3,128,256]{3,2,1,0:T(8,128)(2,1)} %param.6) | copy-start | bytes 589828
  5.3 15.3 %copy-start.1 = (bf16[1,3,128,256]{3,2,1,0:T(8,128)(2,1)S(1)}, bf16[1,3,128,256]{3,2,1,0:T(8,128)(2,1)}, u32[]{:S(2)}) copy-start(bf16[1,3,128,256]{3,2,1,0:T(8,128)(2,1)} %param.7) | copy-start | bytes 589828
  5.3 15.2 %copy-start.2 = (bf16[1,3,128,256]{3,2,1,0:T(8,128)(2,1)S(1)}, bf16[1,3,128,256]{3,2,1,0:T(8,128)(2,1)}, u32[]{:S(2)}) copy-start(bf16[1,3,128,256]{3,2,1,0:T(8,128)(2,1)} %param.8) | copy-start | bytes 589828
  5.3 15.2 %copy-start.3 = (bf16[256,1024]{1,0:T(8,128)(2,1)S(1)}, bf16[256,1024]{1,0:T(8,128)(2,1)}, u32[]{:S(2)}) copy-start(bf16[256,1024]{1,0:T(8,128)(2,1)} %proj_ref.3) | copy-start | bytes 1572868
  5.3 37.3 %all-to-all-start = ((bf16[128,9,2,128]{3,2,1,0:T(2,128)(2,1)}), bf16[128,9,2,128]{3,2,1,0:T(2,128)(2,1)S(1)}, u32[]{:S(2)}, u32[]{:S(2)}) async-start(bf16[128,9,2,128]{3,2,1,0:T(2,128)(2,1)} %bitcast.28), calls=%async_computation | async-start | bytes 1179648 | tf_op jit(solution)/shard_map/all_to_all | solution.py:355
  48.7 26.0 %all-to-all-start.1 = ((bf16[128,7,2,128]{3,2,1,0:T(2,128)(2,1)}), bf16[128,7,2,128]{3,2,1,0:T(2,128)(2,1)S(1)}, u32[]{:S(2)}, u32[]{:S(2)}) async-start(bf16[128,7,2,128]{3,2,1,0:T(2,128)(2,1)} %bitcast.6), calls=%async_computation.1 | async-start | bytes 917504 | tf_op jit(solution)/shard_map/all_to_all | solution.py:355
  55.3 1.0 copy-start.9
  56.3 1.0 copy-start.12
  57.3 1.0 copy-start.15
  59.5 0.8 copy-start.17
  74.7 1.0 copy-start.7
  75.7 3.2 %copy-start.10 = (bf16[6,128,256]{2,1,0:T(8,128)(2,1)S(1)}, bf16[6,128,256]{2,1,0:T(8,128)(2,1)}, u32[]{:S(2)}) copy-start(bf16[6,128,256]{2,1,0:T(8,128)(2,1)} %copy-done.8) | copy-start | bytes 1179652
  75.7 3.2 %copy-start.13 = (bf16[6,128,256]{2,1,0:T(8,128)(2,1)S(1)}, bf16[6,128,256]{2,1,0:T(8,128)(2,1)}, u32[]{:S(2)}) copy-start(bf16[6,128,256]{2,1,0:T(8,128)(2,1)} %copy-done.11) | copy-start | bytes 1179652
  75.7 3.2 %copy-start.16 = (bf16[6,128,256]{2,1,0:T(8,128)(2,1)S(1)}, bf16[6,128,256]{2,1,0:T(8,128)(2,1)}, u32[]{:S(2)}) copy-start(bf16[6,128,256]{2,1,0:T(8,128)(2,1)} %copy-done.14) | copy-start | bytes 1179652
  75.7 3.2 %copy-start.18 = (bf16[3,2,128,256]{3,2,1,0:T(8,128)(2,1)S(1)}, bf16[3,2,128,256]{3,2,1,0:T(8,128)(2,1)}, u32[]{:S(2)}) copy-start(bf16[3,2,128,256]{3,2,1,0:T(8,128)(2,1)} %copy-done.17) | copy-start | bytes 1179652
  75.7 3.2 %copy-start.20 = (bf16[3,2,128,256]{3,2,1,0:T(8,128)(2,1)S(1)}, bf16[3,2,128,256]{3,2,1,0:T(8,128)(2,1)}, u32[]{:S(2)}) copy-start(bf16[3,2,128,256]{3,2,1,0:T(8,128)(2,1)} %copy-done.19) | copy-start | bytes 1179652
  77.7 5.2 %copy-start.21 = (f32[192,1024]{1,0:T(8,128)}, f32[192,1024]{1,0:T(8,128)S(1)}, u32[]{:S(2)}) copy-start(f32[192,1024]{1,0:T(8,128)S(1)} %get-tuple-element.44.kept_ref) | copy-start | bytes 2359300
  77.7 12.6 %collective-permute-start.1 = (bf16[192,1024]{1,0:T(8,128)(2,1)}, bf16[192,1024]{1,0:T(8,128)(2,1)}, u32[]{:S(2)}, u32[]{:S(2)}) collective-permute-start(bf16[192,1024]{1,0:T(8,128)(2,1)} %get-tuple-element.45), channel_id=1, source_target_pairs={{0,1},{1,0},{2,3},{3,2},{4,5},{5,4},{6,7},{7,6},{8,9},{9,8},{10,11... | collective-permute-start | bytes 1179656 | tf_op jit(solution)/shard_map/ppermute | solution.py:444
  83.6 6.7 %copy-start.22 = (f32[192,1024]{1,0:T(8,128)S(1)}, f32[192,1024]{1,0:T(8,128)}, u32[]{:S(2)}) copy-start(f32[192,1024]{1,0:T(8,128)} %copy-done.21) | copy-start | bytes 2359300
  83.6 28.9 %all-to-all-start.2 = ((bf16[128,9,2,128]{3,2,1,0:T(2,128)(2,1)}), bf16[128,9,2,128]{3,2,1,0:T(2,128)(2,1)S(1)}, u32[]{:S(2)}, u32[]{:S(2)}) async-start(bf16[128,9,2,128]{3,2,1,0:T(2,128)(2,1)} %bitcast.9), calls=%async_computation.2 | async-start | bytes 1179648 | tf_op jit(solution)/shard_map/all_to_all | solution.py:355
  90.3 22.2 %copy-start.5 = (f32[3,128,256]{2,1,0:T(8,128)S(1)}, f32[3,128,256]{2,1,0:T(8,128)}, u32[]{:S(2)}) copy-start(f32[3,128,256]{2,1,0:T(8,128)} %copy-done.4) | copy-start | bytes 1179652
  (6 other events, 4.5 us)

commit v4 on v3

--- a/solution.py
+++ b/solution.py
@@ -122,7 +122,7 @@
 def forward_kernel(
     axes_ref, q_ref, k_ref, v_ref, ga_ref, top_ref, sum_ref, own_ref, got_ref,
     send_ref, q6, k6, v6, near_ref, far_ref, totals_ref,
-    stage, parts, rows,
+    stage, parts, rows, probs,
 ):
     masks = lane_masks()
     stage[...] = got_ref[...].astype(F32)
@@ -133,33 +133,33 @@
                 lines = pl.ds(2 * (3 * a + p) + g, N, stride=SENT)
                 six[3 + p, :, N * g : N * g + N] = stage[lines, :].astype(BF)
 
-    def step(p):
-        for b in (p, p + 3):
-            partner = partner_of(axes_ref, b)
-            for g in range(2):
-                lanes = slice(N * g, N * g + N)
-                queries = stack(q6[b, :, lanes] * BF(FACTOR), masks)
-                scores = nt(k6[partner, :, lanes], queries)
-                top = jnp.max(scores, axis=0, keepdims=True)
-                if b is p:
-                    top = jnp.maximum(top, top_ref[p, g])
-                    before = jnp.exp(top_ref[p, g] - top)
-                raised = jnp.exp(scores - top)
-                total = jnp.sum(raised, axis=0, keepdims=True)
-                if b is p:
-                    total = total + sum_ref[p, g] * before
-                scale = 1.0 / total
-                out = tn(tall((raised * scale).astype(BF)), stack(v6[partner, :, lanes], masks))
-                total = top + jnp.log(total)
-                if b is p:
-                    rows[0, p, g] = total
-                    rows[1, p, g] = before * scale
-                    near_ref[p, :, lanes] = out
-                else:
-                    rows[2, p, g] = total
-                    far_ref[p, :, lanes] = out.astype(BF)
-
-    planes(step)
+    blocks = [(b, partner_of(axes_ref, b)) for b in range(6)]
+    for g in range(2):
+        lanes = slice(N * g, N * g + N)
+        for b, c in blocks:
+            p = b % 3
+            scores = nt(k6[c, :, lanes], stack(q6[b, :, lanes] * BF(FACTOR), masks))
+            top = jnp.max(scores, axis=0, keepdims=True)
+            if b < 3:
+                top = jnp.maximum(top, top_ref[p, g])
+                before = jnp.exp(top_ref[p, g] - top)
+            raised = jnp.exp(scores - top)
+            total = jnp.sum(raised, axis=0, keepdims=True)
+            if b < 3:
+                total = total + sum_ref[p, g] * before
+            scale = 1.0 / total
+            probs[2 * b + g] = (raised * scale).astype(BF)
+            rows[b // 3, p, g] = top + jnp.log(total)
+            if b < 3:
+                rows[2, p, g] = before * scale
+    for g in range(2):
+        lanes = slice(N * g, N * g + N)
+        for b, c in blocks:
+            out = tn(tall(probs[2 * b + g]), stack(v6[c, :, lanes], masks))
+            if b < 3:
+                near_ref[b, :, lanes] = out
+            else:
+                far_ref[b - 3, :, lanes] = out.astype(BF)
     totals_ref[...] = jnp.zeros((40, N), F32)
     parts[...] = jnp.zeros((N, N), F32)
     for p in range(3):
@@ -168,8 +168,8 @@
                 r = 4 * p + 2 * g + h
                 half = slice(N * h, N * h + N)
                 totals_ref[r : r + 1, :] = rows[0, p, g, :, half]
-                totals_ref[24 + r : 25 + r, :] = rows[2, p, g, :, half]
-                parts[r : r + 1, :] = rows[1, p, g, :, half]
+                totals_ref[24 + r : 25 + r, :] = rows[1, p, g, :, half]
+                parts[r : r + 1, :] = rows[2, p, g, :, half]
     weights = jnp.transpose(parts[...])
     for p in range(3):
         for g in range(2):
@@ -193,40 +193,15 @@
     send_ref[...] = stage[: MIXED * N, :].astype(BF)
 
 
-def ready_kernel(axes_ref, q6, k6, v6, ga_ref, totals_ref, own_ref, near_ref, far_ref, own_dot, near_dot, rows):
-    masks = lane_masks()
-    for p in range(3):
-        for g in range(2):
-            r = 4 * p + 2 * g
-            rows[0, p, g] = wide(totals_ref[0:12, :], r)
-            rows[1, p, g] = wide(totals_ref[24:36, :], r)
-
-    def step(p):
-        near, far = partner_of(axes_ref, p), partner_of(axes_ref, p + 3)
-        for g in range(2):
-            lanes = slice(N * g, N * g + N)
-            queries = stack(q6[p, :, lanes] * BF(FACTOR), masks)
-            grads = stack(ga_ref[p, :, lanes], masks)
-            total = rows[0, p, g]
-            own_ref[p, g] = jnp.exp(nt(k6[p, :, lanes], queries) - total).astype(BF)
-            near_ref[p, g] = jnp.exp(nt(k6[near, :, lanes], queries) - total).astype(BF)
-            own_dot[p, g] = nt(v6[p, :, lanes], grads)
-            near_dot[p, g] = nt(v6[near, :, lanes], grads)
-            queries = stack(q6[p + 3, :, lanes] * BF(FACTOR), masks)
-            far_ref[p, g] = jnp.exp(nt(k6[far, :, lanes], queries) - rows[1, p, g]).astype(BF)
-
-    planes(step)
-
-
 def both_weights(near, far):
     top = jnp.maximum(near, far)
     log_all = top + jnp.log(jnp.exp(near - top) + jnp.exp(far - top))
-    return jnp.exp(near - log_all), jnp.exp(far - log_all)
+    return log_all, jnp.exp(near - log_all), jnp.exp(far - log_all)
 
 
 def merge_kernel(
-    ga_ref, near_ref, far_ref, totals_ref, proj_ref, got_ref, first_ref,
-    ga_col_ref, weight_ref, delta_ref, given_ref, kept_ref,
+    ga_ref, near_ref, far_ref, totals_ref, proj_ref, got_ref,
+    ga_col_ref, log_all_ref, delta_ref, given_ref, kept_ref,
     stage, parts, att,
 ):
     stage[...] = got_ref[...].astype(F32)
@@ -237,8 +212,8 @@
             ga_col_ref[p, :, N * g : N * g + N] = stage[
                 pl.ds(6 + 2 * p + g, N, stride=MIXED), :
             ].astype(BF)
-    row_near, row_far = both_weights(totals_ref[0:12, :], arrived[24:36])
-    col_near, col_far = both_weights(arrived[0:12], totals_ref[24:36, :])
+    row_log, row_near, row_far = both_weights(totals_ref[0:12, :], arrived[24:36])
+    col_log, col_near, col_far = both_weights(arrived[0:12], totals_ref[24:36, :])
     row_delta = row_near * totals_ref[12:24, :]
     col_delta = col_near * arrived[12:24]
     for p in range(3):
@@ -251,8 +226,8 @@
         row = row_delta[heads] + row_far[heads] * row_sums
         col = col_delta[heads] + col_far[heads] * col_sums
         for g in range(2):
-            weight_ref[p, g] = wide(row_near, 4 * p + 2 * g)
-            weight_ref[3 + p, g] = wide(col_far, 4 * p + 2 * g)
+            log_all_ref[p, g] = wide(row_log, 4 * p + 2 * g)
+            log_all_ref[3 + p, g] = wide(col_log, 4 * p + 2 * g)
             delta_ref[p, g] = wide(row, 2 * g)
             delta_ref[3 + p, g] = wide(col, 2 * g)
     parts[0:12, :] = row_near
@@ -277,58 +252,60 @@
 
 
 def backward_kernel(
-    axes_ref, q6, k6, v6, ga_ref, ga_col_ref, own_p, near_p, far_p, own_dot, near_dot, weight_ref, delta_ref,
+    axes_ref, q6, k6, v6, ga_ref, ga_col_ref, log_all_ref, delta_ref,
     dq_ref, dk_ref, dv_ref, send_ref,
-    stage, dq_col, dk6, dv6,
+    stage, ga6, dq6, probs, steps,
 ):
     masks = lane_masks()
 
-    def pair_step(b, c, g, prob, dots, queries, grads):
-        lanes = slice(N * g, N * g + N)
-        prob = prob.astype(F32) * weight_ref[b, g]
-        step = (prob * (dots - delta_ref[b, g])).astype(BF)
-        dq = tn(tall(step), stack(k6[c, :, lanes], masks))
-        return dq, nn(step, queries), nn(prob.astype(BF), grads)
-
-    def first(p):
+    def pair_step(b, c, g, queries, grads):
+        lanes = slice(N * g, N * g + N)
+        keys = k6[c, :, lanes]
+        prob = jnp.exp(nt(keys, queries) - log_all_ref[b, g]).astype(BF)
+        step = (prob.astype(F32) * (nt(v6[c, :, lanes], grads) - delta_ref[b, g])).astype(BF)
+        return tn(tall(step), stack(keys, masks)), nn(step, queries), nn(prob, grads)
+
+    def operands(b, g):
+        lanes = slice(N * g, N * g + N)
+        return stack(q6[b, :, lanes] * BF(FACTOR), masks), stack(ga6[b, :, lanes], masks)
+
+    for p in range(3):
+        ga6[p] = ga_ref[p]
+        ga6[p + 3] = ga_col_ref[p]
+
+    units = [(c, c) for c in range(3)] + [(partner_of(axes_ref, c), c) for c in range(6)]
+    for g in range(2):
+        lanes = slice(N * g, N * g + N)
+        for u, (b, c) in enumerate(units):
+            queries = stack(q6[b, :, lanes] * BF(FACTOR), masks)
+            prob = jnp.exp(nt(k6[c, :, lanes], queries) - log_all_ref[b, g]).astype(BF)
+            probs[2 * u + g] = prob
+            steps[2 * u + g] = (prob.astype(F32) * (nt(v6[c, :, lanes], stack(ga6[b, :, lanes], masks)) - delta_ref[b, g])).astype(BF)
+    for g in range(2):
+        lanes = slice(N * g, N * g + N)
+        for u, (b, c) in enumerate(units):
+            queries, grads = operands(b, g)
+            step = steps[2 * u + g]
+            dq = tn(tall(step), stack(k6[c, :, lanes], masks))
+            dk = nn(step, queries)
+            dv = nn(probs[2 * u + g], grads)
+            if u < 3:
+                dq_ref[c, :, lanes] = dq
+                dk_ref[c, :, lanes] = dk
+                dv_ref[c, :, lanes] = dv
+            else:
+                dq6[b, :, lanes] = dq
+                if c < 3:
+                    dk_ref[c, :, lanes] += dk
+                    dv_ref[c, :, lanes] += dv
+                else:
+                    stage[pl.ds(2 * c + g, N, stride=SENT), :] = dk
+                    stage[pl.ds(6 + 2 * c + g, N, stride=SENT), :] = dv
+    for p in range(3):
+        dq_ref[p] = (dq_ref[p] + dq6[p]) * FACTOR
         for g in range(2):
             lanes = slice(N * g, N * g + N)
-            queries = stack(q6[p, :, lanes] * BF(FACTOR), masks)
-            grads = stack(ga_ref[p, :, lanes], masks)
-            dq_ref[p, :, lanes], dk6[p, :, lanes], dv6[p, :, lanes] = pair_step(
-                p, p, g, own_p[p, g], own_dot[p, g], queries, grads
-            )
-            dk6[p + 3, :, lanes] = jnp.zeros((N, N), F32)
-            dv6[p + 3, :, lanes] = jnp.zeros((N, N), F32)
-
-    def second(p):
-        near, far = partner_of(axes_ref, p), partner_of(axes_ref, p + 3)
-        for g in range(2):
-            lanes = slice(N * g, N * g + N)
-            queries = stack(q6[p, :, lanes] * BF(FACTOR), masks)
-            grads = stack(ga_ref[p, :, lanes], masks)
-            dq, dk, dv = pair_step(p, near, g, near_p[p, g], near_dot[p, g], queries, grads)
-            dq_ref[p, :, lanes] = (dq_ref[p, :, lanes] + dq) * FACTOR
-            dk6[near, :, lanes] += dk
-            dv6[near, :, lanes] += dv
-            queries = stack(q6[p + 3, :, lanes] * BF(FACTOR), masks)
-            grads = stack(ga_col_ref[p, :, lanes], masks)
-            dots = nt(v6[far, :, lanes], grads)
-            dq, dk, dv = pair_step(p + 3, far, g, far_p[p, g], dots, queries, grads)
-            dq_col[p, :, lanes] = dq * FACTOR
-            dk6[far, :, lanes] += dk
-            dv6[far, :, lanes] += dv
-
-    planes(first)
-    planes(second)
-    for p in range(3):
-        dk_ref[p] = dk6[p]
-        dv_ref[p] = dv6[p]
-        for g in range(2):
-            lanes = slice(N * g, N * g + N)
-            stage[pl.ds(2 * p + g, N, stride=SENT), :] = dq_col[p, :, lanes]
-            stage[pl.ds(6 + 2 * p + g, N, stride=SENT), :] = dk6[3 + p, :, lanes]
-            stage[pl.ds(12 + 2 * p + g, N, stride=SENT), :] = dv6[3 + p, :, lanes]
+            stage[pl.ds(2 * p + g, N, stride=SENT), :] = dq6[3 + p, :, lanes] * FACTOR
     send_ref[...] = stage[...].astype(BF)
 
 
@@ -386,12 +363,7 @@
 def forward(*ins):
     outs = [shape(MIXED * N, N)] + [shape(6, N, 256)] * 3
     outs += [shape(*LINE, dtype=F32), shape(*LINE), shape(40, N, dtype=F32)]
-    return call(forward_kernel, ins, outs, [STAGE, SQUARE, pltpu.VMEM((3, *ROW), F32)], "forward")
-
-
-def ready(*ins):
-    outs = [shape(*PAIR)] * 3 + [shape(*PAIR, dtype=F32)] * 2
-    return call(ready_kernel, ins, outs, [pltpu.VMEM((2, *ROW), F32)], "ready", estimate=cost(10**9, 3000000))
+    return call(forward_kernel, ins, outs, [STAGE, SQUARE, pltpu.VMEM((3, *ROW), F32), pltpu.VMEM((12, N, 256), BF)], "forward")
 
 
 def merge(*ins):
@@ -403,7 +375,8 @@
 
 def backward(*ins):
     outs = [shape(*LINE, dtype=F32)] * 3 + [shape(SENT * N, N)]
-    scratch = [STAGE, pltpu.VMEM(LINE, F32)] + [pltpu.VMEM((6, N, 256), F32)] * 2
+    scratch = [STAGE, pltpu.VMEM((6, N, 256), BF), pltpu.VMEM((6, N, 256), F32)]
+    scratch += [pltpu.VMEM((18, N, 256), BF), pltpu.VMEM((18, N, 256), BF)]
     return call(backward_kernel, ins, outs, scratch, "backward")
 
 
@@ -436,14 +409,10 @@
         plane_axes, q, k, v, ga, top, total, own_out, lines
     )
     mixed = exchange(sent, MIXED)
-    own_p, near_p, far_p, own_dot, near_dot = ready(plane_axes, q6, k6, v6, ga, totals)
-
-    ga_columns, weight, delta, given, kept = merge(
-        ga, near_out, far_out, totals, out_proj, mixed, own_p
-    )
+    ga_columns, log_all, delta, given, kept = merge(ga, near_out, far_out, totals, out_proj, mixed)
     arrived = lax.ppermute(given, "head", swap)
     dq, dk, dv, sent = backward(
-        plane_axes, q6, k6, v6, ga, ga_columns, own_p, near_p, far_p, own_dot, near_dot, weight, delta
+        plane_axes, q6, k6, v6, ga, ga_columns, log_all, delta
     )
     returned = exchange(sent, SENT)
     layer = call(

time: 114 us -> 107 us (0.939)
  blocking collectives: 0 us -> 25.5 us
  waiting for transfers between devices: 55.1 us -> 41.3 us
  local copies, waits for them, and re-layouts: 9.38 us -> 0.13 us
  starting transfers between devices: 32 us -> 25.6 us
  Pallas kernels: 16.1 us -> 13.1 us
    all_to_all x0 -> x1, blocking collectives: none -> 25.5 us  [exchange(): got = lax.all_to_all(sent, 'band', split_axis=0, concat_axis=0, tiled=True)]
    all_to_all x3 -> x2, waiting for transfers between devices: 55.1 us -> 41.3 us  [exchange(): got = lax.all_to_all(sent, 'band', split_axis=0, concat_axis=0, tiled=True)]
    unnamed x51 -> x13, local copies, waits for them, and re-layouts: 9.38 us -> 0.13 us
    all_to_all x3 -> x2, starting transfers between devices: 28.3 us -> 23 us  [exchange(): got = lax.all_to_all(sent, 'band', split_axis=0, concat_axis=0, tiled=True)]
    pallas_call x7 -> x6, Pallas kernels: 14 us -> 11 us  [call(): pl.pallas_call(kernel, out_shape=tuple(outs) if many else outs[0], in_spe...]
  transfers between devices with their start and end apart: 5 -> 4, of which waited for: 3 -> 2; matrix products, arithmetic and copies ran while one was open for 0% -> 0% of each run, Pallas kernels for 9% -> 8%
where the time goes in v4:
time: 107 us; the launch traced here: 106 us
  waiting for transfers between devices  41.3 us (39%)
  starting transfers between devices  25.6 us (24%)
  blocking collectives  25.5 us (24%)
  Pallas kernels  13.1 us (12%)
    all_to_all x2, waiting for transfers between devices, exchange(): got = lax.all_to_all(sent, 'band', split_axis=0, concat_axis=0, tiled=True)  41.3 us
    all_to_all x1, blocking collectives, exchange(): got = lax.all_to_all(sent, 'band', split_axis=0, concat_axis=0, tiled=True)  25.5 us
    all_to_all x2, starting transfers between devices, exchange(): got = lax.all_to_all(sent, 'band', split_axis=0, concat_axis=0, tiled=True)  23 us
    pallas_call x6, Pallas kernels, call(): pl.pallas_call(kernel, out_shape=tuple(outs) if many else outs[0], in_spe...  11 us
    ppermute x1, starting transfers between devices, body(): other = lax.ppermute(cotangent, 'head', swap)  2.55 us
  transfers between devices with their start and end apart: 4, of which 2 were waited for; matrix products, arithmetic and copies ran while one was open for 0% of the time, Pallas kernels for 8%

profile of v4, /device:TPU:1, one launch (start us, length us, event | category | flops | bytes accessed | tf_op | source)
XLA Modules:
  0.0 106.4 jit_solution(11602069612491333463)
XLA Ops:
  0.6 2.6 %collective-permute-start = (bf16[192,1024]{1,0:T(8,128)(2,1)}, bf16[192,1024]{1,0:T(8,128)(2,1)S(1)}, u32[]{:S(2)}, u32[]{:S(2)}) collective-permute-start(bf16[192,1024]{1,0:T(8,128)(2,1)} %bitcast.27), channel_id=1, source_target_pairs={{0,1},{1,0},{2,3},{3,2},{4,5},{5,4},{6,7},{7,6},{8,9},{9,8},{10,11... | collective-permute-start | bytes 1179656 | tf_op jit(solution)/shard_map/ppermute | solution.py:404
  3.2 2.1 %pack_lines.1 = bf16[2304,128]{1,0:T(8,128)(2,1)} custom-call(bf16[3,128,256]{2,1,0:T(8,128)(2,1)} %bitcast.17, bf16[3,128,256]{2,1,0:T(8,128)(2,1)} %bitcast.20, bf16[3,128,256]{2,1,0:T(8,128)(2,1)} %bitcast.23), custom_call_target="tpu_custom_call" | custom-call | tf_op jit(solution)/shard_map/pack_lines/pallas_call | solution.py:388
  5.3 0.0 copy-start.5
  5.3 0.0 copy-start
  5.3 0.0 copy-start.1
  5.3 0.0 copy-start.2
  5.3 0.0 copy-start.3
  5.3 15.1 %all-to-all-start = ((bf16[128,9,2,128]{3,2,1,0:T(2,128)(2,1)}), bf16[128,9,2,128]{3,2,1,0:T(2,128)(2,1)S(1)}, u32[]{:S(2)}, u32[]{:S(2)}) async-start(bf16[128,9,2,128]{3,2,1,0:T(2,128)(2,1)} %bitcast.29), calls=%async_computation | async-start | bytes 1179648 | tf_op jit(solution)/shard_map/all_to_all | solution.py:332
  20.5 0.1 copy.10.axes_ref
  20.5 0.0 collective-permute-done.other_ref
  20.5 0.0 copy-done.4
  20.6 0.0 copy-done.1
  20.6 0.9 own.1
  21.5 21.1 %all-to-all-done = bf16[128,9,2,128]{3,2,1,0:T(2,128)(2,1)S(1)} async-done(((bf16[128,9,2,128]{3,2,1,0:T(2,128)(2,1)}), bf16[128,9,2,128]{3,2,1,0:T(2,128)(2,1)S(1)}, u32[]{:S(2)}, u32[]{:S(2)}) %all-to-all-start) | async-done | bytes 589856 | tf_op jit(solution)/shard_map/all_to_all | solution.py:332
  42.6 2.3 %forward.1 = (bf16[1792,128]{1,0:T(8,128)(2,1)S(1)}, bf16[6,128,256]{2,1,0:T(8,128)(2,1)S(1)}, bf16[6,128,256]{2,1,0:T(8,128)(2,1)S(1)}, bf16[6,128,256]{2,1,0:T...) custom-call(s32[3,2]{1,0:T(4,128)S(1)} %copy.10.axes_ref, ...), custom_call_target="tpu_custom_call" | custom-call | tf_op jit(solution)/shard_map/forward/pallas_call | solution.py:346
  45.0 25.5 %all_to_all.15 = bf16[128,7,2,128]{3,2,1,0:T(2,128)(2,1)S(1)} all-to-all(bf16[128,7,2,128]{3,2,1,0:T(2,128)(2,1)S(1)} %bitcast.26), channel_id=1, replica_groups=mesh['band'=128,'head'=2] {'band'}, dimensions={0} | all-to-all | bytes 917504 | tf_op jit(solution)/shard_map/all_to_all | solution.py:332
  70.4 1.4 %merge.1 = (bf16[3,128,256]{2,1,0:T(8,128)(2,1)S(1)}, f32[6,2,1,256]{3,2,1,0:T(1,128)S(1)}, f32[6,2,1,256]{3,2,1,0:T(1,128)S(1)}, bf16[192,1024]{1,0:T(8,128)(2,1)S(1)}, f32[192,1024]{1,0:T(8,128)S(1)}) custom-call(bf16[3,128,256]{2,1,0:T(8,128)(2,1)S(1)} %get-tuple-element.27.ga_ref, f32[3,128,256]{2,1,0:T(8,128)S(1)} %get-tuple-element.31.near_ref, ...), custom_call_target="tpu_custom_call" | custom-call | tf_op jit(solution)/shard_map/merge/pallas_call | solution.py:346
  71.9 0.1 collective-permute-start.1
  72.0 3.6 %backward.1 = (f32[3,128,256]{2,1,0:T(8,128)S(1)}, f32[3,128,256]{2,1,0:T(8,128)S(1)}, f32[3,128,256]{2,1,0:T(8,128)S(1)}, bf16[2304,128]{1,0:T(8,128)(2,1)}) custom-call(s32[3,2]{1,0:T(4,128)S(1)} %copy.10.axes_ref, bf16[6,128,256]{2,1,0:T(8,128)(2,1)S(1)} %get-tuple-element.37.q6, bf16[6,128,256]{2,1,0:T(8,128)(2,1)S(1)} %get-tuple-element.38.k6, ...), custom_call_target="tpu_custom_call" | custom-call | tf_op jit(solution)/shard_map/backward/pallas_call | solution.py:346
  75.5 7.9 %all-to-all-start.2 = ((bf16[128,9,2,128]{3,2,1,0:T(2,128)(2,1)}), bf16[128,9,2,128]{3,2,1,0:T(2,128)(2,1)S(1)}, u32[]{:S(2)}, u32[]{:S(2)}) async-start(bf16[128,9,2,128]{3,2,1,0:T(2,128)(2,1)} %bitcast.9), calls=%async_computation.2 | async-start | bytes 1179648 | tf_op jit(solution)/shard_map/all_to_all | solution.py:332
  83.4 0.0 collective-permute-done.1.got_ref
  83.4 1.8 %layer.1 = bf16[192,1024]{1,0:T(8,128)(2,1)} custom-call(f32[192,1024]{1,0:T(8,128)S(1)} %get-tuple-element.35.kept_ref, bf16[192,1024]{1,0:T(8,128)(2,1)} %collective-permute-done.1.got_ref), custom_call_target="tpu_custom_call" | custom-call | flops 60000002048 | bytes 1500000 | tf_op jit(solution)/shard_map/layer/pallas_call | solution.py:346
  85.3 20.2 %all-to-all-done.2 = bf16[128,9,2,128]{3,2,1,0:T(2,128)(2,1)S(1)} async-done(((bf16[128,9,2,128]{3,2,1,0:T(2,128)(2,1)}), bf16[128,9,2,128]{3,2,1,0:T(2,128)(2,1)S(1)}, u32[]{:S(2)}, u32[]{:S(2)}) %all-to-all-start.2) | async-done | bytes 589856 | tf_op jit(solution)/shard_map/all_to_all | solution.py:332
  105.4 0.9 finish.1
  (5 shorter events, 0.0 us)
Async XLA Ops:
  0.6 19.9 %collective-permute-start = (bf16[192,1024]{1,0:T(8,128)(2,1)}, bf16[192,1024]{1,0:T(8,128)(2,1)S(1)}, u32[]{:S(2)}, u32[]{:S(2)}) collective-permute-start(bf16[192,1024]{1,0:T(8,128)(2,1)} %bitcast.27), channel_id=1, source_target_pairs={{0,1},{1,0},{2,3},{3,2},{4,5},{5,4},{6,7},{7,6},{8,9},{9,8},{10,11... | collective-permute-start | bytes 1179656 | tf_op jit(solution)/shard_map/ppermute | solution.py:404
  3.2 17.4 %copy-start.4 = (bf16[1,3,64,1024]{3,2,1,0:T(8,128)(2,1)S(1)}, bf16[1,3,64,1024]{3,2,1,0:T(8,128)(2,1)}, u32[]{:S(2)}) copy-start(bf16[1,3,64,1024]{3,2,1,0:T(8,128)(2,1)} %param.10) | copy-start | bytes 1179652
  5.3 15.2 %copy-start.5 = (s32[3,2]{0,1:T(2,128)S(1)}, s32[3,2]{0,1:T(2,128)}, u32[]{:S(2)}) copy-start(s32[3,2]{0,1:T(2,128)} %param.11) | copy-start | bytes 76
  5.3 15.3 %copy-start = (bf16[1,3,128,256]{3,2,1,0:T(8,128)(2,1)S(1)}, bf16[1,3,128,256]{3,2,1,0:T(8,128)(2,1)}, u32[]{:S(2)}) copy-start(bf16[1,3,128,256]{3,2,1,0:T(8,128)(2,1)} %param.6) | copy-start | bytes 589828
  5.3 15.3 %copy-start.1 = (bf16[1,3,128,256]{3,2,1,0:T(8,128)(2,1)S(1)}, bf16[1,3,128,256]{3,2,1,0:T(8,128)(2,1)}, u32[]{:S(2)}) copy-start(bf16[1,3,128,256]{3,2,1,0:T(8,128)(2,1)} %param.7) | copy-start | bytes 589828
  5.3 15.2 %copy-start.2 = (bf16[1,3,128,256]{3,2,1,0:T(8,128)(2,1)S(1)}, bf16[1,3,128,256]{3,2,1,0:T(8,128)(2,1)}, u32[]{:S(2)}) copy-start(bf16[1,3,128,256]{3,2,1,0:T(8,128)(2,1)} %param.8) | copy-start | bytes 589828
  5.3 15.2 %copy-start.3 = (bf16[256,1024]{1,0:T(8,128)(2,1)S(1)}, bf16[256,1024]{1,0:T(8,128)(2,1)}, u32[]{:S(2)}) copy-start(bf16[256,1024]{1,0:T(8,128)(2,1)} %proj_ref.3) | copy-start | bytes 1572868
  5.3 37.3 %all-to-all-start = ((bf16[128,9,2,128]{3,2,1,0:T(2,128)(2,1)}), bf16[128,9,2,128]{3,2,1,0:T(2,128)(2,1)S(1)}, u32[]{:S(2)}, u32[]{:S(2)}) async-start(bf16[128,9,2,128]{3,2,1,0:T(2,128)(2,1)} %bitcast.29), calls=%async_computation | async-start | bytes 1179648 | tf_op jit(solution)/shard_map/all_to_all | solution.py:332
  71.9 11.6 %collective-permute-start.1 = (bf16[192,1024]{1,0:T(8,128)(2,1)S(1)}, bf16[192,1024]{1,0:T(8,128)(2,1)}, u32[]{:S(2)}, u32[]{:S(2)}) collective-permute-start(bf16[192,1024]{1,0:T(8,128)(2,1)S(1)} %get-tuple-element.36), channel_id=1, source_target_pairs={{0,1},{1,0},{2,3},{3,2},{4,5},{5,4},{6,7},{7,6},{8,9},{9,8},{10,11... | collective-permute-start | bytes 1179656 | tf_op jit(solution)/shard_map/ppermute | solution.py:413
  75.5 29.9 %all-to-all-start.2 = ((bf16[128,9,2,128]{3,2,1,0:T(2,128)(2,1)}), bf16[128,9,2,128]{3,2,1,0:T(2,128)(2,1)S(1)}, u32[]{:S(2)}, u32[]{:S(2)}) async-start(bf16[128,9,2,128]{3,2,1,0:T(2,128)(2,1)} %bitcast.9), calls=%async_computation.2 | async-start | bytes 1179648 | tf_op jit(solution)/shard_map/all_to_all | solution.py:332

commit v5 on v4

--- a/solution.py
+++ b/solution.py
@@ -17,6 +17,7 @@
 PARAMS = pltpu.CompilerParams(vmem_limit_bytes=48 * 1024 * 1024)
 ROOMY = pltpu.CompilerParams(vmem_limit_bytes=60 * 1024 * 1024)
 VMEM = pl.BlockSpec(memory_space=pltpu.VMEM)
+HBM = pl.BlockSpec(memory_space=pltpu.HBM)
 SMEM = pl.BlockSpec(memory_space=pltpu.SMEM)
 
 
@@ -77,20 +78,32 @@
     return jnp.where(lane < HALF, columns[:, r : r + 1], columns[:, r + 1 : r + 2])
 
 
-def pack_lines_kernel(q_ref, k_ref, v_ref, out_ref, held, stage, sems):
-    copies = [
-        pltpu.make_async_copy(ref, held.at[a], sems.at[a])
-        for a, ref in enumerate((q_ref, k_ref, v_ref))
-    ]
-    for copy in copies:
-        copy.start()
-    for a, copy in enumerate(copies):
-        copy.wait()
-        for p in range(3):
-            for g in range(2):
-                rows = pl.ds(2 * (3 * a + p) + g, N, stride=SENT)
-                stage[rows, :] = held[a, p, :, N * g : N * g + N].astype(F32)
-    out_ref[...] = stage[...].astype(BF)
+def pack_lines_kernel(q_ref, k_ref, v_ref, out_ref, held, stage, packed, in_sems, out_sems):
+    def arriving(a, ref, h):
+        cols = slice(HALF * h, HALF * h + HALF)
+        return pltpu.make_async_copy(ref.at[:, cols, :], held.at[a, :, cols, :], in_sems.at[a, h])
+
+    def leaving(h):
+        rows = pl.ds(HALF * SENT * h, HALF * SENT)
+        return pltpu.make_async_copy(packed.at[rows], out_ref.at[rows], out_sems.at[h])
+
+    inputs = (q_ref, k_ref, v_ref)
+    for h in range(2):
+        for a, ref in enumerate(inputs):
+            arriving(a, ref, h).start()
+    for h in range(2):
+        cols = slice(HALF * h, HALF * h + HALF)
+        for a, ref in enumerate(inputs):
+            arriving(a, ref, h).wait()
+            for p in range(3):
+                for g in range(2):
+                    rows = pl.ds(HALF * SENT * h + 2 * (3 * a + p) + g, HALF, stride=SENT)
+                    stage[rows, :] = held[a, p, cols, N * g : N * g + N].astype(F32)
+        rows = slice(HALF * SENT * h, HALF * SENT * h + HALF * SENT)
+        packed[rows, :] = stage[rows, :].astype(BF)
+        leaving(h).start()
+    for h in range(2):
+        leaving(h).wait()
 
 
 def own_kernel(
@@ -241,29 +254,24 @@
                 + spread(weights, 12 + r) * stage[pl.ds(2 * p + g, N, stride=MIXED), :]
             ).astype(BF)
     me = lax.axis_index("head")
-    for side, out in ((1 - me, given_ref), (me, kept_ref)):
-        tokens = pl.ds(pl.multiple_of(side * HALF, HALF), HALF)
-        for p in range(3):
-            out[HALF * p : HALF * p + HALF, :] = nn(att[p, tokens, :], proj_ref[...]).astype(out.dtype)
-
-
-def layer_kernel(kept_ref, got_ref, out_ref):
-    out_ref[...] = (kept_ref[...] + got_ref[...].astype(F32)).astype(BF)
+    theirs = pl.ds(pl.multiple_of((1 - me) * HALF, HALF), HALF)
+    mine = pl.ds(pl.multiple_of(me * HALF, HALF), HALF)
+    for p in range(3):
+        rows = slice(HALF * p, HALF * p + HALF)
+        kept_ref[rows, :] = att[p, mine, :]
+        given_ref[rows, :] = nn(att[p, theirs, :], proj_ref[...]).astype(BF)
+
+
+def layer_kernel(kept_ref, proj_ref, got_ref, out_ref):
+    out_ref[...] = (nn(kept_ref[...], proj_ref[...]) + got_ref[...].astype(F32)).astype(BF)
 
 
 def backward_kernel(
     axes_ref, q6, k6, v6, ga_ref, ga_col_ref, log_all_ref, delta_ref,
     dq_ref, dk_ref, dv_ref, send_ref,
-    stage, ga6, dq6, probs, steps,
+    stage, ga6, dq6, probs, steps, packed, sem,
 ):
     masks = lane_masks()
-
-    def pair_step(b, c, g, queries, grads):
-        lanes = slice(N * g, N * g + N)
-        keys = k6[c, :, lanes]
-        prob = jnp.exp(nt(keys, queries) - log_all_ref[b, g]).astype(BF)
-        step = (prob.astype(F32) * (nt(v6[c, :, lanes], grads) - delta_ref[b, g])).astype(BF)
-        return tn(tall(step), stack(keys, masks)), nn(step, queries), nn(prob, grads)
 
     def operands(b, g):
         lanes = slice(N * g, N * g + N)
@@ -273,50 +281,67 @@
         ga6[p] = ga_ref[p]
         ga6[p + 3] = ga_col_ref[p]
 
-    units = [(c, c) for c in range(3)] + [(partner_of(axes_ref, c), c) for c in range(6)]
+    def score(units):
+        for g in range(2):
+            lanes = slice(N * g, N * g + N)
+            for u, b, c in units:
+                queries, grads = operands(b, g)
+                prob = jnp.exp(nt(k6[c, :, lanes], queries) - log_all_ref[b, g]).astype(BF)
+                dots = nt(v6[c, :, lanes], grads)
+                probs[2 * u + g] = prob
+                steps[2 * u + g] = (prob.astype(F32) * (dots - delta_ref[b, g])).astype(BF)
+
+    def multiply(g, u, b, c):
+        queries, grads = operands(b, g)
+        step = steps[2 * u + g]
+        dq = tn(tall(step), stack(k6[c, :, N * g : N * g + N], masks))
+        return dq, nn(step, queries), nn(probs[2 * u + g], grads)
+
+    cross = [(c, partner_of(axes_ref, c), c) for c in range(6)]
+    same = [(c, c, c) for c in range(3)]
+    score(cross)
     for g in range(2):
         lanes = slice(N * g, N * g + N)
-        for u, (b, c) in enumerate(units):
-            queries = stack(q6[b, :, lanes] * BF(FACTOR), masks)
-            prob = jnp.exp(nt(k6[c, :, lanes], queries) - log_all_ref[b, g]).astype(BF)
-            probs[2 * u + g] = prob
-            steps[2 * u + g] = (prob.astype(F32) * (nt(v6[c, :, lanes], stack(ga6[b, :, lanes], masks)) - delta_ref[b, g])).astype(BF)
-    for g in range(2):
-        lanes = slice(N * g, N * g + N)
-        for u, (b, c) in enumerate(units):
-            queries, grads = operands(b, g)
-            step = steps[2 * u + g]
-            dq = tn(tall(step), stack(k6[c, :, lanes], masks))
-            dk = nn(step, queries)
-            dv = nn(probs[2 * u + g], grads)
-            if u < 3:
-                dq_ref[c, :, lanes] = dq
+        for u, b, c in cross:
+            dq, dk, dv = multiply(g, u, b, c)
+            dq6[b, :, lanes] = dq
+            if c < 3:
                 dk_ref[c, :, lanes] = dk
                 dv_ref[c, :, lanes] = dv
             else:
-                dq6[b, :, lanes] = dq
-                if c < 3:
-                    dk_ref[c, :, lanes] += dk
-                    dv_ref[c, :, lanes] += dv
-                else:
-                    stage[pl.ds(2 * c + g, N, stride=SENT), :] = dk
-                    stage[pl.ds(6 + 2 * c + g, N, stride=SENT), :] = dv
-    for p in range(3):
-        dq_ref[p] = (dq_ref[p] + dq6[p]) * FACTOR
+                stage[pl.ds(2 * c + g, N, stride=SENT), :] = dk
+                stage[pl.ds(6 + 2 * c + g, N, stride=SENT), :] = dv
+    for p in range(3):
         for g in range(2):
             lanes = slice(N * g, N * g + N)
             stage[pl.ds(2 * p + g, N, stride=SENT), :] = dq6[3 + p, :, lanes] * FACTOR
-    send_ref[...] = stage[...].astype(BF)
-
-
-def finish_kernel(dq_ref, dk_ref, dv_ref, got_ref, q_out, k_out, v_out, stage):
+    packed[...] = stage[...].astype(BF)
+    leaving = pltpu.make_async_copy(packed, send_ref, sem)
+    leaving.start()
+    score(same)
+    for g in range(2):
+        lanes = slice(N * g, N * g + N)
+        for u, b, c in same:
+            dq, dk, dv = multiply(g, u, b, c)
+            dq_ref[c, :, lanes] = (dq6[c, :, lanes] + dq) * FACTOR
+            dk_ref[c, :, lanes] += dk
+            dv_ref[c, :, lanes] += dv
+    leaving.wait()
+
+
+def finish_kernel(dq_ref, dk_ref, dv_ref, got_ref, q_out, k_out, v_out, stage, made, sems):
     stage[...] = got_ref[...].astype(F32)
+    copies = []
     for a, (mine, out) in enumerate(((dq_ref, q_out), (dk_ref, k_out), (dv_ref, v_out))):
         for p in range(3):
             for g in range(2):
                 lanes = slice(N * g, N * g + N)
                 rows = pl.ds(2 * (3 * a + p) + g, N, stride=SENT)
-                out[p, :, lanes] = (mine[p, :, lanes] + stage[rows, :]).astype(BF)
+                made[a, p, :, lanes] = (mine[p, :, lanes] + stage[rows, :]).astype(BF)
+        copies.append(pltpu.make_async_copy(made.at[a], out, sems.at[a]))
+        copies[-1].start()
+    for copy in copies:
+        copy.wait()
 
 
 def shape(*dims, dtype=BF):
@@ -338,6 +363,7 @@
 PAIR = (3, 2, N, 256)
 ROW = (3, 2, 1, 256)
 STAGE = pltpu.VMEM((SENT * N, N), F32)
+PACKED = pltpu.VMEM((SENT * N, N), BF)
 SQUARE = pltpu.VMEM((N, N), F32)
 
 
@@ -368,29 +394,50 @@
 
 def merge(*ins):
     rows = shape(6, 2, 1, 256, dtype=F32)
-    outs = [shape(*LINE), rows, rows, shape(*TOKENS), shape(*TOKENS, dtype=F32)]
+    outs = [shape(*LINE), rows, rows, shape(*TOKENS), shape(3 * HALF, 256)]
     scratch = [pltpu.VMEM((MIXED * N, N), F32), SQUARE, pltpu.VMEM(LINE, BF)]
     return call(merge_kernel, ins, outs, scratch, "merge")
 
 
 def backward(*ins):
-    outs = [shape(*LINE, dtype=F32)] * 3 + [shape(SENT * N, N)]
     scratch = [STAGE, pltpu.VMEM((6, N, 256), BF), pltpu.VMEM((6, N, 256), F32)]
-    scratch += [pltpu.VMEM((18, N, 256), BF), pltpu.VMEM((18, N, 256), BF)]
-    return call(backward_kernel, ins, outs, scratch, "backward")
+    scratch += [pltpu.VMEM((12, N, 256), BF)] * 2 + [PACKED, pltpu.SemaphoreType.DMA]
+    return pl.pallas_call(
+        backward_kernel,
+        out_shape=(shape(*LINE, dtype=F32),) * 3 + (shape(SENT * N, N),),
+        in_specs=[SMEM] + [VMEM] * (len(ins) - 1),
+        out_specs=(VMEM, VMEM, VMEM, HBM),
+        scratch_shapes=scratch,
+        compiler_params=PARAMS,
+        name="backward",
+    )(*ins)
 
 
 def finish(*ins):
-    return call(finish_kernel, ins, [shape(*LINE)] * 3, [STAGE], "finish")
+    return pl.pallas_call(
+        finish_kernel,
+        out_shape=(shape(*LINE),) * 3,
+        in_specs=[VMEM] * 4,
+        out_specs=(HBM,) * 3,
+        scratch_shapes=[STAGE, pltpu.VMEM((3, *LINE), BF), pltpu.SemaphoreType.DMA((3,))],
+        compiler_params=PARAMS,
+        name="finish",
+    )(*ins)
 
 
 def pack_lines(*ins):
     return pl.pallas_call(
         pack_lines_kernel,
         out_shape=shape(SENT * N, N),
-        in_specs=[pl.BlockSpec(memory_space=pltpu.HBM)] * 3,
-        out_specs=VMEM,
-        scratch_shapes=[pltpu.VMEM((3, *LINE), BF), STAGE, pltpu.SemaphoreType.DMA((3,))],
+        in_specs=[HBM] * 3,
+        out_specs=HBM,
+        scratch_shapes=[
+            pltpu.VMEM((3, *LINE), BF),
+            STAGE,
+            PACKED,
+            pltpu.SemaphoreType.DMA((3, 2)),
+            pltpu.SemaphoreType.DMA((2,)),
+        ],
         compiler_params=ROOMY,
         name="pack_lines",
     )(*ins)
@@ -416,7 +463,7 @@
     )
     returned = exchange(sent, SENT)
     layer = call(
-        layer_kernel, (kept, arrived), [shape(*TOKENS)], [], "layer", estimate=cost(LONG, 1500000)
+        layer_kernel, (kept, out_proj, arrived), [shape(*TOKENS)], [], "layer", estimate=cost(LONG, 1500000)
     )
     dq, dk, dv = finish(dq, dk, dv, returned)
     return layer.reshape(1, 3, HALF, 1024), dq[None], dk[None], dv[None]

time: 107 us -> 106 us (level)
  Pallas kernels: 13.1 us -> 11.6 us
    pallas_call x6 -> x4, Pallas kernels: 11 us -> 5.38 us  [call(): pl.pallas_call(kernel, out_shape=tuple(outs) if many else outs[0], in_spe...]
    pallas_call x0 -> x2, Pallas kernels: none -> 4.26 us  [the longest x1 3.31 us: backward(): pl.pallas_call(backward_kernel, out_shape=(shape(*LINE, dtype=F32),) * 3...]
  transfers between devices with their start and end apart: 4 -> 4, of which waited for: 2 -> 2; matrix products, arithmetic and copies ran while one was open for 0% -> 0% of each run, Pallas kernels for 8% -> 7%
where the time goes in v5:
time: 106 us
  waiting for transfers between devices  42.1 us (40%)
  starting transfers between devices  25.6 us (24%)
  blocking collectives  25.5 us (24%)
  Pallas kernels  11.6 us (11%)
    all_to_all x2, waiting for transfers between devices, exchange(): got = lax.all_to_all(sent, 'band', split_axis=0, concat_axis=0, tiled=True)  42.1 us
    all_to_all x1, blocking collectives, exchange(): got = lax.all_to_all(sent, 'band', split_axis=0, concat_axis=0, tiled=True)  25.5 us
    all_to_all x2, starting transfers between devices, exchange(): got = lax.all_to_all(sent, 'band', split_axis=0, concat_axis=0, tiled=True)  23 us
    pallas_call x4, Pallas kernels, call(): pl.pallas_call(kernel, out_shape=tuple(outs) if many else outs[0], in_spe...  5.38 us
    pallas_call x1, Pallas kernels, backward(): pl.pallas_call(backward_kernel, out_shape=(shape(*LINE, dtype=F32),) * 3...  3.31 us
    ppermute x1, starting transfers between devices, body(): other = lax.ppermute(cotangent, 'head', swap)  2.55 us
  transfers between devices with their start and end apart: 4, of which 2 were waited for; matrix products, arithmetic and copies ran while one was open for 0% of the time, Pallas kernels for 7%

profile of v5, /device:TPU:1, one launch (start us, length us, event | category | flops | bytes accessed | tf_op | source)
XLA Modules:
  0.0 105.7 jit_solution(15137226570441653441)
XLA Ops:
  0.6 2.6 %collective-permute-start = (bf16[192,1024]{1,0:T(8,128)(2,1)}, bf16[192,1024]{1,0:T(8,128)(2,1)S(1)}, u32[]{:S(2)}, u32[]{:S(2)}) collective-permute-start(bf16[192,1024]{1,0:T(8,128)(2,1)} %bitcast.27), channel_id=1, source_target_pairs={{0,1},{1,0},{2,3},{3,2},{4,5},{5,4},{6,7},{7,6},{8,9},{9,8},{10,11... | collective-permute-start | bytes 1179656 | tf_op jit(solution)/shard_map/ppermute | solution.py:451
  3.2 2.0 %pack_lines.1 = bf16[2304,128]{1,0:T(8,128)(2,1)} custom-call(bf16[3,128,256]{2,1,0:T(8,128)(2,1)} %bitcast.17, bf16[3,128,256]{2,1,0:T(8,128)(2,1)} %bitcast.20, bf16[3,128,256]{2,1,0:T(8,128)(2,1)} %bitcast.23), custom_call_target="tpu_custom_call" | custom-call | tf_op jit(solution)/shard_map/pack_lines/pallas_call | solution.py:429
  5.2 0.0 copy-start.5
  5.2 0.0 copy-start
  5.2 0.0 copy-start.1
  5.2 0.0 copy-start.2
  5.2 0.0 copy-start.3
  5.2 15.1 %all-to-all-start = ((bf16[128,9,2,128]{3,2,1,0:T(2,128)(2,1)}), bf16[128,9,2,128]{3,2,1,0:T(2,128)(2,1)S(1)}, u32[]{:S(2)}, u32[]{:S(2)}) async-start(bf16[128,9,2,128]{3,2,1,0:T(2,128)(2,1)} %bitcast.29), calls=%async_computation | async-start | bytes 1179648 | tf_op jit(solution)/shard_map/all_to_all | solution.py:357
  20.3 0.0 copy-done.5
  20.4 0.1 copy.10.axes_ref
  20.5 0.0 collective-permute-done.other_ref
  20.5 0.0 copy-done.4
  20.5 0.9 own.1
  21.4 21.1 %all-to-all-done = bf16[128,9,2,128]{3,2,1,0:T(2,128)(2,1)S(1)} async-done(((bf16[128,9,2,128]{3,2,1,0:T(2,128)(2,1)}), bf16[128,9,2,128]{3,2,1,0:T(2,128)(2,1)S(1)}, u32[]{:S(2)}, u32[]{:S(2)}) %all-to-all-start) | async-done | bytes 589856 | tf_op jit(solution)/shard_map/all_to_all | solution.py:357
  42.5 2.3 %forward.1 = (bf16[1792,128]{1,0:T(8,128)(2,1)S(1)}, bf16[6,128,256]{2,1,0:T(8,128)(2,1)S(1)}, bf16[6,128,256]{2,1,0:T(8,128)(2,1)S(1)}, bf16[6,128,256]{2,1,0:T...) custom-call(s32[3,2]{1,0:T(4,128)S(1)} %copy.10.axes_ref, ...), custom_call_target="tpu_custom_call" | custom-call | tf_op jit(solution)/shard_map/forward/pallas_call | solution.py:372
  44.9 25.5 %all_to_all.15 = bf16[128,7,2,128]{3,2,1,0:T(2,128)(2,1)S(1)} all-to-all(bf16[128,7,2,128]{3,2,1,0:T(2,128)(2,1)S(1)} %bitcast.26), channel_id=1, replica_groups=mesh['band'=128,'head'=2] {'band'}, dimensions={0} | all-to-all | bytes 917504 | tf_op jit(solution)/shard_map/all_to_all | solution.py:357
  70.3 1.1 %merge.1 = (bf16[3,128,256]{2,1,0:T(8,128)(2,1)S(1)}, f32[6,2,1,256]{3,2,1,0:T(1,128)S(1)}, f32[6,2,1,256]{3,2,1,0:T(1,128)S(1)}, bf16[192,1024]{1,0:T(8,128)(2,1)S(1)}, bf16[192,256]{1,0:T(8,128)(2,1)S(1)}) custom-call(bf16[3,128,256]{2,1,0:T(8,128)(2,1)S(1)} %get-tuple-element.27.ga_ref, f32[3,128,256]{2,1,0:T(8,128)S(1)} %get-tuple-element.31.near_ref, ...), custom_call_target="tpu_custom_call" | custom-call | tf_op jit(solution)/shard_map/merge/pallas_call | solution.py:372
  71.4 0.1 collective-permute-start.1
  71.5 3.3 %backward.1 = (f32[3,128,256]{2,1,0:T(8,128)S(1)}, f32[3,128,256]{2,1,0:T(8,128)S(1)}, f32[3,128,256]{2,1,0:T(8,128)S(1)}, bf16[2304,128]{1,0:T(8,128)(2,1)}) custom-call(s32[3,2]{1,0:T(4,128)S(1)} %copy.10.axes_ref, bf16[6,128,256]{2,1,0:T(8,128)(2,1)S(1)} %get-tuple-element.37.q6, bf16[6,128,256]{2,1,0:T(8,128)(2,1)S(1)} %get-tuple-element.38.k6, ...), custom_call_target="tpu_custom_call" | custom-call | tf_op jit(solution)/shard_map/backward/pallas_call | solution.py:405
  74.9 7.9 %all-to-all-start.2 = ((bf16[128,9,2,128]{3,2,1,0:T(2,128)(2,1)}), bf16[128,9,2,128]{3,2,1,0:T(2,128)(2,1)S(1)}, u32[]{:S(2)}, u32[]{:S(2)}) async-start(bf16[128,9,2,128]{3,2,1,0:T(2,128)(2,1)} %bitcast.9), calls=%async_computation.2 | async-start | bytes 1179648 | tf_op jit(solution)/shard_map/all_to_all | solution.py:357
  82.8 0.0 collective-permute-done.1.got_ref
  82.8 1.0 layer.1
  83.8 21.0 %all-to-all-done.2 = bf16[128,9,2,128]{3,2,1,0:T(2,128)(2,1)S(1)} async-done(((bf16[128,9,2,128]{3,2,1,0:T(2,128)(2,1)}), bf16[128,9,2,128]{3,2,1,0:T(2,128)(2,1)S(1)}, u32[]{:S(2)}, u32[]{:S(2)}) %all-to-all-start.2) | async-done | bytes 589856 | tf_op jit(solution)/shard_map/all_to_all | solution.py:357
  104.8 1.0 finish.1
  (5 shorter events, 0.0 us)
Async XLA Ops:
  0.6 19.8 %collective-permute-start = (bf16[192,1024]{1,0:T(8,128)(2,1)}, bf16[192,1024]{1,0:T(8,128)(2,1)S(1)}, u32[]{:S(2)}, u32[]{:S(2)}) collective-permute-start(bf16[192,1024]{1,0:T(8,128)(2,1)} %bitcast.27), channel_id=1, source_target_pairs={{0,1},{1,0},{2,3},{3,2},{4,5},{5,4},{6,7},{7,6},{8,9},{9,8},{10,11... | collective-permute-start | bytes 1179656 | tf_op jit(solution)/shard_map/ppermute | solution.py:451
  3.2 17.3 %copy-start.4 = (bf16[1,3,64,1024]{3,2,1,0:T(8,128)(2,1)S(1)}, bf16[1,3,64,1024]{3,2,1,0:T(8,128)(2,1)}, u32[]{:S(2)}) copy-start(bf16[1,3,64,1024]{3,2,1,0:T(8,128)(2,1)} %param.10) | copy-start | bytes 1179652
  5.2 15.2 %copy-start.5 = (s32[3,2]{0,1:T(2,128)S(1)}, s32[3,2]{0,1:T(2,128)}, u32[]{:S(2)}) copy-start(s32[3,2]{0,1:T(2,128)} %param.11) | copy-start | bytes 76
  5.2 15.3 %copy-start = (bf16[1,3,128,256]{3,2,1,0:T(8,128)(2,1)S(1)}, bf16[1,3,128,256]{3,2,1,0:T(8,128)(2,1)}, u32[]{:S(2)}) copy-start(bf16[1,3,128,256]{3,2,1,0:T(8,128)(2,1)} %param.6) | copy-start | bytes 589828
  5.2 15.3 %copy-start.1 = (bf16[1,3,128,256]{3,2,1,0:T(8,128)(2,1)S(1)}, bf16[1,3,128,256]{3,2,1,0:T(8,128)(2,1)}, u32[]{:S(2)}) copy-start(bf16[1,3,128,256]{3,2,1,0:T(8,128)(2,1)} %param.7) | copy-start | bytes 589828
  5.2 15.2 %copy-start.2 = (bf16[1,3,128,256]{3,2,1,0:T(8,128)(2,1)S(1)}, bf16[1,3,128,256]{3,2,1,0:T(8,128)(2,1)}, u32[]{:S(2)}) copy-start(bf16[1,3,128,256]{3,2,1,0:T(8,128)(2,1)} %param.8) | copy-start | bytes 589828
  5.2 15.2 %copy-start.3 = (bf16[256,1024]{1,0:T(8,128)(2,1)S(1)}, bf16[256,1024]{1,0:T(8,128)(2,1)}, u32[]{:S(2)}) copy-start(bf16[256,1024]{1,0:T(8,128)(2,1)} %proj_ref.5) | copy-start | bytes 1572868
  5.2 37.3 %all-to-all-start = ((bf16[128,9,2,128]{3,2,1,0:T(2,128)(2,1)}), bf16[128,9,2,128]{3,2,1,0:T(2,128)(2,1)S(1)}, u32[]{:S(2)}, u32[]{:S(2)}) async-start(bf16[128,9,2,128]{3,2,1,0:T(2,128)(2,1)} %bitcast.29), calls=%async_computation | async-start | bytes 1179648 | tf_op jit(solution)/shard_map/all_to_all | solution.py:357
  71.4 11.3 %collective-permute-start.1 = (bf16[192,1024]{1,0:T(8,128)(2,1)S(1)}, bf16[192,1024]{1,0:T(8,128)(2,1)S(1)}, u32[]{:S(2)}, u32[]{:S(2)}) collective-permute-start(bf16[192,1024]{1,0:T(8,128)(2,1)S(1)} %get-tuple-element.36), channel_id=1, source_target_pairs={{0,1},{1,0},{2,3},{3,2},{4,5},{5,4},{6,7},{7,6},{8,9},{9,8},{10,11... | collective-permute-start | bytes 1179656 | tf_op jit(solution)/shard_map/ppermute | solution.py:460
  74.9 29.9 %all-to-all-start.2 = ((bf16[128,9,2,128]{3,2,1,0:T(2,128)(2,1)}), bf16[128,9,2,128]{3,2,1,0:T(2,128)(2,1)S(1)}, u32[]{:S(2)}, u32[]{:S(2)}) async-start(bf16[128,9,2,128]{3,2,1,0:T(2,128)(2,1)} %bitcast.9), calls=%async_computation.2 | async-start | bytes 1179648 | tf_op jit(solution)/shard_map/all_to_all | solution.py:357

commit v6 on v5

--- a/solution.py
+++ b/solution.py
@@ -18,7 +18,6 @@
 ROOMY = pltpu.CompilerParams(vmem_limit_bytes=60 * 1024 * 1024)
 VMEM = pl.BlockSpec(memory_space=pltpu.VMEM)
 HBM = pl.BlockSpec(memory_space=pltpu.HBM)
-SMEM = pl.BlockSpec(memory_space=pltpu.SMEM)
 
 
 def nt(a, b):
@@ -52,12 +51,16 @@
     return nt(pick, high) + nt(pick, low)
 
 
-def partner_of(axes_ref, b):
-    axis = axes_ref[lax.rem(b, 3), lax.div(b, 3)]
-    found = jnp.int32(0)
-    for c in range(6):
-        same = jnp.logical_and(axes_ref[c % 3, c // 3] == axis, b != c)
-        found = found + jnp.where(same, jnp.int32(c), jnp.int32(0))
+def partners(axes_ref):
+    axes = axes_ref[...]
+    axis = [axes[b % 3, b // 3] for b in range(6)]
+    found = []
+    for b in range(6):
+        other = jnp.int32(0)
+        for c in range(6):
+            if c != b:
+                other = other + jnp.where(axis[c] == axis[b], jnp.int32(c), jnp.int32(0))
+        found.append(other)
     return found
 
 
@@ -146,7 +149,7 @@
                 lines = pl.ds(2 * (3 * a + p) + g, N, stride=SENT)
                 six[3 + p, :, N * g : N * g + N] = stage[lines, :].astype(BF)
 
-    blocks = [(b, partner_of(axes_ref, b)) for b in range(6)]
+    blocks = list(enumerate(partners(axes_ref)))
     for g in range(2):
         lanes = slice(N * g, N * g + N)
         for b, c in blocks:
@@ -286,10 +289,10 @@
             lanes = slice(N * g, N * g + N)
             for u, b, c in units:
                 queries, grads = operands(b, g)
-                prob = jnp.exp(nt(k6[c, :, lanes], queries) - log_all_ref[b, g]).astype(BF)
+                prob = jnp.exp(nt(k6[c, :, lanes], queries) - log_all_ref[b, g])
                 dots = nt(v6[c, :, lanes], grads)
-                probs[2 * u + g] = prob
-                steps[2 * u + g] = (prob.astype(F32) * (dots - delta_ref[b, g])).astype(BF)
+                probs[2 * u + g] = prob.astype(BF)
+                steps[2 * u + g] = (prob * (dots - delta_ref[b, g])).astype(BF)
 
     def multiply(g, u, b, c):
         queries, grads = operands(b, g)
@@ -297,7 +300,7 @@
         dq = tn(tall(step), stack(k6[c, :, N * g : N * g + N], masks))
         return dq, nn(step, queries), nn(probs[2 * u + g], grads)
 
-    cross = [(c, partner_of(axes_ref, c), c) for c in range(6)]
+    cross = [(c, b, c) for c, b in enumerate(partners(axes_ref))]
     same = [(c, c, c) for c in range(3)]
     score(cross)
     for g in range(2):
@@ -372,7 +375,7 @@
     return pl.pallas_call(
         kernel,
         out_shape=tuple(outs) if many else outs[0],
-        in_specs=[SMEM if x.dtype == jnp.int32 else VMEM for x in ins],
+        in_specs=[VMEM] * len(ins),
         out_specs=(VMEM,) * len(outs) if many else VMEM,
         scratch_shapes=scratch,
         compiler_params=params,
@@ -405,7 +408,7 @@
     return pl.pallas_call(
         backward_kernel,
         out_shape=(shape(*LINE, dtype=F32),) * 3 + (shape(SENT * N, N),),
-        in_specs=[SMEM] + [VMEM] * (len(ins) - 1),
+        in_specs=[VMEM] * len(ins),
         out_specs=(VMEM, VMEM, VMEM, HBM),
         scratch_shapes=scratch,
         compiler_params=PARAMS,

time: 106 us -> 105 us (level)
  transfers between devices with their start and end apart: 4 -> 4, of which waited for: 2 -> 2; matrix products, arithmetic and copies ran while one was open for 0% -> 0% of each run, Pallas kernels for 7% -> 6%
where the time goes in v6:
time: 105 us
  waiting for transfers between devices  42.1 us (40%)
  starting transfers between devices  25.6 us (24%)
  blocking collectives  25.5 us (24%)
  Pallas kernels  10.6 us (10%)
    all_to_all x2, waiting for transfers between devices, exchange(): got = lax.all_to_all(sent, 'band', split_axis=0, concat_axis=0, tiled=True)  42.1 us
    all_to_all x1, blocking collectives, exchange(): got = lax.all_to_all(sent, 'band', split_axis=0, concat_axis=0, tiled=True)  25.5 us
    all_to_all x2, starting transfers between devices, exchange(): got = lax.all_to_all(sent, 'band', split_axis=0, concat_axis=0, tiled=True)  23 us
    pallas_call x4, Pallas kernels, call(): pl.pallas_call(kernel, out_shape=tuple(outs) if many else outs[0], in_spe...  4.88 us
    pallas_call x1, Pallas kernels, backward(): pl.pallas_call(backward_kernel, out_shape=(shape(*LINE, dtype=F32),) * 3...  2.72 us
    ppermute x1, starting transfers between devices, body(): other = lax.ppermute(cotangent, 'head', swap)  2.55 us
  transfers between devices with their start and end apart: 4, of which 2 were waited for; matrix products, arithmetic and copies ran while one was open for 0% of the time, Pallas kernels for 6%

profile of v6, /device:TPU:1, one launch (start us, length us, event | category | flops | bytes accessed | tf_op | source)
XLA Modules:
  0.0 104.6 jit_solution(17133192141349810186)
XLA Ops:
  0.6 2.6 %collective-permute-start = (bf16[192,1024]{1,0:T(8,128)(2,1)}, bf16[192,1024]{1,0:T(8,128)(2,1)S(1)}, u32[]{:S(2)}, u32[]{:S(2)}) collective-permute-start(bf16[192,1024]{1,0:T(8,128)(2,1)} %bitcast.27), channel_id=1, source_target_pairs={{0,1},{1,0},{2,3},{3,2},{4,5},{5,4},{6,7},{7,6},{8,9},{9,8},{10,11... | collective-permute-start | bytes 1179656 | tf_op jit(solution)/shard_map/ppermute | solution.py:454
  3.2 2.0 %pack_lines.1 = bf16[2304,128]{1,0:T(8,128)(2,1)} custom-call(bf16[3,128,256]{2,1,0:T(8,128)(2,1)} %bitcast.17, bf16[3,128,256]{2,1,0:T(8,128)(2,1)} %bitcast.20, bf16[3,128,256]{2,1,0:T(8,128)(2,1)} %bitcast.23), custom_call_target="tpu_custom_call" | custom-call | tf_op jit(solution)/shard_map/pack_lines/pallas_call | solution.py:432
  5.2 0.0 copy-start.5
  5.2 0.0 copy-start
  5.2 0.0 copy-start.1
  5.2 0.0 copy-start.2
  5.2 0.0 copy-start.3
  5.2 15.1 %all-to-all-start = ((bf16[128,9,2,128]{3,2,1,0:T(2,128)(2,1)}), bf16[128,9,2,128]{3,2,1,0:T(2,128)(2,1)S(1)}, u32[]{:S(2)}, u32[]{:S(2)}) async-start(bf16[128,9,2,128]{3,2,1,0:T(2,128)(2,1)} %bitcast.29), calls=%async_computation | async-start | bytes 1179648 | tf_op jit(solution)/shard_map/all_to_all | solution.py:360
  20.3 0.0 copy-done.5
  20.4 0.1 copy.10.axes_ref
  20.5 0.0 collective-permute-done.other_ref
  20.5 0.0 copy-done.4
  20.5 0.9 own.1
  21.4 21.1 %all-to-all-done = bf16[128,9,2,128]{3,2,1,0:T(2,128)(2,1)S(1)} async-done(((bf16[128,9,2,128]{3,2,1,0:T(2,128)(2,1)}), bf16[128,9,2,128]{3,2,1,0:T(2,128)(2,1)S(1)}, u32[]{:S(2)}, u32[]{:S(2)}) %all-to-all-start) | async-done | bytes 589856 | tf_op jit(solution)/shard_map/all_to_all | solution.py:360
  42.5 1.8 %forward.1 = (bf16[1792,128]{1,0:T(8,128)(2,1)S(1)}, bf16[6,128,256]{2,1,0:T(8,128)(2,1)S(1)}, bf16[6,128,256]{2,1,0:T(8,128)(2,1)S(1)}, bf16[6,128,256]{2,1,0:T...) custom-call(s32[3,2]{1,0:T(4,128)S(1)} %copy.10.axes_ref, ...), custom_call_target="tpu_custom_call" | custom-call | tf_op jit(solution)/shard_map/forward/pallas_call | solution.py:375
  44.4 25.5 %all_to_all.15 = bf16[128,7,2,128]{3,2,1,0:T(2,128)(2,1)S(1)} all-to-all(bf16[128,7,2,128]{3,2,1,0:T(2,128)(2,1)S(1)} %bitcast.26), channel_id=1, replica_groups=mesh['band'=128,'head'=2] {'band'}, dimensions={0} | all-to-all | bytes 917504 | tf_op jit(solution)/shard_map/all_to_all | solution.py:360
  69.8 1.1 %merge.1 = (bf16[3,128,256]{2,1,0:T(8,128)(2,1)S(1)}, f32[6,2,1,256]{3,2,1,0:T(1,128)S(1)}, f32[6,2,1,256]{3,2,1,0:T(1,128)S(1)}, bf16[192,1024]{1,0:T(8,128)(2,1)S(1)}, bf16[192,256]{1,0:T(8,128)(2,1)S(1)}) custom-call(bf16[3,128,256]{2,1,0:T(8,128)(2,1)S(1)} %get-tuple-element.27.ga_ref, f32[3,128,256]{2,1,0:T(8,128)S(1)} %get-tuple-element.31.near_ref, ...), custom_call_target="tpu_custom_call" | custom-call | tf_op jit(solution)/shard_map/merge/pallas_call | solution.py:375
  70.9 0.1 collective-permute-start.1
  71.0 2.7 %backward.1 = (f32[3,128,256]{2,1,0:T(8,128)S(1)}, f32[3,128,256]{2,1,0:T(8,128)S(1)}, f32[3,128,256]{2,1,0:T(8,128)S(1)}, bf16[2304,128]{1,0:T(8,128)(2,1)}) custom-call(s32[3,2]{1,0:T(4,128)S(1)} %copy.10.axes_ref, bf16[6,128,256]{2,1,0:T(8,128)(2,1)S(1)} %get-tuple-element.37.q6, bf16[6,128,256]{2,1,0:T(8,128)(2,1)S(1)} %get-tuple-element.38.k6, ...), custom_call_target="tpu_custom_call" | custom-call | tf_op jit(solution)/shard_map/backward/pallas_call | solution.py:408
  73.8 7.9 %all-to-all-start.2 = ((bf16[128,9,2,128]{3,2,1,0:T(2,128)(2,1)}), bf16[128,9,2,128]{3,2,1,0:T(2,128)(2,1)S(1)}, u32[]{:S(2)}, u32[]{:S(2)}) async-start(bf16[128,9,2,128]{3,2,1,0:T(2,128)(2,1)} %bitcast.9), calls=%async_computation.2 | async-start | bytes 1179648 | tf_op jit(solution)/shard_map/all_to_all | solution.py:360
  81.7 0.0 collective-permute-done.1.got_ref
  81.7 1.0 layer.1
  82.7 21.0 %all-to-all-done.2 = bf16[128,9,2,128]{3,2,1,0:T(2,128)(2,1)S(1)} async-done(((bf16[128,9,2,128]{3,2,1,0:T(2,128)(2,1)}), bf16[128,9,2,128]{3,2,1,0:T(2,128)(2,1)S(1)}, u32[]{:S(2)}, u32[]{:S(2)}) %all-to-all-start.2) | async-done | bytes 589856 | tf_op jit(solution)/shard_map/all_to_all | solution.py:360
  103.7 1.0 finish.1
  (5 shorter events, 0.0 us)
Async XLA Ops:
  0.6 19.8 %collective-permute-start = (bf16[192,1024]{1,0:T(8,128)(2,1)}, bf16[192,1024]{1,0:T(8,128)(2,1)S(1)}, u32[]{:S(2)}, u32[]{:S(2)}) collective-permute-start(bf16[192,1024]{1,0:T(8,128)(2,1)} %bitcast.27), channel_id=1, source_target_pairs={{0,1},{1,0},{2,3},{3,2},{4,5},{5,4},{6,7},{7,6},{8,9},{9,8},{10,11... | collective-permute-start | bytes 1179656 | tf_op jit(solution)/shard_map/ppermute | solution.py:454
  3.2 17.3 %copy-start.4 = (bf16[1,3,64,1024]{3,2,1,0:T(8,128)(2,1)S(1)}, bf16[1,3,64,1024]{3,2,1,0:T(8,128)(2,1)}, u32[]{:S(2)}) copy-start(bf16[1,3,64,1024]{3,2,1,0:T(8,128)(2,1)} %param.10) | copy-start | bytes 1179652
  5.2 15.2 %copy-start.5 = (s32[3,2]{0,1:T(2,128)S(1)}, s32[3,2]{0,1:T(2,128)}, u32[]{:S(2)}) copy-start(s32[3,2]{0,1:T(2,128)} %param.11) | copy-start | bytes 76
  5.2 15.3 %copy-start = (bf16[1,3,128,256]{3,2,1,0:T(8,128)(2,1)S(1)}, bf16[1,3,128,256]{3,2,1,0:T(8,128)(2,1)}, u32[]{:S(2)}) copy-start(bf16[1,3,128,256]{3,2,1,0:T(8,128)(2,1)} %param.6) | copy-start | bytes 589828
  5.2 15.3 %copy-start.1 = (bf16[1,3,128,256]{3,2,1,0:T(8,128)(2,1)S(1)}, bf16[1,3,128,256]{3,2,1,0:T(8,128)(2,1)}, u32[]{:S(2)}) copy-start(bf16[1,3,128,256]{3,2,1,0:T(8,128)(2,1)} %param.7) | copy-start | bytes 589828
  5.2 15.2 %copy-start.2 = (bf16[1,3,128,256]{3,2,1,0:T(8,128)(2,1)S(1)}, bf16[1,3,128,256]{3,2,1,0:T(8,128)(2,1)}, u32[]{:S(2)}) copy-start(bf16[1,3,128,256]{3,2,1,0:T(8,128)(2,1)} %param.8) | copy-start | bytes 589828
  5.2 15.2 %copy-start.3 = (bf16[256,1024]{1,0:T(8,128)(2,1)S(1)}, bf16[256,1024]{1,0:T(8,128)(2,1)}, u32[]{:S(2)}) copy-start(bf16[256,1024]{1,0:T(8,128)(2,1)} %proj_ref.5) | copy-start | bytes 1572868
  5.2 37.3 %all-to-all-start = ((bf16[128,9,2,128]{3,2,1,0:T(2,128)(2,1)}), bf16[128,9,2,128]{3,2,1,0:T(2,128)(2,1)S(1)}, u32[]{:S(2)}, u32[]{:S(2)}) async-start(bf16[128,9,2,128]{3,2,1,0:T(2,128)(2,1)} %bitcast.29), calls=%async_computation | async-start | bytes 1179648 | tf_op jit(solution)/shard_map/all_to_all | solution.py:360
  70.9 10.7 %collective-permute-start.1 = (bf16[192,1024]{1,0:T(8,128)(2,1)S(1)}, bf16[192,1024]{1,0:T(8,128)(2,1)S(1)}, u32[]{:S(2)}, u32[]{:S(2)}) collective-permute-start(bf16[192,1024]{1,0:T(8,128)(2,1)S(1)} %get-tuple-element.36), channel_id=1, source_target_pairs={{0,1},{1,0},{2,3},{3,2},{4,5},{5,4},{6,7},{7,6},{8,9},{9,8},{10,11... | collective-permute-start | bytes 1179656 | tf_op jit(solution)/shard_map/ppermute | solution.py:463
  73.8 29.9 %all-to-all-start.2 = ((bf16[128,9,2,128]{3,2,1,0:T(2,128)(2,1)}), bf16[128,9,2,128]{3,2,1,0:T(2,128)(2,1)S(1)}, u32[]{:S(2)}, u32[]{:S(2)}) async-start(bf16[128,9,2,128]{3,2,1,0:T(2,128)(2,1)} %bitcast.9), calls=%async_computation.2 | async-start | bytes 1179648 | tf_op jit(solution)/shard_map/all_to_all | solution.py:360

commit v7 on v6

--- a/solution.py
+++ b/solution.py
@@ -215,17 +215,28 @@
     return log_all, jnp.exp(near - log_all), jnp.exp(far - log_all)
 
 
-def merge_kernel(
-    ga_ref, near_ref, far_ref, totals_ref, proj_ref, got_ref,
-    ga_col_ref, log_all_ref, delta_ref, given_ref, kept_ref,
-    stage, parts, att,
+def score(queries, grads, keys, values, log_all, delta):
+    prob = jnp.exp(nt(keys, queries) - log_all)
+    return (prob * (nt(values, grads) - delta)).astype(BF), prob.astype(BF)
+
+
+def multiply(queries, grads, keys, step, prob):
+    return tn(tall(step), keys), nn(step, queries), nn(prob, grads)
+
+
+def backward_kernel(
+    axes_ref, q6, k6, v6, ga_ref, near_ref, far_ref, totals_ref, proj_ref, got_ref,
+    dq_ref, dk_ref, dv_ref, send_ref, given_ref, kept_ref, log_row_ref, delta_row_ref,
+    mixed, parts, att, log_all, delta, stage, ga6, dq6, probs, steps, packed, kept, sem, kept_sem,
 ):
-    stage[...] = got_ref[...].astype(F32)
-    parts[...] = jnp.transpose(stage[pl.ds(12, N, stride=MIXED), :])
+    masks = lane_masks()
+    mixed[...] = got_ref[...].astype(F32)
+    parts[...] = jnp.transpose(mixed[pl.ds(12, N, stride=MIXED), :])
     arrived = parts[0:40, :] + (parts[40:80, :] + parts[80:120, :])
     for p in range(3):
-        for g in range(2):
-            ga_col_ref[p, :, N * g : N * g + N] = stage[
+        ga6[p] = ga_ref[p]
+        for g in range(2):
+            ga6[3 + p, :, N * g : N * g + N] = mixed[
                 pl.ds(6 + 2 * p + g, N, stride=MIXED), :
             ].astype(BF)
     row_log, row_near, row_far = both_weights(totals_ref[0:12, :], arrived[24:36])
@@ -234,79 +245,43 @@
     col_delta = col_near * arrived[12:24]
     for p in range(3):
         far_row = jnp.concatenate(
-            [stage[pl.ds(2 * p + g, N, stride=MIXED), :] for g in range(2)], axis=1
+            [mixed[pl.ds(2 * p + g, N, stride=MIXED), :] for g in range(2)], axis=1
         )
         heads = slice(4 * p, 4 * p + 4)
         row_sums = head_sums(ga_ref[p].astype(F32) * far_row)[:4]
-        col_sums = head_sums(ga_col_ref[p].astype(F32) * far_ref[p].astype(F32))[:4]
+        col_sums = head_sums(ga6[3 + p].astype(F32) * far_ref[p].astype(F32))[:4]
         row = row_delta[heads] + row_far[heads] * row_sums
         col = col_delta[heads] + col_far[heads] * col_sums
         for g in range(2):
-            log_all_ref[p, g] = wide(row_log, 4 * p + 2 * g)
-            log_all_ref[3 + p, g] = wide(col_log, 4 * p + 2 * g)
-            delta_ref[p, g] = wide(row, 2 * g)
-            delta_ref[3 + p, g] = wide(col, 2 * g)
+            log_all[p, g] = wide(row_log, 4 * p + 2 * g)
+            log_all[3 + p, g] = wide(col_log, 4 * p + 2 * g)
+            delta[p, g] = wide(row, 2 * g)
+            delta[3 + p, g] = wide(col, 2 * g)
     parts[0:12, :] = row_near
     parts[12:24, :] = row_far
-    weights = jnp.transpose(parts[...])
-    for p in range(3):
-        for g in range(2):
-            r = 4 * p + 2 * g
-            att[p, :, N * g : N * g + N] = (
-                spread(weights, r) * near_ref[p, :, N * g : N * g + N]
-                + spread(weights, 12 + r) * stage[pl.ds(2 * p + g, N, stride=MIXED), :]
-            ).astype(BF)
-    me = lax.axis_index("head")
-    theirs = pl.ds(pl.multiple_of((1 - me) * HALF, HALF), HALF)
-    mine = pl.ds(pl.multiple_of(me * HALF, HALF), HALF)
-    for p in range(3):
-        rows = slice(HALF * p, HALF * p + HALF)
-        kept_ref[rows, :] = att[p, mine, :]
-        given_ref[rows, :] = nn(att[p, theirs, :], proj_ref[...]).astype(BF)
-
-
-def layer_kernel(kept_ref, proj_ref, got_ref, out_ref):
-    out_ref[...] = (nn(kept_ref[...], proj_ref[...]) + got_ref[...].astype(F32)).astype(BF)
-
-
-def backward_kernel(
-    axes_ref, q6, k6, v6, ga_ref, ga_col_ref, log_all_ref, delta_ref,
-    dq_ref, dk_ref, dv_ref, send_ref,
-    stage, ga6, dq6, probs, steps, packed, sem,
-):
-    masks = lane_masks()
-
-    def operands(b, g):
-        lanes = slice(N * g, N * g + N)
-        return stack(q6[b, :, lanes] * BF(FACTOR), masks), stack(ga6[b, :, lanes], masks)
-
-    for p in range(3):
-        ga6[p] = ga_ref[p]
-        ga6[p + 3] = ga_col_ref[p]
-
-    def score(units):
-        for g in range(2):
-            lanes = slice(N * g, N * g + N)
-            for u, b, c in units:
-                queries, grads = operands(b, g)
-                prob = jnp.exp(nt(k6[c, :, lanes], queries) - log_all_ref[b, g])
-                dots = nt(v6[c, :, lanes], grads)
-                probs[2 * u + g] = prob.astype(BF)
-                steps[2 * u + g] = (prob * (dots - delta_ref[b, g])).astype(BF)
-
-    def multiply(g, u, b, c):
-        queries, grads = operands(b, g)
-        step = steps[2 * u + g]
-        dq = tn(tall(step), stack(k6[c, :, N * g : N * g + N], masks))
-        return dq, nn(step, queries), nn(probs[2 * u + g], grads)
-
-    cross = [(c, b, c) for c, b in enumerate(partners(axes_ref))]
-    same = [(c, c, c) for c in range(3)]
-    score(cross)
+
+    cross = list(enumerate(partners(axes_ref)))
     for g in range(2):
         lanes = slice(N * g, N * g + N)
-        for u, b, c in cross:
-            dq, dk, dv = multiply(g, u, b, c)
+        for c, b in cross:
+            steps[2 * c + g], probs[2 * c + g] = score(
+                stack(q6[b, :, lanes] * BF(FACTOR), masks),
+                stack(ga6[b, :, lanes], masks),
+                k6[c, :, lanes],
+                v6[c, :, lanes],
+                log_all[b, g],
+                delta[b, g],
+            )
+    for g in range(2):
+        lanes = slice(N * g, N * g + N)
+        for c, b in cross:
+            dq, dk, dv = multiply(
+                stack(q6[b, :, lanes] * BF(FACTOR), masks),
+                stack(ga6[b, :, lanes], masks),
+                stack(k6[c, :, lanes], masks),
+                steps[2 * c + g],
+                probs[2 * c + g],
+            )
             dq6[b, :, lanes] = dq
             if c < 3:
                 dk_ref[c, :, lanes] = dk
@@ -321,15 +296,62 @@
     packed[...] = stage[...].astype(BF)
     leaving = pltpu.make_async_copy(packed, send_ref, sem)
     leaving.start()
-    score(same)
-    for g in range(2):
-        lanes = slice(N * g, N * g + N)
-        for u, b, c in same:
-            dq, dk, dv = multiply(g, u, b, c)
-            dq_ref[c, :, lanes] = (dq6[c, :, lanes] + dq) * FACTOR
-            dk_ref[c, :, lanes] += dk
-            dv_ref[c, :, lanes] += dv
+
+    weights = jnp.transpose(parts[...])
+    for p in range(3):
+        dq_ref[p] = dq6[p]
+        log_row_ref[p] = log_all[p]
+        delta_row_ref[p] = delta[p]
+        for g in range(2):
+            r = 4 * p + 2 * g
+            att[p, :, N * g : N * g + N] = (
+                spread(weights, r) * near_ref[p, :, N * g : N * g + N]
+                + spread(weights, 12 + r) * mixed[pl.ds(2 * p + g, N, stride=MIXED), :]
+            ).astype(BF)
+    me = lax.axis_index("head")
+    theirs = pl.ds(pl.multiple_of((1 - me) * HALF, HALF), HALF)
+    mine = pl.ds(pl.multiple_of(me * HALF, HALF), HALF)
+    for p in range(3):
+        kept[HALF * p : HALF * p + HALF, :] = att[p, mine, :]
+    keeping = pltpu.make_async_copy(kept, kept_ref, kept_sem)
+    keeping.start()
+    for p in range(3):
+        given_ref[HALF * p : HALF * p + HALF, :] = nn(att[p, theirs, :], proj_ref[...]).astype(BF)
+    keeping.wait()
     leaving.wait()
+
+
+def rows_kernel(
+    q_ref, k_ref, v_ref, ga_ref, log_row_ref, delta_row_ref, dq_in, dk_in, dv_in,
+    dq_ref, dk_ref, dv_ref,
+    probs, steps,
+):
+    masks = lane_masks()
+    units = [(p, g, slice(N * g, N * g + N)) for p in range(3) for g in range(2)]
+    for p, g, lanes in units:
+        steps[2 * p + g], probs[2 * p + g] = score(
+            stack(q_ref[p, :, lanes] * BF(FACTOR), masks),
+            stack(ga_ref[p, :, lanes], masks),
+            k_ref[p, :, lanes],
+            v_ref[p, :, lanes],
+            log_row_ref[p, g],
+            delta_row_ref[p, g],
+        )
+    for p, g, lanes in units:
+        dq, dk, dv = multiply(
+            stack(q_ref[p, :, lanes] * BF(FACTOR), masks),
+            stack(ga_ref[p, :, lanes], masks),
+            stack(k_ref[p, :, lanes], masks),
+            steps[2 * p + g],
+            probs[2 * p + g],
+        )
+        dq_ref[p, :, lanes] = (dq_in[p, :, lanes] + dq) * FACTOR
+        dk_ref[p, :, lanes] = dk_in[p, :, lanes] + dk
+        dv_ref[p, :, lanes] = dv_in[p, :, lanes] + dv
+
+
+def layer_kernel(kept_ref, proj_ref, got_ref, out_ref):
+    out_ref[...] = (nn(kept_ref[...], proj_ref[...]) + got_ref[...].astype(F32)).astype(BF)
 
 
 def finish_kernel(dq_ref, dk_ref, dv_ref, got_ref, q_out, k_out, v_out, stage, made, sems):
@@ -395,24 +417,37 @@
     return call(forward_kernel, ins, outs, [STAGE, SQUARE, pltpu.VMEM((3, *ROW), F32), pltpu.VMEM((12, N, 256), BF)], "forward")
 
 
-def merge(*ins):
-    rows = shape(6, 2, 1, 256, dtype=F32)
-    outs = [shape(*LINE), rows, rows, shape(*TOKENS), shape(3 * HALF, 256)]
-    scratch = [pltpu.VMEM((MIXED * N, N), F32), SQUARE, pltpu.VMEM(LINE, BF)]
-    return call(merge_kernel, ins, outs, scratch, "merge")
-
-
 def backward(*ins):
-    scratch = [STAGE, pltpu.VMEM((6, N, 256), BF), pltpu.VMEM((6, N, 256), F32)]
-    scratch += [pltpu.VMEM((12, N, 256), BF)] * 2 + [PACKED, pltpu.SemaphoreType.DMA]
+    row = shape(*ROW, dtype=F32)
+    outs = (shape(*LINE, dtype=F32),) * 3 + (shape(SENT * N, N), shape(*TOKENS), pltpu.HBM((3 * HALF, 256), BF))
+    places = (VMEM, VMEM, VMEM, HBM, VMEM, HBM, VMEM, VMEM)
+    six_rows = pltpu.VMEM((6, 2, 1, 256), F32)
+    pairs = pltpu.VMEM((12, N, 256), BF)
+    scratch = [pltpu.VMEM((MIXED * N, N), F32), SQUARE, pltpu.VMEM(LINE, BF), six_rows, six_rows, STAGE]
+    scratch += [pltpu.VMEM((6, N, 256), BF), pltpu.VMEM((6, N, 256), F32), pairs, pairs, PACKED]
     return pl.pallas_call(
         backward_kernel,
-        out_shape=(shape(*LINE, dtype=F32),) * 3 + (shape(SENT * N, N),),
+        out_shape=outs + (row, row),
         in_specs=[VMEM] * len(ins),
-        out_specs=(VMEM, VMEM, VMEM, HBM),
-        scratch_shapes=scratch,
+        out_specs=places,
+        scratch_shapes=scratch + [pltpu.VMEM((3 * HALF, 256), BF)] + [pltpu.SemaphoreType.DMA] * 2,
         compiler_params=PARAMS,
         name="backward",
+    )(*ins)
+
+
+def own_rows(*ins):
+    pairs = pltpu.VMEM((6, N, 256), BF)
+    return pl.pallas_call(
+        rows_kernel,
+        out_shape=(shape(*LINE, dtype=F32),) * 3,
+        in_specs=[VMEM] * len(ins),
+        out_specs=(VMEM,) * 3,
+        scratch_shapes=[pairs, pairs],
+        input_output_aliases={6: 0, 7: 1, 8: 2},
+        compiler_params=PARAMS,
+        cost_estimate=cost(10**8, 10**5),
+        name="own_rows",
     )(*ins)
 
 
@@ -459,12 +494,12 @@
         plane_axes, q, k, v, ga, top, total, own_out, lines
     )
     mixed = exchange(sent, MIXED)
-    ga_columns, log_all, delta, given, kept = merge(ga, near_out, far_out, totals, out_proj, mixed)
+    dq, dk, dv, sent, given, kept, log_rows, delta_rows = backward(
+        plane_axes, q6, k6, v6, ga, near_out, far_out, totals, out_proj, mixed
+    )
     arrived = lax.ppermute(given, "head", swap)
-    dq, dk, dv, sent = backward(
-        plane_axes, q6, k6, v6, ga, ga_columns, log_all, delta
-    )
     returned = exchange(sent, SENT)
+    dq, dk, dv = own_rows(q, k, v, ga, log_rows, delta_rows, dq, dk, dv)
     layer = call(
         layer_kernel, (kept, out_proj, arrived), [shape(*TOKENS)], [], "layer", estimate=cost(LONG, 1500000)
     )

time: 105 us -> 104 us (level)
  waiting for transfers between devices: 42.1 us -> 40.2 us
    all_to_all x2, waiting for transfers between devices: 42.1 us -> 39.7 us  [exchange(): got = lax.all_to_all(sent, 'band', split_axis=0, concat_axis=0, tiled=True)]
    pallas_call x1 -> x2, Pallas kernels: 2.72 us -> 3.5 us  [the longest x1 2.65 us: backward(): pl.pallas_call(backward_kernel, out_shape=outs + (row, row), in_specs=[VM...]
    pallas_call x4 -> x3, Pallas kernels: 4.88 us -> 4.77 us  [call(): pl.pallas_call(kernel, out_shape=tuple(outs) if many else outs[0], in_spe...]
  transfers between devices with their start and end apart: 4 -> 4, of which waited for: 2 -> 3; matrix products, arithmetic and copies ran while one was open for 0% -> 0% of each run, Pallas kernels for 6% -> 6%
where the time goes in v7:
time: 104 us; the launch traced here: 103 us
  waiting for transfers between devices  40.2 us (39%)
  starting transfers between devices  25.6 us (25%)
  blocking collectives  25.5 us (25%)
  Pallas kernels  11.2 us (11%)
    all_to_all x2, waiting for transfers between devices, exchange(): got = lax.all_to_all(sent, 'band', split_axis=0, concat_axis=0, tiled=True)  39.7 us
    all_to_all x1, blocking collectives, exchange(): got = lax.all_to_all(sent, 'band', split_axis=0, concat_axis=0, tiled=True)  25.5 us
    all_to_all x2, starting transfers between devices, exchange(): got = lax.all_to_all(sent, 'band', split_axis=0, concat_axis=0, tiled=True)  23 us
    pallas_call x3, Pallas kernels, call(): pl.pallas_call(kernel, out_shape=tuple(outs) if many else outs[0], in_spe...  4.77 us
    pallas_call x1, Pallas kernels, backward(): pl.pallas_call(backward_kernel, out_shape=outs + (row, row), in_specs=[VM...  2.65 us
    ppermute x1, starting transfers between devices, body(): other = lax.ppermute(cotangent, 'head', swap)  2.55 us
  transfers between devices with their start and end apart: 4, of which 3 were waited for; matrix products, arithmetic and copies ran while one was open for 0% of the time, Pallas kernels for 6%

profile of v7, /device:TPU:1, one launch (start us, length us, event | category | flops | bytes accessed | tf_op | source)
XLA Modules:
  0.0 103.5 jit_solution(14595079435781285492)
XLA Ops:
  0.6 2.6 %collective-permute-start = (bf16[192,1024]{1,0:T(8,128)(2,1)}, bf16[192,1024]{1,0:T(8,128)(2,1)S(1)}, u32[]{:S(2)}, u32[]{:S(2)}) collective-permute-start(bf16[192,1024]{1,0:T(8,128)(2,1)} %bitcast.30), channel_id=1, source_target_pairs={{0,1},{1,0},{2,3},{3,2},{4,5},{5,4},{6,7},{7,6},{8,9},{9,8},{10,11... | collective-permute-start | bytes 1179656 | tf_op jit(solution)/shard_map/ppermute | solution.py:489
  3.2 2.0 %pack_lines.1 = bf16[2304,128]{1,0:T(8,128)(2,1)} custom-call(bf16[3,128,256]{2,1,0:T(8,128)(2,1)} %bitcast.17, bf16[3,128,256]{2,1,0:T(8,128)(2,1)} %bitcast.21, bf16[3,128,256]{2,1,0:T(8,128)(2,1)} %bitcast.25), custom_call_target="tpu_custom_call" | custom-call | tf_op jit(solution)/shard_map/pack_lines/pallas_call | solution.py:467
  5.2 0.0 copy-start.6
  5.2 0.0 copy-start
  5.2 0.0 copy-start.1
  5.2 0.0 copy-start.2
  5.2 0.0 copy-start.3
  5.3 15.1 %all-to-all-start = ((bf16[128,9,2,128]{3,2,1,0:T(2,128)(2,1)}), bf16[128,9,2,128]{3,2,1,0:T(2,128)(2,1)S(1)}, u32[]{:S(2)}, u32[]{:S(2)}) async-start(bf16[128,9,2,128]{3,2,1,0:T(2,128)(2,1)} %bitcast.32), calls=%async_computation | async-start | bytes 1179648 | tf_op jit(solution)/shard_map/all_to_all | solution.py:382
  20.4 0.0 copy-done.6
  20.4 0.1 copy.14.axes_ref
  20.5 0.0 collective-permute-done.other_ref
  20.5 0.9 own.1
  21.4 21.1 %all-to-all-done = bf16[128,9,2,128]{3,2,1,0:T(2,128)(2,1)S(1)} async-done(((bf16[128,9,2,128]{3,2,1,0:T(2,128)(2,1)}), bf16[128,9,2,128]{3,2,1,0:T(2,128)(2,1)S(1)}, u32[]{:S(2)}, u32[]{:S(2)}) %all-to-all-start) | async-done | bytes 589856 | tf_op jit(solution)/shard_map/all_to_all | solution.py:382
  42.6 1.8 %forward.1 = (bf16[1792,128]{1,0:T(8,128)(2,1)S(1)}, bf16[6,128,256]{2,1,0:T(8,128)(2,1)S(1)}, bf16[6,128,256]{2,1,0:T(8,128)(2,1)S(1)}, bf16[6,128,256]{2,1,0:T...) custom-call(s32[3,2]{1,0:T(4,128)S(1)} %copy.14.axes_ref, ...), custom_call_target="tpu_custom_call" | custom-call | tf_op jit(solution)/shard_map/forward/pallas_call | solution.py:397
  44.4 25.5 %all_to_all.15 = bf16[128,7,2,128]{3,2,1,0:T(2,128)(2,1)S(1)} all-to-all(bf16[128,7,2,128]{3,2,1,0:T(2,128)(2,1)S(1)} %bitcast.29), channel_id=1, replica_groups=mesh['band'=128,'head'=2] {'band'}, dimensions={0} | all-to-all | bytes 917504 | tf_op jit(solution)/shard_map/all_to_all | solution.py:382
  69.8 2.7 %backward.1 = (f32[3,128,256]{2,1,0:T(8,128)S(1)}, f32[3,128,256]{2,1,0:T(8,128)S(1)}, f32[3,128,256]{2,1,0:T(8,128)S(1)}, bf16[2304,128]{1,0:T(8,128)(2,1)}, bf...) custom-call(s32[3,2]{1,0:T(4,128)S(1)} %copy.14.axes_ref, ...), custom_call_target="tpu_custom_call" | custom-call | tf_op jit(solution)/shard_map/backward/pallas_call | solution.py:428
  72.5 0.1 collective-permute-start.1
  72.6 7.9 %all-to-all-start.2 = ((bf16[128,9,2,128]{3,2,1,0:T(2,128)(2,1)}), bf16[128,9,2,128]{3,2,1,0:T(2,128)(2,1)S(1)}, u32[]{:S(2)}, u32[]{:S(2)}) async-start(bf16[128,9,2,128]{3,2,1,0:T(2,128)(2,1)} %bitcast.9), calls=%async_computation.2 | async-start | bytes 1179648 | tf_op jit(solution)/shard_map/all_to_all | solution.py:382
  80.5 0.0 copy-start.5
  80.5 0.9 own_rows.1
  81.4 0.5 collective-permute-done.1.got_ref
  81.9 2.0 %layer.1 = bf16[192,1024]{1,0:T(8,128)(2,1)} custom-call(bf16[192,256]{1,0:T(8,128)(2,1)S(1)} %copy-done.5, bf16[256,1024]{1,0:T(8,128)(2,1)S(1)} %copy-done.3, bf16[192,1024]{1,0:T(8,128)(2,1)} %collective-permute-done.1.got_ref), custom_call_target="tpu_custom_call" | custom-call | flops 60000002048 | bytes 1500000 | tf_op jit(solution)/shard_map/layer/pallas_call | solution.py:397
  83.9 18.6 %all-to-all-done.2 = bf16[128,9,2,128]{3,2,1,0:T(2,128)(2,1)S(1)} async-done(((bf16[128,9,2,128]{3,2,1,0:T(2,128)(2,1)}), bf16[128,9,2,128]{3,2,1,0:T(2,128)(2,1)S(1)}, u32[]{:S(2)}, u32[]{:S(2)}) %all-to-all-start.2) | async-done | bytes 589856 | tf_op jit(solution)/shard_map/all_to_all | solution.py:382
  102.5 1.0 finish.1
  (7 shorter events, 0.0 us)
Async XLA Ops:
  0.6 19.8 %collective-permute-start = (bf16[192,1024]{1,0:T(8,128)(2,1)}, bf16[192,1024]{1,0:T(8,128)(2,1)S(1)}, u32[]{:S(2)}, u32[]{:S(2)}) collective-permute-start(bf16[192,1024]{1,0:T(8,128)(2,1)} %bitcast.30), channel_id=1, source_target_pairs={{0,1},{1,0},{2,3},{3,2},{4,5},{5,4},{6,7},{7,6},{8,9},{9,8},{10,11... | collective-permute-start | bytes 1179656 | tf_op jit(solution)/shard_map/ppermute | solution.py:489
  3.2 17.3 %copy-start.4 = (bf16[1,3,64,1024]{3,2,1,0:T(8,128)(2,1)S(1)}, bf16[1,3,64,1024]{3,2,1,0:T(8,128)(2,1)}, u32[]{:S(2)}) copy-start(bf16[1,3,64,1024]{3,2,1,0:T(8,128)(2,1)} %param.10) | copy-start | bytes 1179652
  5.2 15.2 %copy-start.6 = (s32[3,2]{0,1:T(2,128)S(1)}, s32[3,2]{0,1:T(2,128)}, u32[]{:S(2)}) copy-start(s32[3,2]{0,1:T(2,128)} %param.11) | copy-start | bytes 76
  5.2 15.3 %copy-start = (bf16[1,3,128,256]{3,2,1,0:T(8,128)(2,1)S(1)}, bf16[1,3,128,256]{3,2,1,0:T(8,128)(2,1)}, u32[]{:S(2)}) copy-start(bf16[1,3,128,256]{3,2,1,0:T(8,128)(2,1)} %param.6) | copy-start | bytes 589828
  5.2 15.3 %copy-start.1 = (bf16[1,3,128,256]{3,2,1,0:T(8,128)(2,1)S(1)}, bf16[1,3,128,256]{3,2,1,0:T(8,128)(2,1)}, u32[]{:S(2)}) copy-start(bf16[1,3,128,256]{3,2,1,0:T(8,128)(2,1)} %param.7) | copy-start | bytes 589828
  5.2 15.2 %copy-start.2 = (bf16[1,3,128,256]{3,2,1,0:T(8,128)(2,1)S(1)}, bf16[1,3,128,256]{3,2,1,0:T(8,128)(2,1)}, u32[]{:S(2)}) copy-start(bf16[1,3,128,256]{3,2,1,0:T(8,128)(2,1)} %param.8) | copy-start | bytes 589828
  5.2 15.2 %copy-start.3 = (bf16[256,1024]{1,0:T(8,128)(2,1)S(1)}, bf16[256,1024]{1,0:T(8,128)(2,1)}, u32[]{:S(2)}) copy-start(bf16[256,1024]{1,0:T(8,128)(2,1)} %proj_ref.5) | copy-start | bytes 1572868
  5.3 37.3 %all-to-all-start = ((bf16[128,9,2,128]{3,2,1,0:T(2,128)(2,1)}), bf16[128,9,2,128]{3,2,1,0:T(2,128)(2,1)S(1)}, u32[]{:S(2)}, u32[]{:S(2)}) async-start(bf16[128,9,2,128]{3,2,1,0:T(2,128)(2,1)} %bitcast.32), calls=%async_computation | async-start | bytes 1179648 | tf_op jit(solution)/shard_map/all_to_all | solution.py:382
  72.5 9.4 %collective-permute-start.1 = (bf16[192,1024]{1,0:T(8,128)(2,1)S(1)}, bf16[192,1024]{1,0:T(8,128)(2,1)}, u32[]{:S(2)}, u32[]{:S(2)}) collective-permute-start(bf16[192,1024]{1,0:T(8,128)(2,1)S(1)} %get-tuple-element.41), channel_id=1, source_target_pairs={{0,1},{1,0},{2,3},{3,2},{4,5},{5,4},{6,7},{7,6},{8,9},{9,8},{10,11... | collective-permute-start | bytes 1179656 | tf_op jit(solution)/shard_map/ppermute | solution.py:500
  72.6 29.9 %all-to-all-start.2 = ((bf16[128,9,2,128]{3,2,1,0:T(2,128)(2,1)}), bf16[128,9,2,128]{3,2,1,0:T(2,128)(2,1)S(1)}, u32[]{:S(2)}, u32[]{:S(2)}) async-start(bf16[128,9,2,128]{3,2,1,0:T(2,128)(2,1)} %bitcast.9), calls=%async_computation.2 | async-start | bytes 1179648 | tf_op jit(solution)/shard_map/all_to_all | solution.py:382
  80.5 1.4 %copy-start.5 = (bf16[192,256]{1,0:T(8,128)(2,1)S(1)}, bf16[192,256]{1,0:T(8,128)(2,1)}, u32[]{:S(2)}) copy-start(bf16[192,256]{1,0:T(8,128)(2,1)} %get-tuple-element.40.kept_ref) | copy-start | bytes 294916

commit v8 on v7

--- a/solution.py
+++ b/solution.py
@@ -272,6 +272,23 @@
                 log_all[b, g],
                 delta[b, g],
             )
+    weights = jnp.transpose(parts[...])
+    for p in range(3):
+        log_row_ref[p] = log_all[p]
+        delta_row_ref[p] = delta[p]
+        for g in range(2):
+            r = 4 * p + 2 * g
+            att[p, :, N * g : N * g + N] = (
+                spread(weights, r) * near_ref[p, :, N * g : N * g + N]
+                + spread(weights, 12 + r) * mixed[pl.ds(2 * p + g, N, stride=MIXED), :]
+            ).astype(BF)
+    me = lax.axis_index("head")
+    theirs = pl.ds(pl.multiple_of((1 - me) * HALF, HALF), HALF)
+    mine = pl.ds(pl.multiple_of(me * HALF, HALF), HALF)
+    for p in range(3):
+        kept[HALF * p : HALF * p + HALF, :] = att[p, mine, :]
+    keeping = pltpu.make_async_copy(kept, kept_ref, kept_sem)
+    keeping.start()
     for g in range(2):
         lanes = slice(N * g, N * g + N)
         for c, b in cross:
@@ -297,24 +314,8 @@
     leaving = pltpu.make_async_copy(packed, send_ref, sem)
     leaving.start()
 
-    weights = jnp.transpose(parts[...])
     for p in range(3):
         dq_ref[p] = dq6[p]
-        log_row_ref[p] = log_all[p]
-        delta_row_ref[p] = delta[p]
-        for g in range(2):
-            r = 4 * p + 2 * g
-            att[p, :, N * g : N * g + N] = (
-                spread(weights, r) * near_ref[p, :, N * g : N * g + N]
-                + spread(weights, 12 + r) * mixed[pl.ds(2 * p + g, N, stride=MIXED), :]
-            ).astype(BF)
-    me = lax.axis_index("head")
-    theirs = pl.ds(pl.multiple_of((1 - me) * HALF, HALF), HALF)
-    mine = pl.ds(pl.multiple_of(me * HALF, HALF), HALF)
-    for p in range(3):
-        kept[HALF * p : HALF * p + HALF, :] = att[p, mine, :]
-    keeping = pltpu.make_async_copy(kept, kept_ref, kept_sem)
-    keeping.start()
     for p in range(3):
         given_ref[HALF * p : HALF * p + HALF, :] = nn(att[p, theirs, :], proj_ref[...]).astype(BF)
     keeping.wait()

time: 104 us -> 104 us (level)
  no operation moved by 1% of the time
where the time goes in v8:
time: 104 us
  waiting for transfers between devices  40.2 us (39%)
  starting transfers between devices  25.6 us (25%)
  blocking collectives  25.5 us (25%)
  Pallas kernels  11.3 us (11%)
    all_to_all x2, waiting for transfers between devices, exchange(): got = lax.all_to_all(sent, 'band', split_axis=0, concat_axis=0, tiled=True)  39.7 us
    all_to_all x1, blocking collectives, exchange(): got = lax.all_to_all(sent, 'band', split_axis=0, concat_axis=0, tiled=True)  25.5 us
    all_to_all x2, starting transfers between devices, exchange(): got = lax.all_to_all(sent, 'band', split_axis=0, concat_axis=0, tiled=True)  23 us
    pallas_call x3, Pallas kernels, call(): pl.pallas_call(kernel, out_shape=tuple(outs) if many else outs[0], in_spe...  4.77 us
    pallas_call x1, Pallas kernels, backward(): pl.pallas_call(backward_kernel, out_shape=outs + (row, row), in_specs=[VM...  2.69 us
    ppermute x1, starting transfers between devices, body(): other = lax.ppermute(cotangent, 'head', swap)  2.55 us
  transfers between devices with their start and end apart: 4, of which 3 were waited for; matrix products, arithmetic and copies ran while one was open for 0% of the time, Pallas kernels for 6%

profile of v8, /device:TPU:1, one launch (start us, length us, event | category | flops | bytes accessed | tf_op | source)
XLA Modules:
  0.0 103.5 jit_solution(1684967052769053122)
XLA Ops:
  0.6 2.6 %collective-permute-start = (bf16[192,1024]{1,0:T(8,128)(2,1)}, bf16[192,1024]{1,0:T(8,128)(2,1)S(1)}, u32[]{:S(2)}, u32[]{:S(2)}) collective-permute-start(bf16[192,1024]{1,0:T(8,128)(2,1)} %bitcast.30), channel_id=1, source_target_pairs={{0,1},{1,0},{2,3},{3,2},{4,5},{5,4},{6,7},{7,6},{8,9},{9,8},{10,11... | collective-permute-start | bytes 1179656 | tf_op jit(solution)/shard_map/ppermute | solution.py:490
  3.2 2.0 %pack_lines.1 = bf16[2304,128]{1,0:T(8,128)(2,1)} custom-call(bf16[3,128,256]{2,1,0:T(8,128)(2,1)} %bitcast.17, bf16[3,128,256]{2,1,0:T(8,128)(2,1)} %bitcast.21, bf16[3,128,256]{2,1,0:T(8,128)(2,1)} %bitcast.25), custom_call_target="tpu_custom_call" | custom-call | tf_op jit(solution)/shard_map/pack_lines/pallas_call | solution.py:468
  5.2 0.0 copy-start.6
  5.2 0.0 copy-start
  5.2 0.0 copy-start.1
  5.2 0.0 copy-start.2
  5.2 0.0 copy-start.3
  5.3 15.1 %all-to-all-start = ((bf16[128,9,2,128]{3,2,1,0:T(2,128)(2,1)}), bf16[128,9,2,128]{3,2,1,0:T(2,128)(2,1)S(1)}, u32[]{:S(2)}, u32[]{:S(2)}) async-start(bf16[128,9,2,128]{3,2,1,0:T(2,128)(2,1)} %bitcast.32), calls=%async_computation | async-start | bytes 1179648 | tf_op jit(solution)/shard_map/all_to_all | solution.py:383
  20.4 0.0 copy-done.6
  20.4 0.1 copy.14.axes_ref
  20.5 0.0 collective-permute-done.other_ref
  20.5 0.9 own.1
  21.4 21.1 %all-to-all-done = bf16[128,9,2,128]{3,2,1,0:T(2,128)(2,1)S(1)} async-done(((bf16[128,9,2,128]{3,2,1,0:T(2,128)(2,1)}), bf16[128,9,2,128]{3,2,1,0:T(2,128)(2,1)S(1)}, u32[]{:S(2)}, u32[]{:S(2)}) %all-to-all-start) | async-done | bytes 589856 | tf_op jit(solution)/shard_map/all_to_all | solution.py:383
  42.6 1.8 %forward.1 = (bf16[1792,128]{1,0:T(8,128)(2,1)S(1)}, bf16[6,128,256]{2,1,0:T(8,128)(2,1)S(1)}, bf16[6,128,256]{2,1,0:T(8,128)(2,1)S(1)}, bf16[6,128,256]{2,1,0:T...) custom-call(s32[3,2]{1,0:T(4,128)S(1)} %copy.14.axes_ref, ...), custom_call_target="tpu_custom_call" | custom-call | tf_op jit(solution)/shard_map/forward/pallas_call | solution.py:398
  44.4 25.5 %all_to_all.15 = bf16[128,7,2,128]{3,2,1,0:T(2,128)(2,1)S(1)} all-to-all(bf16[128,7,2,128]{3,2,1,0:T(2,128)(2,1)S(1)} %bitcast.29), channel_id=1, replica_groups=mesh['band'=128,'head'=2] {'band'}, dimensions={0} | all-to-all | bytes 917504 | tf_op jit(solution)/shard_map/all_to_all | solution.py:383
  69.8 2.7 %backward.1 = (f32[3,128,256]{2,1,0:T(8,128)S(1)}, f32[3,128,256]{2,1,0:T(8,128)S(1)}, f32[3,128,256]{2,1,0:T(8,128)S(1)}, bf16[2304,128]{1,0:T(8,128)(2,1)}, bf...) custom-call(s32[3,2]{1,0:T(4,128)S(1)} %copy.14.axes_ref, ...), custom_call_target="tpu_custom_call" | custom-call | tf_op jit(solution)/shard_map/backward/pallas_call | solution.py:429
  72.5 0.1 collective-permute-start.1
  72.6 7.9 %all-to-all-start.2 = ((bf16[128,9,2,128]{3,2,1,0:T(2,128)(2,1)}), bf16[128,9,2,128]{3,2,1,0:T(2,128)(2,1)S(1)}, u32[]{:S(2)}, u32[]{:S(2)}) async-start(bf16[128,9,2,128]{3,2,1,0:T(2,128)(2,1)} %bitcast.9), calls=%async_computation.2 | async-start | bytes 1179648 | tf_op jit(solution)/shard_map/all_to_all | solution.py:383
  80.5 0.0 copy-start.5
  80.6 0.9 own_rows.1
  81.4 0.5 collective-permute-done.1.got_ref
  82.0 2.0 %layer.1 = bf16[192,1024]{1,0:T(8,128)(2,1)} custom-call(bf16[192,256]{1,0:T(8,128)(2,1)S(1)} %copy-done.5, bf16[256,1024]{1,0:T(8,128)(2,1)S(1)} %copy-done.3, bf16[192,1024]{1,0:T(8,128)(2,1)} %collective-permute-done.1.got_ref), custom_call_target="tpu_custom_call" | custom-call | flops 60000002048 | bytes 1500000 | tf_op jit(solution)/shard_map/layer/pallas_call | solution.py:398
  84.0 18.6 %all-to-all-done.2 = bf16[128,9,2,128]{3,2,1,0:T(2,128)(2,1)S(1)} async-done(((bf16[128,9,2,128]{3,2,1,0:T(2,128)(2,1)}), bf16[128,9,2,128]{3,2,1,0:T(2,128)(2,1)S(1)}, u32[]{:S(2)}, u32[]{:S(2)}) %all-to-all-start.2) | async-done | bytes 589856 | tf_op jit(solution)/shard_map/all_to_all | solution.py:383
  102.6 1.0 finish.1
  (7 shorter events, 0.0 us)
Async XLA Ops:
  0.6 19.8 %collective-permute-start = (bf16[192,1024]{1,0:T(8,128)(2,1)}, bf16[192,1024]{1,0:T(8,128)(2,1)S(1)}, u32[]{:S(2)}, u32[]{:S(2)}) collective-permute-start(bf16[192,1024]{1,0:T(8,128)(2,1)} %bitcast.30), channel_id=1, source_target_pairs={{0,1},{1,0},{2,3},{3,2},{4,5},{5,4},{6,7},{7,6},{8,9},{9,8},{10,11... | collective-permute-start | bytes 1179656 | tf_op jit(solution)/shard_map/ppermute | solution.py:490
  3.2 17.3 %copy-start.4 = (bf16[1,3,64,1024]{3,2,1,0:T(8,128)(2,1)S(1)}, bf16[1,3,64,1024]{3,2,1,0:T(8,128)(2,1)}, u32[]{:S(2)}) copy-start(bf16[1,3,64,1024]{3,2,1,0:T(8,128)(2,1)} %param.10) | copy-start | bytes 1179652
  5.2 15.2 %copy-start.6 = (s32[3,2]{0,1:T(2,128)S(1)}, s32[3,2]{0,1:T(2,128)}, u32[]{:S(2)}) copy-start(s32[3,2]{0,1:T(2,128)} %param.11) | copy-start | bytes 76
  5.2 15.3 %copy-start = (bf16[1,3,128,256]{3,2,1,0:T(8,128)(2,1)S(1)}, bf16[1,3,128,256]{3,2,1,0:T(8,128)(2,1)}, u32[]{:S(2)}) copy-start(bf16[1,3,128,256]{3,2,1,0:T(8,128)(2,1)} %param.6) | copy-start | bytes 589828
  5.2 15.3 %copy-start.1 = (bf16[1,3,128,256]{3,2,1,0:T(8,128)(2,1)S(1)}, bf16[1,3,128,256]{3,2,1,0:T(8,128)(2,1)}, u32[]{:S(2)}) copy-start(bf16[1,3,128,256]{3,2,1,0:T(8,128)(2,1)} %param.7) | copy-start | bytes 589828
  5.2 15.2 %copy-start.2 = (bf16[1,3,128,256]{3,2,1,0:T(8,128)(2,1)S(1)}, bf16[1,3,128,256]{3,2,1,0:T(8,128)(2,1)}, u32[]{:S(2)}) copy-start(bf16[1,3,128,256]{3,2,1,0:T(8,128)(2,1)} %param.8) | copy-start | bytes 589828
  5.2 15.2 %copy-start.3 = (bf16[256,1024]{1,0:T(8,128)(2,1)S(1)}, bf16[256,1024]{1,0:T(8,128)(2,1)}, u32[]{:S(2)}) copy-start(bf16[256,1024]{1,0:T(8,128)(2,1)} %proj_ref.5) | copy-start | bytes 1572868
  5.3 37.3 %all-to-all-start = ((bf16[128,9,2,128]{3,2,1,0:T(2,128)(2,1)}), bf16[128,9,2,128]{3,2,1,0:T(2,128)(2,1)S(1)}, u32[]{:S(2)}, u32[]{:S(2)}) async-start(bf16[128,9,2,128]{3,2,1,0:T(2,128)(2,1)} %bitcast.32), calls=%async_computation | async-start | bytes 1179648 | tf_op jit(solution)/shard_map/all_to_all | solution.py:383
  72.5 9.4 %collective-permute-start.1 = (bf16[192,1024]{1,0:T(8,128)(2,1)S(1)}, bf16[192,1024]{1,0:T(8,128)(2,1)}, u32[]{:S(2)}, u32[]{:S(2)}) collective-permute-start(bf16[192,1024]{1,0:T(8,128)(2,1)S(1)} %get-tuple-element.41), channel_id=1, source_target_pairs={{0,1},{1,0},{2,3},{3,2},{4,5},{5,4},{6,7},{7,6},{8,9},{9,8},{10,11... | collective-permute-start | bytes 1179656 | tf_op jit(solution)/shard_map/ppermute | solution.py:501
  72.6 29.9 %all-to-all-start.2 = ((bf16[128,9,2,128]{3,2,1,0:T(2,128)(2,1)}), bf16[128,9,2,128]{3,2,1,0:T(2,128)(2,1)S(1)}, u32[]{:S(2)}, u32[]{:S(2)}) async-start(bf16[128,9,2,128]{3,2,1,0:T(2,128)(2,1)} %bitcast.9), calls=%async_computation.2 | async-start | bytes 1179648 | tf_op jit(solution)/shard_map/all_to_all | solution.py:383
  80.5 1.4 %copy-start.5 = (bf16[192,256]{1,0:T(8,128)(2,1)S(1)}, bf16[192,256]{1,0:T(8,128)(2,1)}, u32[]{:S(2)}) copy-start(bf16[192,256]{1,0:T(8,128)(2,1)} %get-tuple-element.40.kept_ref) | copy-start | bytes 294916

commit v9 on v7

--- a/solution.py
+++ b/solution.py
@@ -149,7 +149,7 @@
                 lines = pl.ds(2 * (3 * a + p) + g, N, stride=SENT)
                 six[3 + p, :, N * g : N * g + N] = stage[lines, :].astype(BF)
 
-    blocks = list(enumerate(partners(axes_ref)))
+    blocks = list(enumerate(partners(axes_ref)))[::-1]
     for g in range(2):
         lanes = slice(N * g, N * g + N)
         for b, c in blocks:
@@ -486,8 +486,10 @@
     q, k, v = queries[0], attn_keys[0], attn_values[0]
 
     cotangent = grad_out.reshape(TOKENS)
+    packed = pack_lines(q, k, v)
+    cotangent, packed = lax.optimization_barrier((cotangent, packed))
     other = lax.ppermute(cotangent, "head", swap)
-    lines = exchange(pack_lines(q, k, v), SENT)
+    lines = exchange(packed, SENT)
     ga, top, total, own_out = own(cotangent, other, out_proj, q, k, v)
 
     sent, q6, k6, v6, near_out, far_out, totals = forward(

time: 104 us -> 104 us (level)
  transfers between devices with their start and end apart: 4 -> 4, of which waited for: 3 -> 3; matrix products, arithmetic and copies ran while one was open for 0% -> 0% of each run, Pallas kernels for 6% -> 4%
where the time goes in v9:
time: 104 us; the launch traced here: 103 us
  waiting for transfers between devices  40.2 us (39%)
  starting transfers between devices  25.6 us (25%)
  blocking collectives  25.5 us (25%)
  Pallas kernels  11.2 us (11%)
    all_to_all x2, waiting for transfers between devices, exchange(): got = lax.all_to_all(sent, 'band', split_axis=0, concat_axis=0, tiled=True)  39.7 us
    all_to_all x1, blocking collectives, exchange(): got = lax.all_to_all(sent, 'band', split_axis=0, concat_axis=0, tiled=True)  25.5 us
    all_to_all x2, starting transfers between devices, exchange(): got = lax.all_to_all(sent, 'band', split_axis=0, concat_axis=0, tiled=True)  23 us
    pallas_call x3, Pallas kernels, call(): pl.pallas_call(kernel, out_shape=tuple(outs) if many else outs[0], in_spe...  4.73 us
    pallas_call x1, Pallas kernels, backward(): pl.pallas_call(backward_kernel, out_shape=outs + (row, row), in_specs=[VM...  2.65 us
    ppermute x1, starting transfers between devices, body(): other = lax.ppermute(cotangent, 'head', swap)  2.55 us
  transfers between devices with their start and end apart: 4, of which 3 were waited for; matrix products, arithmetic and copies ran while one was open for 0% of the time, Pallas kernels for 4%

profile of v9, /device:TPU:1, one launch (start us, length us, event | category | flops | bytes accessed | tf_op | source)
XLA Modules:
  0.0 103.4 jit_solution(6098167535804753809)
XLA Ops:
  0.6 0.0 copy-start.4
  0.6 2.0 %pack_lines.1 = bf16[2304,128]{1,0:T(8,128)(2,1)} custom-call(bf16[3,128,256]{2,1,0:T(8,128)(2,1)} %bitcast.17, bf16[3,128,256]{2,1,0:T(8,128)(2,1)} %bitcast.21, bf16[3,128,256]{2,1,0:T(8,128)(2,1)} %bitcast.25), custom_call_target="tpu_custom_call" | custom-call | tf_op jit(solution)/shard_map/pack_lines/pallas_call | solution.py:467
  2.6 0.0 copy-done.4
  2.7 2.6 %collective-permute-start = (bf16[192,1024]{1,0:T(8,128)(2,1)S(1)}, bf16[192,1024]{1,0:T(8,128)(2,1)S(1)}, u32[]{:S(2)}, u32[]{:S(2)}) collective-permute-start(bf16[192,1024]{1,0:T(8,128)(2,1)S(1)} %bitcast.30), channel_id=1, source_target_pairs={{0,1},{1,0},{2,3},{3,2},{4,5},{5,4},{6,7},{7,6},{8,9},{9,8},{10,11... | collective-permute-start | bytes 1179656 | tf_op jit(solution)/shard_map/ppermute | solution.py:491
  5.2 0.0 copy-start.3
  5.2 15.1 %all-to-all-start = ((bf16[128,9,2,128]{3,2,1,0:T(2,128)(2,1)}), bf16[128,9,2,128]{3,2,1,0:T(2,128)(2,1)S(1)}, u32[]{:S(2)}, u32[]{:S(2)}) async-start(bf16[128,9,2,128]{3,2,1,0:T(2,128)(2,1)} %bitcast.32), calls=%async_computation | async-start | bytes 1179648 | tf_op jit(solution)/shard_map/all_to_all | solution.py:382
  20.3 0.0 copy-done.6
  20.3 0.1 copy.14.axes_ref
  20.4 0.0 collective-permute-done.other_ref
  20.4 0.0 copy-done
  20.4 0.0 copy-done.1
  20.5 0.9 own.1
  21.4 21.1 %all-to-all-done = bf16[128,9,2,128]{3,2,1,0:T(2,128)(2,1)S(1)} async-done(((bf16[128,9,2,128]{3,2,1,0:T(2,128)(2,1)}), bf16[128,9,2,128]{3,2,1,0:T(2,128)(2,1)S(1)}, u32[]{:S(2)}, u32[]{:S(2)}) %all-to-all-start) | async-done | bytes 589856 | tf_op jit(solution)/shard_map/all_to_all | solution.py:382
  42.5 1.8 %forward.1 = (bf16[1792,128]{1,0:T(8,128)(2,1)S(1)}, bf16[6,128,256]{2,1,0:T(8,128)(2,1)S(1)}, bf16[6,128,256]{2,1,0:T(8,128)(2,1)S(1)}, bf16[6,128,256]{2,1,0:T...) custom-call(s32[3,2]{1,0:T(4,128)S(1)} %copy.14.axes_ref, ...), custom_call_target="tpu_custom_call" | custom-call | tf_op jit(solution)/shard_map/forward/pallas_call | solution.py:397
  44.3 25.5 %all_to_all.15 = bf16[128,7,2,128]{3,2,1,0:T(2,128)(2,1)S(1)} all-to-all(bf16[128,7,2,128]{3,2,1,0:T(2,128)(2,1)S(1)} %bitcast.29), channel_id=1, replica_groups=mesh['band'=128,'head'=2] {'band'}, dimensions={0} | all-to-all | bytes 917504 | tf_op jit(solution)/shard_map/all_to_all | solution.py:382
  69.8 2.7 %backward.1 = (f32[3,128,256]{2,1,0:T(8,128)S(1)}, f32[3,128,256]{2,1,0:T(8,128)S(1)}, f32[3,128,256]{2,1,0:T(8,128)S(1)}, bf16[2304,128]{1,0:T(8,128)(2,1)}, bf...) custom-call(s32[3,2]{1,0:T(4,128)S(1)} %copy.14.axes_ref, ...), custom_call_target="tpu_custom_call" | custom-call | tf_op jit(solution)/shard_map/backward/pallas_call | solution.py:428
  72.5 0.1 collective-permute-start.1
  72.6 7.9 %all-to-all-start.2 = ((bf16[128,9,2,128]{3,2,1,0:T(2,128)(2,1)}), bf16[128,9,2,128]{3,2,1,0:T(2,128)(2,1)S(1)}, u32[]{:S(2)}, u32[]{:S(2)}) async-start(bf16[128,9,2,128]{3,2,1,0:T(2,128)(2,1)} %bitcast.9), calls=%async_computation.2 | async-start | bytes 1179648 | tf_op jit(solution)/shard_map/all_to_all | solution.py:382
  80.5 0.0 copy-start.5
  80.5 0.8 own_rows.1
  81.3 0.5 collective-permute-done.1.got_ref
  81.9 2.0 %layer.1 = bf16[192,1024]{1,0:T(8,128)(2,1)} custom-call(bf16[192,256]{1,0:T(8,128)(2,1)S(1)} %copy-done.5, bf16[256,1024]{1,0:T(8,128)(2,1)S(1)} %copy-done.3, bf16[192,1024]{1,0:T(8,128)(2,1)} %collective-permute-done.1.got_ref), custom_call_target="tpu_custom_call" | custom-call | flops 60000002048 | bytes 1500000 | tf_op jit(solution)/shard_map/layer/pallas_call | solution.py:397
  83.9 18.6 %all-to-all-done.2 = bf16[128,9,2,128]{3,2,1,0:T(2,128)(2,1)S(1)} async-done(((bf16[128,9,2,128]{3,2,1,0:T(2,128)(2,1)}), bf16[128,9,2,128]{3,2,1,0:T(2,128)(2,1)S(1)}, u32[]{:S(2)}, u32[]{:S(2)}) %all-to-all-start.2) | async-done | bytes 589856 | tf_op jit(solution)/shard_map/all_to_all | solution.py:382
  102.5 1.0 finish.1
  (7 shorter events, 0.0 us)
Async XLA Ops:
  0.6 2.0 %copy-start.4 = (bf16[1,3,64,1024]{3,2,1,0:T(8,128)(2,1)S(1)}, bf16[1,3,64,1024]{3,2,1,0:T(8,128)(2,1)}, u32[]{:S(2)}) copy-start(bf16[1,3,64,1024]{3,2,1,0:T(8,128)(2,1)} %param.10) | copy-start | bytes 1179652
  2.7 17.8 %collective-permute-start = (bf16[192,1024]{1,0:T(8,128)(2,1)S(1)}, bf16[192,1024]{1,0:T(8,128)(2,1)S(1)}, u32[]{:S(2)}, u32[]{:S(2)}) collective-permute-start(bf16[192,1024]{1,0:T(8,128)(2,1)S(1)} %bitcast.30), channel_id=1, source_target_pairs={{0,1},{1,0},{2,3},{3,2},{4,5},{5,4},{6,7},{7,6},{8,9},{9,8},{10,11... | collective-permute-start | bytes 1179656 | tf_op jit(solution)/shard_map/ppermute | solution.py:491
  5.2 15.1 %copy-start.6 = (s32[3,2]{0,1:T(2,128)S(1)}, s32[3,2]{0,1:T(2,128)}, u32[]{:S(2)}) copy-start(s32[3,2]{0,1:T(2,128)} %param.11) | copy-start | bytes 76
  5.2 15.2 %copy-start = (bf16[1,3,128,256]{3,2,1,0:T(8,128)(2,1)S(1)}, bf16[1,3,128,256]{3,2,1,0:T(8,128)(2,1)}, u32[]{:S(2)}) copy-start(bf16[1,3,128,256]{3,2,1,0:T(8,128)(2,1)} %param.6) | copy-start | bytes 589828
  5.2 15.2 %copy-start.1 = (bf16[1,3,128,256]{3,2,1,0:T(8,128)(2,1)S(1)}, bf16[1,3,128,256]{3,2,1,0:T(8,128)(2,1)}, u32[]{:S(2)}) copy-start(bf16[1,3,128,256]{3,2,1,0:T(8,128)(2,1)} %param.7) | copy-start | bytes 589828
  5.2 15.2 %copy-start.2 = (bf16[1,3,128,256]{3,2,1,0:T(8,128)(2,1)S(1)}, bf16[1,3,128,256]{3,2,1,0:T(8,128)(2,1)}, u32[]{:S(2)}) copy-start(bf16[1,3,128,256]{3,2,1,0:T(8,128)(2,1)} %param.8) | copy-start | bytes 589828
  5.2 15.2 %copy-start.3 = (bf16[256,1024]{1,0:T(8,128)(2,1)S(1)}, bf16[256,1024]{1,0:T(8,128)(2,1)}, u32[]{:S(2)}) copy-start(bf16[256,1024]{1,0:T(8,128)(2,1)} %proj_ref.5) | copy-start | bytes 1572868
  5.2 37.3 %all-to-all-start = ((bf16[128,9,2,128]{3,2,1,0:T(2,128)(2,1)}), bf16[128,9,2,128]{3,2,1,0:T(2,128)(2,1)S(1)}, u32[]{:S(2)}, u32[]{:S(2)}) async-start(bf16[128,9,2,128]{3,2,1,0:T(2,128)(2,1)} %bitcast.32), calls=%async_computation | async-start | bytes 1179648 | tf_op jit(solution)/shard_map/all_to_all | solution.py:382
  72.5 9.4 %collective-permute-start.1 = (bf16[192,1024]{1,0:T(8,128)(2,1)S(1)}, bf16[192,1024]{1,0:T(8,128)(2,1)}, u32[]{:S(2)}, u32[]{:S(2)}) collective-permute-start(bf16[192,1024]{1,0:T(8,128)(2,1)S(1)} %get-tuple-element.45), channel_id=1, source_target_pairs={{0,1},{1,0},{2,3},{3,2},{4,5},{5,4},{6,7},{7,6},{8,9},{9,8},{10,11... | collective-permute-start | bytes 1179656 | tf_op jit(solution)/shard_map/ppermute | solution.py:502
  72.6 29.9 %all-to-all-start.2 = ((bf16[128,9,2,128]{3,2,1,0:T(2,128)(2,1)}), bf16[128,9,2,128]{3,2,1,0:T(2,128)(2,1)S(1)}, u32[]{:S(2)}, u32[]{:S(2)}) async-start(bf16[128,9,2,128]{3,2,1,0:T(2,128)(2,1)} %bitcast.9), calls=%async_computation.2 | async-start | bytes 1179648 | tf_op jit(solution)/shard_map/all_to_all | solution.py:382
  80.5 1.4 %copy-start.5 = (bf16[192,256]{1,0:T(8,128)(2,1)S(1)}, bf16[192,256]{1,0:T(8,128)(2,1)}, u32[]{:S(2)}) copy-start(bf16[192,256]{1,0:T(8,128)(2,1)} %get-tuple-element.44.kept_ref) | copy-start | bytes 294916
